TPU v7x, 256 devices: a whole 4x4x8 slice. The times are simulated.
256 devices in a mesh: seq: 64 (over z, y, core), view: 4 (over x).
Axes of the slice: x: 4, y: 4, z: 8, core: 2. Of those that a mesh axis runs over, the one named last changes fastest.
Arguments:
- ssd_input: bfloat16 [64, 4, 512, 2048], P('seq', 'view'), may hold values from -21 to 21
- gate_input: bfloat16 [64, 4, 512, 2048], P('seq', 'view'), may hold values from -6 to 6
- b_matrix: bfloat16 [64, 4, 512, 128], P('seq', 'view'), may hold values from -6 to 6
- c_matrix: bfloat16 [64, 4, 512, 128], P('seq', 'view'), may hold values from -0.52734375 to 0.52734375
- log_decay: float32 [64, 4, 32, 512], P('seq', 'view'), may hold values from -1 to 0, as said below
- d_skip: float32 [32], replicated, may hold values from 1 to 4
- norm_gain: float32 [2048], replicated, may hold values from 0.1 to 1.9
- out_weight: bfloat16 [2048, 1536], replicated, may hold values from -0.125 to 0.125
- view_order: int32 [64, 4], P('seq'), may hold values from 0 to 3, each once within a row
- tile_order: int32 [64, 4], P('seq'), may hold values from 0 to 3, each once within a row
Outputs:
- next_tokens: bfloat16 [64, 4, 512, 1536], P('seq', 'view')
Inputs may be any that keep to these rules, and one draw needn't show every extreme that they name: `log_decay`: negative everywhere. `view_order`: each row is a permutation of the views. `tile_order`: each row is a permutation of the tiles of a block.
All inputs are finite; a program needn't handle non-finite values.
Results may differ from a plain program's by a relative error of at most 0.0059.
Values may be sent and summed in bfloat16 or wider, within the bound.
No kernel may reach another device: no remote copies, remote signals or barrier semaphores. Data moves between devices by JAX's collectives and lax.ppermute only.
A program may use at most 128 MiB of HBM per device.

v0:
```python
import jax
import jax.numpy as jnp
from jax import lax
from jax.sharding import Mesh
from jax.sharding import PartitionSpec as P

H = 32
HEAD = 64
N = 128
GROUP = 256
TILE = 128
TOKENS_PER_BLOCK = 512
SEQ = ("seq_0", "seq_1", "seq_2")


EPS = 1e-05


def sent_to_all(x, axis):
    count = lax.axis_size(axis)
    return lax.all_to_all(jnp.broadcast_to(x[None], (count, *x.shape)), axis, 0, 0, tiled=True)


def joined_along(parts, dim):
    lengths = list(parts.shape[1:])
    lengths[dim] *= parts.shape[0]
    return jnp.moveaxis(parts, 0, dim).reshape(lengths)


def collect(x, axis, dim):
    parts = sent_to_all(x, axis)
    return joined_along(parts, dim)


def filled_with(x, identity):
    return jax.tree.map(
        lambda part, zero: jnp.zeros_like(part) + jnp.asarray(zero, part.dtype), x, identity
    )


def entering_2(x, axes, combine, identity):
    before = start = filled_with(x, identity)
    total = x
    for axis in reversed(axes):
        count, position = (lax.axis_size(axis), lax.axis_index(axis))
        pieces = jax.tree.map(lambda part: lax.all_gather(part, axis), total)
        inside, total = (start, start)
        for k in range(count):
            passed = k < position
            total = combine(total, jax.tree.map(lambda part: part[k], pieces))
            inside = jax.tree.map(lambda new, old: jnp.where(passed, new, old), total, inside)
        before = combine(inside, before)
    return before


def compose(earlier, later):
    return (earlier[0] * later[0], later[0][:, None, None] * earlier[1] + later[1])


def masked_product(decays, keep_mask):
    return jnp.prod(jnp.where(keep_mask[:, :, None], decays[None], 1.0), axis=1)


def shards(
    ssd_input,
    gate_input,
    b_matrix,
    c_matrix,
    log_decay,
    d_skip,
    norm_gain,
    out_weight,
    view_order,
    tile_order,
):
    group_count = TOKENS_PER_BLOCK // GROUP
    view_count = lax.axis_size("view")
    band_count = lax.axis_size(SEQ)
    piece_len = TOKENS_PER_BLOCK // band_count
    x_groups = ssd_input[0, 0].reshape(group_count, GROUP, H, HEAD)
    b_groups = b_matrix[0, 0].reshape(group_count, GROUP, N)
    c_groups = c_matrix[0, 0].reshape(group_count, GROUP, N)
    cum_log = jnp.cumsum(log_decay[0, 0].reshape(H, group_count, GROUP), axis=2)
    group_end = cum_log[:, :, GROUP - 1]
    group_decay = jnp.exp(group_end)
    scaled = (
        jnp.exp(group_end[:, :, None] - cum_log)[..., None] * b_groups[None].astype(jnp.float32)
    ).astype(jnp.bfloat16)
    states = jnp.einsum("hckn,ckhp->hcpn", scaled, x_groups, preferred_element_type=jnp.float32)
    running = jnp.zeros((H, HEAD, N), jnp.float32)
    before = jnp.ones((H,), jnp.float32)
    prefixes = []
    befores = []
    for lookup_index in range(group_count):
        prefixes.append(running)
        befores.append(before)
        running = group_decay[:, lookup_index, None, None] * running + states[:, lookup_index]
        before = before * group_decay[:, lookup_index]
    band_order = view_order[0]
    view_slots = jnp.arange(view_count, dtype=jnp.int32)
    order_hot = band_order[:, None] == view_slots[None, :]
    view_rank = jnp.sum(jnp.where(order_hot, view_slots[:, None], 0), axis=0)
    my_view = lax.axis_index("view")
    heads_share = H // view_count
    all_decay = collect(before[None], "view", 0)
    share_decay = lax.dynamic_slice_in_dim(all_decay, my_view * heads_share, heads_share, 1)
    split_state = running.reshape(view_count, heads_share, HEAD, N)
    view_states = lax.all_to_all(split_state, "view", split_axis=0, concat_axis=0, tiled=True)
    after_mask = view_rank[None, :] > view_rank[:, None]
    to_total = masked_product(share_decay, after_mask)
    share_state = jnp.sum(to_total[:, :, None, None] * view_states, axis=0)
    share_row_decay = jnp.prod(share_decay, axis=0)
    identity = (jnp.ones_like(share_row_decay), jnp.zeros_like(share_state))
    _, share_in = entering_2((share_row_decay, share_state), SEQ, compose, identity)
    pre_decays = masked_product(share_decay, view_rank[None, :] < view_rank[:, None])
    targets = []
    for target in range(view_count):
        target_rank = view_rank[target]
        between = after_mask & (view_rank[None, :] < target_rank)
        to_target = jnp.where(
            (view_rank < target_rank)[:, None], masked_product(share_decay, between), 0.0
        )
        within = jnp.sum(to_target[:, :, None, None] * view_states, axis=0)
        targets.append(pre_decays[target][:, None, None] * share_in + within)
    target_states = jnp.stack(targets, axis=0)
    entering = lax.all_to_all(target_states, "view", split_axis=0, concat_axis=1, tiled=True)[0]
    entries = jnp.stack(
        [prefix + factor[:, None, None] * entering for prefix, factor in zip(prefixes, befores)],
        axis=1,
    ).astype(jnp.bfloat16)
    scores = jnp.einsum("cqn,ckn->cqk", c_groups, b_groups, preferred_element_type=jnp.float32)
    log_gaps = cum_log[:, :, :, None] - cum_log[:, :, None, :]
    causal = jnp.tril(jnp.ones((GROUP, GROUP), dtype=bool))
    weights = (jnp.exp(jnp.where(causal, log_gaps, -jnp.inf)) * scores[None]).astype(jnp.bfloat16)
    inside = jnp.einsum("hcqk,ckhp->cqhp", weights, x_groups, preferred_element_type=jnp.float32)
    carried = jnp.einsum("cqn,hcpn->cqhp", c_groups, entries, preferred_element_type=jnp.float32)
    carried = carried * jnp.transpose(jnp.exp(cum_log), (1, 2, 0))[..., None]
    mixed = inside + carried + d_skip[None, None, :, None] * x_groups.astype(jnp.float32)
    gated = mixed * jax.nn.silu(
        gate_input[0, 0].reshape(group_count, GROUP, H, HEAD).astype(jnp.float32)
    )
    inv_rms = lax.rsqrt(jnp.mean(gated * gated, axis=-1, keepdims=True) + EPS)
    normed = (
        (gated * inv_rms * norm_gain.reshape(H, HEAD))
        .astype(jnp.bfloat16)
        .reshape(band_count, piece_len, H * HEAD)
    )
    arrived = lax.all_to_all(
        jnp.einsum("bpd,de->bpe", normed, out_weight, preferred_element_type=jnp.float32).astype(
            jnp.bfloat16
        ),
        SEQ,
        split_axis=0,
        concat_axis=0,
        tiled=True,
    )
    width_out = out_weight.shape[1]
    tile_rows = arrived.reshape(TOKENS_PER_BLOCK // TILE, TILE, width_out)
    chosen = jnp.take(tile_rows, tile_order[0], axis=0)
    return chosen.reshape(1, 1, TOKENS_PER_BLOCK, width_out)


def solution(mesh):
    split = Mesh(
        mesh.devices.reshape(8, 4, 2, mesh.shape["view"]), ("seq_0", "seq_1", "seq_2", "view")
    )
    in_specs = (
        P(SEQ, "view", None, None),
        P(SEQ, "view", None, None),
        P(SEQ, "view", None, None),
        P(SEQ, "view", None, None),
        P(SEQ, "view", None, None),
        P(),
        P(),
        P(),
        P(SEQ, None),
        P(SEQ, None),
    )
    out_specs = P(SEQ, "view", None, None)
    return jax.shard_map(
        shards, mesh=split, in_specs=in_specs, out_specs=out_specs, check_vma=False
    )
```

profile of v0, /device:TPU:1, one launch (start us, length us, event | category | flops | bytes accessed | tf_op | source)
XLA Modules:
  0.0 244.2 jit_solution(1874271033634736183)
XLA Ops:
  6.5 0.9 reshape.540
  7.5 1.2 reduce-window.6
  9.0 0.6 copy-done.10
  10.3 0.6 broadcast_in_dim.199
  10.9 4.8 %all-to-all-start = ((f32[4,1,32]{2,1,0:T(1,128)}), f32[4,1,32]{2,1,0:T(1,128)S(1)}, u32[]{:S(2)}, u32[]{:S(2)}) async-start(f32[4,1,32]{2,1,0:T(1,128)} %broadcast_in_dim.199), calls=%async_computation | async-start | bytes 4096 | tf_op jit(solution)/shard_map/all_to_all | solution.py:21
  15.8 0.7 exponential_bitcast_fusion
  16.5 0.6 slice_reduce_fusion.1
  17.1 2.9 %copy.66 = bf16[1,1,512,2048]{2,3,1,0:T(8,128)(2,1)S(1)} copy(bf16[1,1,512,2048]{3,2,1,0:T(8,128)(2,1)} %param.10) | data formatting | bytes 4194304 | tf_op args[0]
  20.0 2.1 reshape_squeeze.13
  22.4 4.6 %fusion.19 = f32[32,2,64,128]{3,2,1,0:T(8,128)S(1)} fusion(f32[2,256,128]{2,1,0:T(8,128)S(1)} %convert_element_type.31, f32[32,2,256]{2,1,0:T(2,128)S(1)} %copy.68, bf16[2,256,32,64]{1,0,3,2:T(2,128)(2,1)} %reshape_squeeze.13), kind=kOutput, calls=%fused_computation.23 | convolution fusion | flops 272629760 | bytes 4521984 | tf_op jit(solution)/shard_map/hckn,ckhp->hcpn/dot_general | solution.py:89
  26.9 1.2 fusion.37
  28.2 0.7 fusion.39
  28.8 0.6 dynamic-slice.2
  30.0 2.4 bitcast_add_fusion
  32.4 2.5 %broadcast_compare_fusion.2 = (pred[4]{0:T(512)(128)(4,1)S(1)}, pred[4]{0:T(512)(128)(4,1)S(1)}, pred[4]{0:T(512)(128)(4,1)S(1)}, pred[4]{0:T(512)(128)(4,1)S(1)}) fusion(s32[4]{0:T(128)S(1)} %select_reduce_fusion.6, s32[]{:T(128)} %bitcast.36, s32[]{:T(128)} %bitcast.33, s32[]{:T(128)} %bitcast.30, s32[]{:T(128)} %bitcast.27), kind=kLoop, calls=%fused_computation.117 | loop fusion | flops 16 | bytes 48 | tf_op jit(solution)/shard_map/lt | solution.py:121
  36.1 4.2 %all-to-all-start.1 = ((f32[4,8,64,128]{3,2,1,0:T(8,128)}), f32[4,8,64,128]{3,2,1,0:T(8,128)S(1)}, u32[]{:S(2)}, u32[]{:S(2)}) async-start(f32[4,8,64,128]{3,2,1,0:T(8,128)} %bitcast_add_fusion), calls=%async_computation.1 | async-start | bytes 2097152 | tf_op jit(solution)/shard_map/all_to_all | solution.py:108
  40.7 4.3 %all-reduce = f32[16]{0:T(128)S(1)} all-reduce(f32[16]{0:T(128)S(1)} %dynamic-update-slice), channel_id=2, replica_groups=mesh['seq_0'=8,'seq_1'=4,'seq_2'=2,'view'=4] {'seq_2'}, use_global_device_ids=true, to_apply=%add | all-reduce | flops 16 | bytes 128
  45.0 0.6 fusion.34
  45.6 8.6 %all-reduce.1 = f32[32]{0:T(128)S(1)} all-reduce(f32[32]{0:T(128)S(1)} %get-tuple-element.54), channel_id=4, replica_groups=mesh['seq_0'=8,'seq_1'=4,'seq_2'=2,'view'=4] {'seq_1'}, use_global_device_ids=true, to_apply=%add.1 | all-reduce | flops 32 | bytes 256
  54.3 0.7 multiply_bitcast_fusion
  55.0 0.7 broadcast_select_fusion.3
  55.7 0.7 broadcast_select_fusion.1
  56.3 2.1 multiply_reduce_fusion.4
  58.5 3.6 %all-gather.1 = f32[16,64,128]{2,1,0:T(8,128)S(1)} all-gather(f32[8,64,128]{2,1,0:T(8,128)S(1)} %get-tuple-element.9), channel_id=3, replica_groups=mesh['seq_0'=8,'seq_1'=4,'seq_2'=2,'view'=4] {'seq_2'}, dimensions={0}, use_global_device_ids=true | all-gather | bytes 786432 | tf_op jit(solution)/shard_map/all_gather | solution.py:46
  62.0 1.4 fusion.28
  63.6 26.5 %all-gather.7.cloned.1.call-done = f32[4,8,64,128]{3,2,1,0:T(8,128)} async-done(((f32[1,8,64,128]{3,2,1,0:T(8,128)}), f32[4,8,64,128]{3,2,1,0:T(8,128)}) %all-gather.7.cloned.1.call-update) | async-done | bytes 1048592 | tf_op jit(solution)/shard_map/all_gather | solution.py:46
  90.1 2.0 slice_add_fusion.8
  92.2 13.0 %all-gather.3 = f32[8,1,8]{2,1,0:T(1,128)S(1)} all-gather(f32[1,1,8]{2,1,0:T(1,128)} %get-tuple-element.46), channel_id=1, replica_groups=mesh['seq_0'=8,'seq_1'=4,'seq_2'=2,'view'=4] {'seq_0'}, dimensions={0}, use_global_device_ids=true | all-gather | bytes 288 | tf_op jit(solution)/shard_map/all_gather | solution.py:46
  105.2 0.6 slice_bitcast_fusion.11
  105.8 0.6 slice_bitcast_fusion.8
  106.4 24.6 %all-gather.9.cloned.1.call-done = f32[8,8,64,128]{3,2,1,0:T(8,128)} async-done(((f32[1,8,64,128]{3,2,1,0:T(8,128)}), f32[8,8,64,128]{3,2,1,0:T(8,128)}) %all-gather.9.cloned.1.call-update) | async-done | bytes 2097168 | tf_op jit(solution)/shard_map/all_gather | solution.py:46
  131.0 2.6 %bitcast_add_fusion.5 = (f32[1,8,64,128]{3,2,1,0:T(8,128)S(1)}, f32[1,8,64,128]{3,2,1,0:T(8,128)S(1)}) fusion(f32[8,64,128]{2,1,0:T(8,128)S(1)} %get-tuple-element.5, f32[8]{0:T(128)} %get-tuple-element.42, f32[16,64,128]{2,1,0:T(8,128)S(1)} %all-gather.1, f32[8]{0:T(128)} %get-tuple-element.51, pred[]{:T(512)S(6)} %gt.72, pred[]{:T(512)S(6)} %gt.71, ...), kind=kLoop, calls=%fused_computation.60 | loop fusion | flops 2949120 | bytes 4457006 | tf_op jit(solution)/shard_map/add | solution.py:124
  133.8 1.1 pad_maximum_fusion
  134.8 4.0 %all-to-all-start.2 = ((f32[4,8,64,128]{3,2,1,0:T(8,128)}), f32[4,8,64,128]{3,2,1,0:T(8,128)S(1)}, u32[]{:S(2)}, u32[]{:S(2)}) async-start(f32[4,8,64,128]{3,2,1,0:T(8,128)} %pad_maximum_fusion), calls=%async_computation.2 | async-start | bytes 2097152 | tf_op jit(solution)/shard_map/all_to_all | solution.py:126
  138.8 7.4 %reshape.607 = f32[2,256,32,64]{3,2,1,0:T(8,128)} reshape(bf16[1,1,512,2048]{3,2,1,0:T(8,128)(2,1)} %param.11) | data formatting | bytes 6291456 | tf_op jit(solution)/shard_map/convert_element_type | solution.py:140
  146.2 7.9 %copy.74 = f32[2,256,32,64]{1,3,2,0:T(8,128)} copy(f32[2,256,32,64]{3,2,1,0:T(8,128)} %reshape.607) | data formatting | bytes 8388608 | tf_op jit(solution)/shard_map/convert_element_type | solution.py:140
  154.2 1.0 fusion.40
  155.6 0.7 fusion.23
  156.3 1.2 copy-done.2
  157.5 0.7 copy-done.3
  158.2 5.6 %multiply_reduce_fusion = (f32[2,256,32]{1,2,0:T(8,128)S(1)}, f32[2,256,32,64]{1,3,2,0:T(8,128)S(1)}) fusion(f32[2,256,32,64]{1,3,2,0:T(8,128)S(1)} %copy-done.2, bf16[2,256,32,64]{1,0,3,2:T(2,128)(2,1)S(1)} %copy-done.3, f32[32]{0:T(128)S(1)} %copy-done.20, f32[2,256,32]{1,2,0:T(8,128)S(1)} %copy-done.12, f32[2,32,64,256]{3,2,1,0:T(8,128)S(1)} %fusion.23, ...), kind=kOutput, calls=%fused_computation.17 | convolution fusion | flops 566214656 | bytes 15466624 | tf_op jit(solution)/shard_map/hcqk,ckhp->cqhp/dot_general | solution.py:135
  164.4 6.6 %copy.75 = bf16[2,256,32,64]{3,2,1,0:T(8,128)(2,1)} copy(bf16[2,256,32,64]{1,3,2,0:T(8,128)(2,1)S(1)} %multiply_convert_fusion.4) | data formatting | bytes 4194304 | tf_op jit(solution)/shard_map/convert_element_type | solution.py:145
  171.0 6.0 %reshape.542 = bf16[64,8,2048]{2,1,0:T(8,128)(2,1)S(1)} reshape(bf16[2,256,32,64]{3,2,1,0:T(8,128)(2,1)} %copy.75) | data formatting | bytes 4194304 | tf_op jit(solution)/shard_map/reshape | solution.py:146
  177.1 7.3 %fusion.14 = bf16[64,8,1536]{2,1,0:T(8,128)(2,1)} fusion(bf16[64,8,2048]{2,1,0:T(8,128)(2,1)S(1)} %reshape.542, bf16[2048,1536]{1,0:T(8,128)(2,1)} %param.17), kind=kOutput, calls=%fused_computation.20 | convolution fusion | flops 3222011904 | bytes 9961472 | tf_op jit(solution)/shard_map/bpd,de->bpe/dot_general | solution.py:149
  184.4 11.9 %all-to-all-start.3 = ((bf16[64,8,1536]{2,1,0:T(8,128)(2,1)}), bf16[64,8,1536]{2,1,0:T(8,128)(2,1)S(1)}, u32[]{:S(2)}, u32[]{:S(2)}) async-start(bf16[64,8,1536]{2,1,0:T(8,128)(2,1)} %fusion.14), calls=%async_computation.3 | async-start | bytes 3145728 | tf_op jit(solution)/shard_map/all_to_all | solution.py:148
  196.4 38.9 %all-to-all-done.3 = bf16[64,8,1536]{2,1,0:T(8,128)(2,1)S(1)} async-done(((bf16[64,8,1536]{2,1,0:T(8,128)(2,1)}), bf16[64,8,1536]{2,1,0:T(8,128)(2,1)S(1)}, u32[]{:S(2)}, u32[]{:S(2)}) %all-to-all-start.3) | async-done | bytes 1572896 | tf_op jit(solution)/shard_map/all_to_all | solution.py:148
  235.3 0.6 gather_fusion
  236.0 1.4 broadcast_select_fusion
  (86 shorter events, 4.0 us)
Async XLA Ops:
  6.5 147.6 %copy-start = (bf16[1,1,512,128]{3,2,1,0:T(8,128)(2,1)S(1)}, bf16[1,1,512,128]{3,2,1,0:T(8,128)(2,1)}, u32[]{:S(2)}) copy-start(bf16[1,1,512,128]{3,2,1,0:T(8,128)(2,1)} %param.13) | copy-start | bytes 393220
  9.0 0.6 copy-start.10
  10.9 25.2 %all-to-all-start = ((f32[4,1,32]{2,1,0:T(1,128)}), f32[4,1,32]{2,1,0:T(1,128)S(1)}, u32[]{:S(2)}, u32[]{:S(2)}) async-start(f32[4,1,32]{2,1,0:T(1,128)} %broadcast_in_dim.199), calls=%async_computation | async-start | bytes 4096 | tf_op jit(solution)/shard_map/all_to_all | solution.py:21
  17.1 5.2 %copy-start.8 = (bf16[1,1,512,128]{3,2,1,0:T(8,128)(2,1)S(1)}, bf16[1,1,512,128]{3,2,1,0:T(8,128)(2,1)}, u32[]{:S(2)}) copy-start(bf16[1,1,512,128]{3,2,1,0:T(8,128)(2,1)} %param.12) | copy-start | bytes 393220
  22.3 5.8 %copy-start.19 = (s32[1,4]{1,0:T(1,128)S(1)}, s32[1,4]{1,0:T(1,128)}, u32[]{:S(2)}) copy-start(s32[1,4]{1,0:T(1,128)} %param.18) | copy-start | bytes 52
  22.3 6.5 %copy-start.23 = (u32[256]{0:T(256)S(1)}, u32[256]{0:T(256)}, u32[]{:S(2)}) copy-start(u32[256]{0:T(256)} %constant.87) | copy-start | bytes 3076
  22.4 7.1 %copy-start.22 = (u32[256]{0:T(256)S(1)}, u32[256]{0:T(256)}, u32[]{:S(2)}) copy-start(u32[256]{0:T(256)} %constant.82) | copy-start | bytes 3076
  36.1 20.2 %all-to-all-start.1 = ((f32[4,8,64,128]{3,2,1,0:T(8,128)}), f32[4,8,64,128]{3,2,1,0:T(8,128)S(1)}, u32[]{:S(2)}, u32[]{:S(2)}) async-start(f32[4,8,64,128]{3,2,1,0:T(8,128)} %bitcast_add_fusion), calls=%async_computation.1 | async-start | bytes 2097152 | tf_op jit(solution)/shard_map/all_to_all | solution.py:108
  40.4 49.8 %all-gather.7.cloned.1.call-start = ((), (), s32[]{:S(2)}) async-start(), calls=%async_computation.4 | async-start | bytes 1310720 | tf_op jit(solution)/shard_map/all_gather | solution.py:46
  63.5 67.5 %all-gather.9.cloned.1.call-start = ((), (), s32[]{:S(2)}) async-start(), calls=%async_computation.5 | async-start | bytes 2359296 | tf_op jit(solution)/shard_map/all_gather | solution.py:46
  131.0 2.6 %copy-start.4 = (f32[8,64,128]{2,1,0:T(8,128)S(1)}, f32[8,64,128]{2,1,0:T(8,128)}, u32[]{:S(2)}) copy-start(f32[8,64,128]{2,1,0:T(8,128)} %get-tuple-element.6) | copy-start | bytes 786436
  131.0 2.6 %copy-start.5 = (f32[8,64,128]{2,1,0:T(8,128)S(1)}, f32[8,64,128]{2,1,0:T(8,128)}, u32[]{:S(2)}) copy-start(f32[8,64,128]{2,1,0:T(8,128)} %get-tuple-element.7) | copy-start | bytes 786436
  131.0 2.6 %copy-start.6 = (f32[8,64,128]{2,1,0:T(8,128)S(1)}, f32[8,64,128]{2,1,0:T(8,128)}, u32[]{:S(2)}) copy-start(f32[8,64,128]{2,1,0:T(8,128)} %get-tuple-element.8) | copy-start | bytes 786436
  131.0 2.6 %copy-start.16 = (f32[8]{0:T(128)S(1)}, f32[8]{0:T(128)}, u32[]{:S(2)}) copy-start(f32[8]{0:T(128)} %get-tuple-element.39) | copy-start | bytes 100
  131.0 2.6 %copy-start.17 = (f32[8]{0:T(128)S(1)}, f32[8]{0:T(128)}, u32[]{:S(2)}) copy-start(f32[8]{0:T(128)} %get-tuple-element.40) | copy-start | bytes 100
  131.0 2.6 %copy-start.18 = (f32[8]{0:T(128)S(1)}, f32[8]{0:T(128)}, u32[]{:S(2)}) copy-start(f32[8]{0:T(128)} %get-tuple-element.41) | copy-start | bytes 100
  134.8 20.4 %all-to-all-start.2 = ((f32[4,8,64,128]{3,2,1,0:T(8,128)}), f32[4,8,64,128]{3,2,1,0:T(8,128)S(1)}, u32[]{:S(2)}, u32[]{:S(2)}) async-start(f32[4,8,64,128]{3,2,1,0:T(8,128)} %pad_maximum_fusion), calls=%async_computation.2 | async-start | bytes 2097152 | tf_op jit(solution)/shard_map/all_to_all | solution.py:126
  146.2 7.9 %copy-start.13 = (f32[2048]{0:T(1024)S(1)}, f32[2048]{0:T(1024)}, u32[]{:S(2)}) copy-start(f32[2048]{0:T(1024)} %param.16) | copy-start | bytes 24580
  146.2 8.0 %copy-start.9 = (bf16[1,1,512,128]{3,2,1,0:T(8,128)(2,1)S(1)}, bf16[1,1,512,128]{3,2,1,0:T(8,128)(2,1)}, u32[]{:S(2)}) copy-start(bf16[1,1,512,128]{3,2,1,0:T(8,128)(2,1)} %param.12) | copy-start | bytes 393220
  146.2 9.2 %copy-start.14 = (f32[32]{0:T(128)S(1)}, f32[32]{0:T(128)}, u32[]{:S(2)}) copy-start(f32[32]{0:T(128)} %get-tuple-element.45) | copy-start | bytes 388
  146.2 9.2 %copy-start.15 = (f32[32]{0:T(128)S(1)}, f32[32]{0:T(128)}, u32[]{:S(2)}) copy-start(f32[32]{0:T(128)} %get-tuple-element.43) | copy-start | bytes 388
  155.3 2.2 copy-start.2
  155.3 2.9 %copy-start.3 = (bf16[2,256,32,64]{1,0,3,2:T(2,128)(2,1)S(1)}, bf16[2,256,32,64]{1,0,3,2:T(2,128)(2,1)}, u32[]{:S(2)}) copy-start(bf16[2,256,32,64]{1,0,3,2:T(2,128)(2,1)} %reshape_squeeze.13) | copy-start | bytes 6291460
  155.3 2.9 %copy-start.7 = (f32[2,256,256]{2,1,0:T(8,128)S(1)}, f32[2,256,256]{2,1,0:T(8,128)}, u32[]{:S(2)}) copy-start(f32[2,256,256]{2,1,0:T(8,128)} %fusion.40) | copy-start | bytes 1572868
  155.3 2.9 %copy-start.11 = (f32[32,2,256]{2,0,1:T(8,128)S(1)}, f32[32,2,256]{2,0,1:T(8,128)}, u32[]{:S(2)}) copy-start(f32[32,2,256]{2,0,1:T(8,128)} %copy-done.10) | copy-start | bytes 196612
  155.3 2.9 %copy-start.12 = (f32[2,256,32]{1,2,0:T(8,128)S(1)}, f32[2,256,32]{1,2,0:T(8,128)}, u32[]{:S(2)}) copy-start(f32[2,256,32]{1,2,0:T(8,128)} %get-tuple-element.29) | copy-start | bytes 196612
  155.3 2.9 %copy-start.20 = (f32[32]{0:T(128)S(1)}, f32[32]{0:T(128)}, u32[]{:S(2)}) copy-start(f32[32]{0:T(128)} %param.15) | copy-start | bytes 388
  177.0 19.3 %copy-start.21 = (s32[1,4]{1,0:T(1,128)S(1)}, s32[1,4]{1,0:T(1,128)}, u32[]{:S(2)}) copy-start(s32[1,4]{1,0:T(1,128)} %param.19) | copy-start | bytes 52
  177.0 60.3 %copy-start.1 = (bf16[1,1,512,128]{3,2,1,0:T(8,128)(2,1)S(1)}, bf16[1,1,512,128]{3,2,1,0:T(8,128)(2,1)}, u32[]{:S(2)}) copy-start(bf16[1,1,512,128]{3,2,1,0:T(8,128)(2,1)} %param.13) | copy-start | bytes 393220
  184.4 50.9 %all-to-all-start.3 = ((bf16[64,8,1536]{2,1,0:T(8,128)(2,1)}), bf16[64,8,1536]{2,1,0:T(8,128)(2,1)S(1)}, u32[]{:S(2)}, u32[]{:S(2)}) async-start(bf16[64,8,1536]{2,1,0:T(8,128)(2,1)} %fusion.14), calls=%async_computation.3 | async-start | bytes 3145728 | tf_op jit(solution)/shard_map/all_to_all | solution.py:148
Sparse Core Ops, SparseCore 0:
  63.6 26.4 all-gather.6
  92.3 38.6 all-gather.8
where the time goes:
time: 246 us; the launch traced here: 244 us
  waiting for transfers between devices  90 us (37%)
  local copies, waits for them, and re-layouts  42.2 us (17%)
  blocking collectives  29.4 us (12%)
  starting transfers between devices  25 us (10%)
  other arithmetic  23.3 us (9%)
  matrix products  19.2 us (8%)
  between operations  15 us (6%)
    all_gather x2, waiting for transfers between devices, entering_2(): pieces = jax.tree.map(lambda part: lax.all_gather(part, axis), total)  51.1 us
    all_to_all x1, waiting for transfers between devices, shards(): lax.all_to_all(jnp.einsum('bpd,de->bpe', normed, out_weight, preferred_el...  38.9 us
    all_gather x2, blocking collectives, entering_2(): pieces = jax.tree.map(lambda part: lax.all_gather(part, axis), total)  16.5 us
    convert_element_type x2, local copies, waits for them, and re-layouts, shards(): gate_input[0, 0].reshape(group_count, GROUP, H, HEAD).astype(jnp.float32)  15.2 us
    unnamed x2, blocking collectives  12.9 us
    all_to_all x1, starting transfers between devices, shards(): lax.all_to_all(jnp.einsum('bpd,de->bpe', normed, out_weight, preferred_el...  11.9 us
    dot_general x1, matrix products, shards(): jnp.einsum('bpd,de->bpe', normed, out_weight, preferred_element_type=jnp....  7.31 us
    unnamed x54, local copies, waits for them, and re-layouts  6.9 us
  transfers between devices with their start and end apart: 6, of which 3 were waited for; matrix products, arithmetic and copies ran while one was open for 16% of the time, Pallas kernels for 0%

commit v1 on v0

v1 whole, which is shorter than its diff:
```python
import functools

import jax
import jax.numpy as jnp
from jax import lax
from jax.experimental import pallas as pl
from jax.experimental.pallas import tpu as pltpu
from jax.sharding import Mesh
from jax.sharding import PartitionSpec as P

H = 32
HEAD = 64
N = 128
TILE = 128
TOKENS_PER_BLOCK = 512
DI = H * HEAD
CHUNK = 128
CHUNKS = TOKENS_PER_BLOCK // CHUNK
COLS = 512
EPS = 1e-05
SEQ = ("z", "y", "core")
PLANE = ("y", "core", "view")
TAIL = 16
ROWS = HEAD + TAIL
BF = jnp.bfloat16
F32 = jnp.float32
MIB = 2**20


def dot(a, b, contract=(1, 0)):
    return lax.dot_general(
        a, b, (((contract[0],), (contract[1],)), ((), ())), preferred_element_type=F32
    )


def three_terms(x):
    hi = x.astype(BF).astype(F32)
    rest = x - hi
    mid = rest.astype(BF).astype(F32)
    return hi, mid, rest - mid


def sums_over(mask, logs):
    return sum(dot(mask, part.astype(BF), (1, 1)) for part in three_terms(logs))


def halves(x):
    hi = x.astype(BF).astype(F32)
    lane = lax.broadcasted_iota(jnp.int32, x.shape, x.ndim - 1)
    return jnp.where(lane < H, hi, x - hi).astype(BF)


def spread(first_head, heads_twice=True):
    shape = (2 * H if heads_twice else H, COLS)
    head = lax.broadcasted_iota(jnp.int32, shape, 0) % H
    column = lax.broadcasted_iota(jnp.int32, shape, 1) // HEAD + first_head
    return jnp.where(head == column, 1.0, 0.0).astype(BF)


def state_kernel(order_ref, log_ref, b_ref, x_ref, out_ref, w_scr, decay_scr, bt_scr):
    step = pl.program_id(0)

    @pl.when(step == 0)
    def _():
        logs = log_ref[...]
        row = lax.broadcasted_iota(jnp.int32, (TOKENS_PER_BLOCK, TOKENS_PER_BLOCK), 0)
        column = lax.broadcasted_iota(jnp.int32, (TOKENS_PER_BLOCK, TOKENS_PER_BLOCK), 1)
        after = jnp.where(column > row, 1.0, 0.0).astype(BF)
        w_scr[...] = halves(jnp.exp(sums_over(after, jnp.concatenate([logs, logs], axis=0))))
        total = jnp.exp(jnp.sum(logs, axis=1, keepdims=True))
        decay_scr[...] = jnp.broadcast_to(total, (H, N))
        bt_scr[...] = b_ref[...].astype(F32).T.astype(BF)

    heads = COLS // HEAD
    weight = dot(w_scr[...], spread(step * heads))
    scaled = (x_ref[...].astype(F32) * weight).astype(BF)
    state = dot(bt_scr[...], scaled)
    out_ref[:, 0:HEAD, :] = state.T.astype(BF).reshape(heads, HEAD, N)
    view = lax.axis_index("view")
    rank = jnp.int32(0)
    for k in range(1, 4):
        rank = rank + jnp.where(order_ref[0, k] == view, k, 0)
    decay = decay_scr[pl.ds(pl.multiple_of(step * heads, heads), heads), :]
    hi, mid, lo = (part[:, None, :] for part in three_terms(decay))
    place = lax.broadcasted_iota(jnp.int32, (heads, TAIL, N), 1)
    tail = jnp.where(place == 0, hi, jnp.where(place == 1, mid, jnp.where(place == 2, lo, 0.0)))
    tail = jnp.where(place == 3, rank.astype(F32), tail)
    out_ref[:, HEAD:ROWS, :] = tail.astype(BF)


def block_states(order, logs, b, x):
    steps = DI // COLS
    heads = COLS // HEAD
    return pl.pallas_call(
        state_kernel,
        grid=(steps,),
        in_specs=[
            pl.BlockSpec(memory_space=pltpu.SMEM),
            pl.BlockSpec((H, TOKENS_PER_BLOCK), lambda i: (0, 0)),
            pl.BlockSpec((TOKENS_PER_BLOCK, N), lambda i: (0, 0)),
            pl.BlockSpec((TOKENS_PER_BLOCK, COLS), lambda i: (0, i)),
        ],
        out_specs=pl.BlockSpec((heads, ROWS, N), lambda i: (i, 0, 0)),
        out_shape=jax.ShapeDtypeStruct((H, ROWS, N), BF),
        scratch_shapes=[
            pltpu.VMEM((TOKENS_PER_BLOCK, 2 * H), BF),
            pltpu.VMEM((H, N), F32),
            pltpu.VMEM((N, TOKENS_PER_BLOCK), BF),
        ],
        compiler_params=pltpu.CompilerParams(vmem_limit_bytes=16 * MIB),
        cost_estimate=pl.CostEstimate(flops=2 * 10**9, bytes_accessed=3 * MIB, transcendentals=0),
        name="block_states",
    )(order, logs, b, x)


def read_tail(ref, at):
    tail = ref[at, HEAD:ROWS, :].astype(F32)
    return tail[0:1] + tail[1:2] + tail[2:3], tail[3:4]


def scan_plane(ref, running, emit):
    views = 4
    product = jnp.ones((1, N), F32)
    for band in range(ref.shape[0] // views):
        blocks = [band * views + v for v in range(views)]
        states = [ref[k, 0:HEAD, :].astype(F32) for k in blocks]
        decays, ranks = zip(*(read_tail(ref, k) for k in blocks))
        entering = [None] * views
        for place in range(views):
            chosen, decay = states[0], decays[0]
            for v in range(views):
                here = ranks[v] == float(place)
                entering[v] = running if place == 0 else jnp.where(here, running, entering[v])
                if v:
                    chosen = jnp.where(here, states[v], chosen)
                    decay = jnp.where(here, decays[v], decay)
            running = decay * running + chosen
            product = product * decay
        if emit is not None:
            for v in range(views):
                emit(blocks[v], entering[v])
    return running, product


def total_kernel(in_ref, out_ref):
    total, product = scan_plane(in_ref, jnp.zeros((HEAD, N), F32), None)
    hi, mid, lo = three_terms(product)
    place = lax.broadcasted_iota(jnp.int32, (TAIL, N), 0)
    tail = jnp.where(place == 0, hi, jnp.where(place == 1, mid, jnp.where(place == 2, lo, 0.0)))
    for k in range(out_ref.shape[0]):
        out_ref[k, 0:HEAD, :] = total.astype(BF)
        out_ref[k, HEAD:ROWS, :] = tail.astype(BF)


def plane_totals(states, planes):
    return pl.pallas_call(
        total_kernel,
        out_shape=jax.ShapeDtypeStruct((planes, ROWS, N), BF),
        compiler_params=pltpu.CompilerParams(vmem_limit_bytes=8 * MIB),
        cost_estimate=pl.CostEstimate(flops=10**6, bytes_accessed=MIB, transcendentals=0),
        name="plane_totals",
    )(states)


def entering_kernel(in_ref, totals_ref, out_ref):
    mine = lax.axis_index("z")
    carry = jnp.zeros((HEAD, N), F32)
    for k in range(totals_ref.shape[0] - 1):
        decay, _ = read_tail(totals_ref, k)
        later = decay * carry + totals_ref[k, 0:HEAD, :].astype(F32)
        carry = jnp.where(k < mine, later, carry)

    def emit(block, value):
        out_ref[block, :, :] = value.astype(BF)

    scan_plane(in_ref, carry, emit)


def entering_states(states, totals):
    return pl.pallas_call(
        entering_kernel,
        out_shape=jax.ShapeDtypeStruct((states.shape[0], HEAD, N), BF),
        compiler_params=pltpu.CompilerParams(vmem_limit_bytes=8 * MIB),
        cost_estimate=pl.CostEstimate(flops=10**6, bytes_accessed=2 * MIB, transcendentals=0),
        name="entering_states",
    )(states, totals)


def local_kernel(
    log_ref, skip_ref, b_ref, c_ref, x_ref, gate_ref, local_ref, factor_ref,
    bt_scr, left_scr, in_scr, out_scr, enter_scr, row_scr,
):
    step = pl.program_id(0)

    @pl.when(step == 0)
    def _():
        logs = log_ref[...]
        shape = (TOKENS_PER_BLOCK, TOKENS_PER_BLOCK)
        row = lax.broadcasted_iota(jnp.int32, shape, 0)
        column = lax.broadcasted_iota(jnp.int32, shape, 1)
        upto = (column <= row) & (column // CHUNK == row // CHUNK)
        sums = sums_over(
            jnp.where(upto, 1.0, 0.0).astype(BF), jnp.concatenate([logs, logs], axis=0)
        )
        before = jnp.zeros((1, 2 * H), F32)
        row_scr[...] = jnp.zeros_like(row_scr)
        causal = upto[0:CHUNK, 0:CHUNK]
        for k in range(CHUNKS):
            rows = slice(k * CHUNK, (k + 1) * CHUNK)
            part = sums[rows]
            middle = part[CHUNK // 2 - 1 : CHUNK // 2]
            end = part[CHUNK - 1 : CHUNK]
            in_scr[rows, :] = halves(jnp.exp(middle - part))
            out_scr[rows, :] = halves(jnp.exp(part - middle))
            enter_scr[rows, :] = halves(jnp.exp(before + part))
            row_scr[k : k + 1, :] = jnp.exp(end - middle)
            row_scr[4 + k : 5 + k, :] = jnp.exp(middle)
            row_scr[8 + k : 9 + k, :] = jnp.exp(end)
            before = before + end
            b_part, c_part = b_ref[rows, :], c_ref[rows, :]
            bt_scr[k] = b_part.astype(F32).T.astype(BF)
            scores = dot(c_part, b_part, (1, 1))
            left_scr[k, :, 0:CHUNK] = jnp.where(causal, scores, 0.0).astype(BF)
            left_scr[k, :, CHUNK : CHUNK + N] = c_part

    heads = COLS // HEAD
    twice = spread(step * heads)
    once = spread(step * heads, False)
    ends = dot(halves(row_scr[...]), twice)
    skip_parts = three_terms(jnp.broadcast_to(skip_ref[...], (16, H)))
    skip = sum(dot(part.astype(BF), once) for part in skip_parts)[0:1]
    running = None
    for k in range(CHUNKS):
        rows = slice(k * CHUNK, (k + 1) * CHUNK)
        x = x_ref[rows, :].astype(F32)
        scaled = (x * dot(in_scr[rows, :], twice)).astype(BF)
        if running is None:
            inner = dot(left_scr[k, :, 0:CHUNK], scaled)
        else:
            carried = (running * ends[4 + k : 5 + k]).astype(BF)
            inner = dot(left_scr[k], jnp.concatenate([scaled, carried], axis=0))
        if k + 1 < CHUNKS:
            made = dot(bt_scr[k], scaled) * ends[k : k + 1]
            running = made if running is None else running * ends[8 + k : 9 + k] + made
        gate = gate_ref[rows, :].astype(F32)
        opened = gate / (1.0 + jnp.exp(-gate))
        mixed = inner * dot(out_scr[rows, :], twice) + skip * x
        local_ref[rows, :] = mixed * opened
        factor_ref[rows, :] = dot(enter_scr[rows, :], twice) * opened


def local_part(logs, skip, b, c, x, gate):
    whole = lambda i: (0, 0)
    columns = lambda i: (0, i)
    shape = jax.ShapeDtypeStruct((TOKENS_PER_BLOCK, DI), F32)
    return pl.pallas_call(
        local_kernel,
        grid=(DI // COLS,),
        in_specs=[
            pl.BlockSpec((H, TOKENS_PER_BLOCK), whole),
            pl.BlockSpec((1, H), whole),
            pl.BlockSpec((TOKENS_PER_BLOCK, N), whole),
            pl.BlockSpec((TOKENS_PER_BLOCK, N), whole),
            pl.BlockSpec((TOKENS_PER_BLOCK, COLS), columns),
            pl.BlockSpec((TOKENS_PER_BLOCK, COLS), columns),
        ],
        out_specs=[pl.BlockSpec((TOKENS_PER_BLOCK, COLS), columns)] * 2,
        out_shape=[shape, shape],
        scratch_shapes=[
            pltpu.VMEM((CHUNKS, N, CHUNK), BF),
            pltpu.VMEM((CHUNKS, CHUNK, CHUNK + N), BF),
            pltpu.VMEM((TOKENS_PER_BLOCK, 2 * H), BF),
            pltpu.VMEM((TOKENS_PER_BLOCK, 2 * H), BF),
            pltpu.VMEM((TOKENS_PER_BLOCK, 2 * H), BF),
            pltpu.VMEM((16, 2 * H), F32),
        ],
        compiler_params=pltpu.CompilerParams(vmem_limit_bytes=24 * MIB),
        cost_estimate=pl.CostEstimate(
            flops=8 * 10**9, bytes_accessed=12 * MIB, transcendentals=2 * 10**6
        ),
        name="local_part",
    )(logs, skip, b, c, x, gate)


def output_kernel(state_ref, c_ref, local_ref, factor_ref, gain_ref, weight_ref, out_ref, normed_scr):
    width = 256
    shape = (width, width)
    same = (
        lax.broadcasted_iota(jnp.int32, shape, 0) // HEAD
        == lax.broadcasted_iota(jnp.int32, shape, 1) // HEAD
    )
    mean_of = jnp.where(same, 1.0 / HEAD, 0.0).astype(BF)
    c = c_ref[...]
    for k in range(DI // width):
        columns = slice(k * width, (k + 1) * width)
        carried = dot(c, state_ref[columns, :], (1, 1))
        gated = local_ref[:, columns] + factor_ref[:, columns] * carried
        square = gated * gated
        hi = square.astype(BF)
        mean = dot(hi, mean_of) + dot((square - hi.astype(F32)).astype(BF), mean_of)
        normed = gated * lax.rsqrt(mean + EPS) * gain_ref[:, columns]
        normed_scr[:, columns] = normed.astype(BF)
    out_ref[...] = dot(normed_scr[...], weight_ref[...]).astype(BF)


def projected_tokens(state, c, local, factor, gain, weight):
    rows = 128
    width_out = weight.shape[1]
    whole = lambda i: (0, 0)
    block = lambda i: (i, 0)
    return pl.pallas_call(
        output_kernel,
        grid=(TOKENS_PER_BLOCK // rows,),
        in_specs=[
            pl.BlockSpec((DI, N), whole),
            pl.BlockSpec((rows, N), block),
            pl.BlockSpec((rows, DI), block),
            pl.BlockSpec((rows, DI), block),
            pl.BlockSpec((1, DI), whole),
            pl.BlockSpec((DI, width_out), whole),
        ],
        out_specs=pl.BlockSpec((rows, width_out), block),
        out_shape=jax.ShapeDtypeStruct((TOKENS_PER_BLOCK, width_out), BF),
        scratch_shapes=[pltpu.VMEM((rows, DI), BF)],
        compiler_params=pltpu.CompilerParams(vmem_limit_bytes=32 * MIB),
        cost_estimate=pl.CostEstimate(
            flops=4 * 10**9, bytes_accessed=16 * MIB, transcendentals=10**6
        ),
        name="projected_tokens",
    )(state, c, local, factor, gain, weight)


def tile_kernel(order_ref, in_ref, out_ref, sems):
    tiles = TOKENS_PER_BLOCK // TILE
    copies = [
        pltpu.make_async_copy(
            in_ref.at[pl.ds(pl.multiple_of(order_ref[0, k] * TILE, TILE), TILE), :],
            out_ref.at[pl.ds(k * TILE, TILE), :],
            sems.at[k],
        )
        for k in range(tiles)
    ]
    for copy in copies:
        copy.start()
    for copy in copies:
        copy.wait()


def chosen_tiles(order, arrived):
    return pl.pallas_call(
        tile_kernel,
        in_specs=[pl.BlockSpec(memory_space=pltpu.SMEM), pl.BlockSpec(memory_space=pl.ANY)],
        out_specs=pl.BlockSpec(memory_space=pl.ANY),
        out_shape=jax.ShapeDtypeStruct(arrived.shape, arrived.dtype),
        scratch_shapes=[pltpu.SemaphoreType.DMA((TOKENS_PER_BLOCK // TILE,))],
        compiler_params=pltpu.CompilerParams(vmem_limit_bytes=MIB),
        cost_estimate=pl.CostEstimate(flops=0, bytes_accessed=3 * MIB, transcendentals=0),
        name="chosen_tiles",
    )(order, arrived)


def swapped(x, axes):
    return lax.all_to_all(x, axes, split_axis=0, concat_axis=0, tiled=True)


def shards(
    ssd_input,
    gate_input,
    b_matrix,
    c_matrix,
    log_decay,
    d_skip,
    norm_gain,
    out_weight,
    view_order,
    tile_order,
):
    bands = lax.axis_size(SEQ)
    width_out = out_weight.shape[1]
    x, gate, b, c = (part[0, 0] for part in (ssd_input, gate_input, b_matrix, c_matrix))
    logs = log_decay[0, 0]
    states = swapped(block_states(view_order, logs, b, x), PLANE)
    local, factor = local_part(logs, d_skip.reshape(1, H), b, c, x, gate)
    totals = swapped(plane_totals(states, lax.axis_size("z")), "z")
    entering = swapped(entering_states(states, totals), PLANE).reshape(DI, N)
    projected = projected_tokens(
        entering, c, local, factor, norm_gain.reshape(1, DI), out_weight
    )
    arrived = swapped(projected.reshape(bands, TOKENS_PER_BLOCK // bands, width_out), SEQ)
    chosen = chosen_tiles(tile_order, arrived.reshape(TOKENS_PER_BLOCK, width_out))
    return chosen.reshape(1, 1, TOKENS_PER_BLOCK, width_out)


def solution(mesh):
    split = Mesh(mesh.devices.reshape(8, 4, 2, mesh.shape["view"]), (*SEQ, "view"))
    whole = P(SEQ, "view", None, None)
    in_specs = (whole,) * 5 + (P(),) * 3 + (P(SEQ, None),) * 2
    return jax.shard_map(shards, mesh=split, in_specs=in_specs, out_specs=whole, check_vma=False)
```

time: 246 us -> 127 us (0.52)
  waiting for transfers between devices: 90 us -> 0.01 us
  blocking collectives: 29.4 us -> 81.4 us
  local copies, waits for them, and re-layouts: 42.2 us -> 16.7 us
  other arithmetic: 23.3 us -> 0 us
  Pallas kernels: 0 us -> 22.1 us
  matrix products: 19.2 us -> 0 us
  starting transfers between devices: 25 us -> 6.21 us
  between operations: 15 us -> 0.12 us
    all_to_all x0 -> x3, blocking collectives: none -> 81.4 us  [swapped(): return lax.all_to_all(x, axes, split_axis=0, concat_axis=0, tiled=True)]
    all_gather x2 -> x0, waiting for transfers between devices: 51.1 us -> none  [entering_2(): pieces = jax.tree.map(lambda part: lax.all_gather(part, axis), total)]
    all_to_all x4 -> x1, waiting for transfers between devices: 38.9 us -> 0.01 us  [swapped(): return lax.all_to_all(x, axes, split_axis=0, concat_axis=0, tiled=True)]
    pallas_call x0 -> x6, Pallas kernels: none -> 22.1 us  [the longest x1 7.76 us: local_part(): pl.pallas_call(local_kernel, grid=(DI // COLS,), in_specs=[pl.BlockSpec((...]
    convert_element_type x3 -> x0, local copies, waits for them, and re-layouts: 21.9 us -> none  [the longest x2 15.2 us: shards(): gate_input[0, 0].reshape(group_count, GROUP, H, HEAD).astype(jnp.float32)]
    dot_general x5 -> x0, matrix products: 19.2 us -> none  [the longest x1 7.31 us: shards(): jnp.einsum('bpd,de->bpe', normed, out_weight, preferred_element_type=jnp....]
    all_to_all x4 -> x1, starting transfers between devices: 25 us -> 6.21 us  [swapped(): return lax.all_to_all(x, axes, split_axis=0, concat_axis=0, tiled=True)]
    all_gather x2 -> x0, blocking collectives: 16.5 us -> none  [entering_2(): pieces = jax.tree.map(lambda part: lax.all_gather(part, axis), total)]
  transfers between devices with their start and end apart: 6 -> 1, of which waited for: 3 -> 0; matrix products, arithmetic and copies ran while one was open for 16% -> 0% of each run, Pallas kernels for 0% -> 6%
where the time goes in v1:
time: 127 us; the launch traced here: 126 us
  blocking collectives  81.4 us (64%)
  Pallas kernels  22.1 us (17%)
  local copies, waits for them, and re-layouts  16.7 us (13%)
  starting transfers between devices  6.21 us (5%)
    all_to_all x3, blocking collectives, swapped(): return lax.all_to_all(x, axes, split_axis=0, concat_axis=0, tiled=True)  81.4 us
    unnamed x34, local copies, waits for them, and re-layouts  16.7 us
    pallas_call x1, Pallas kernels, local_part(): pl.pallas_call(local_kernel, grid=(DI // COLS,), in_specs=[pl.BlockSpec((...  7.76 us
    pallas_call x1, Pallas kernels, projected_tokens(): pl.pallas_call(output_kernel, grid=(TOKENS_PER_BLOCK // rows,), in_specs=...  7.51 us
    all_to_all x1, starting transfers between devices, swapped(): return lax.all_to_all(x, axes, split_axis=0, concat_axis=0, tiled=True)  6.21 us
    pallas_call x1, Pallas kernels, block_states(): pl.pallas_call(state_kernel, grid=(steps,), in_specs=[pl.BlockSpec(memory...  3.49 us
  transfers between devices with their start and end apart: 1, of which 0 were waited for; matrix products, arithmetic and copies ran while one was open for 0% of the time, Pallas kernels for 6%

profile of v1, /device:TPU:1, one launch (start us, length us, event | category | flops | bytes accessed | tf_op | source)
XLA Modules:
  0.0 126.5 jit_solution(14669127464585847802)
XLA Ops:
  0.0 0.0 copy-start.8
  0.0 1.6 %copy-done.8 = bf16[1,1,512,2048]{3,2,1,0:T(8,128)(2,1)S(1)} copy-done((bf16[1,1,512,2048]{3,2,1,0:T(8,128)(2,1)S(1)}, bf16[1,1,512,2048]{3,2,1,0:T(8,128)(2,1)}, u32[]{:S(2)}) %copy-start.8) | copy-done | bytes 2097176
  1.6 0.0 copy-start.11
  1.6 0.9 copy-done.11
  2.5 0.0 copy-start.13
  2.5 0.8 copy-done.13
  3.3 0.0 copy-start.15
  3.3 0.7 copy-done.15
  4.0 3.5 %block_states.1 = bf16[32,80,128]{2,1,0:T(8,128)(2,1)S(1)} custom-call(s32[1,4]{1,0:T(1,128)S(1)} %copy-done.15, f32[32,512]{1,0:T(8,128)S(1)} %bitcast.22, bf16[512,128]{1,0:T(8,128)(2,1)S(1)} %bitcast.20, bf16[512,2048]{1,0:T(8,128)(2,1)S(1)} %bitcast.17), custom_call_target="tpu_custom_call" | custom-call | flops 2000000000 | bytes 3145728 | tf_op jit(solution)/shard_map/block_states/pallas_call | solution.py:94
  7.5 20.9 %all_to_all.20.in_ref = bf16[32,80,128]{2,1,0:T(8,128)(2,1)S(1)} all-to-all(bf16[32,80,128]{2,1,0:T(8,128)(2,1)S(1)} %block_states.1), channel_id=1, replica_groups=mesh['z'=8,'y'=4,'core'=2,'view'=4] {'y','core','view'}, dimensions={0} | all-to-all | bytes 1310720 | tf_op jit(solution)/shard_map/all_to_all | solution.py:363
  28.4 0.0 copy-start.5
  28.4 0.0 copy-start.9
  28.4 0.0 copy-start.12
  28.4 0.0 copy-start.14
  28.4 0.0 copy-start.16
  28.4 0.4 plane_totals.1
  28.8 16.2 %all_to_all.21.totals_ref = bf16[8,80,128]{2,1,0:T(8,128)(2,1)S(1)} all-to-all(bf16[8,80,128]{2,1,0:T(8,128)(2,1)S(1)} %plane_totals.1), channel_id=1, replica_groups=mesh['z'=8,'y'=4,'core'=2,'view'=4] {'z'}, dimensions={0} | all-to-all | bytes 327680 | tf_op jit(solution)/shard_map/all_to_all | solution.py:363
  45.0 1.3 entering_states.1
  46.3 6.2 %all-to-all-start.2 = ((bf16[32,64,128]{2,1,0:T(8,128)(2,1)}), bf16[32,64,128]{2,1,0:T(8,128)(2,1)S(1)}, u32[]{:S(2)}, u32[]{:S(2)}) async-start(bf16[32,64,128]{2,1,0:T(8,128)(2,1)} %entering_states.1), calls=%async_computation.2 | async-start | bytes 1048576 | tf_op jit(solution)/shard_map/all_to_all | solution.py:363
  52.5 0.0 copy-done.5
  52.5 0.0 copy-done.9
  52.5 0.0 copy-done.12
  52.5 0.0 copy-done.14
  52.5 0.0 copy-done.16
  52.5 0.0 copy-start.10
  52.5 1.6 %copy-done.10 = bf16[1,1,512,2048]{3,2,1,0:T(8,128)(2,1)S(1)} copy-done((bf16[1,1,512,2048]{3,2,1,0:T(8,128)(2,1)S(1)}, bf16[1,1,512,2048]{3,2,1,0:T(8,128)(2,1)}, u32[]{:S(2)}) %copy-start.10) | copy-done | bytes 2097176
  54.1 0.0 copy-start.6
  54.1 7.8 %local_part.1 = (f32[512,2048]{1,0:T(8,128)S(1)}, f32[512,2048]{1,0:T(8,128)S(1)}) custom-call(f32[32,512]{1,0:T(8,128)S(1)} %bitcast.23, f32[1,32]{1,0:T(1,128)S(1)} %bitcast.24, bf16[512,128]{1,0:T(8,128)(2,1)S(1)} %bitcast.21, bf16[512,128]{1,0:T(8,128)(2,1)S(1)} %bitcast.14, bf16[512,2048]{1,0:T(8,128)(2,1)S(1)} %bitcast.18, bf16[512,2048]{1,0:T(8,128)(2,1)S(1)} %bitcast.19), custom_call_target="tpu_custom_call" | custom-call | flops 8000000000 | bytes 12582912 | tf_op jit(solution)/shard_map/local_part/pallas_call | solution.py:256
  61.9 0.0 copy-start.1
  61.9 1.9 %copy-done.1 = f32[512,2048]{1,0:T(8,128)} copy-done((f32[512,2048]{1,0:T(8,128)}, f32[512,2048]{1,0:T(8,128)S(1)}, u32[]{:S(2)}) %copy-start.1) | copy-done | bytes 4194328
  63.8 0.0 copy-start.3
  63.9 2.0 %copy-done.3 = f32[512,2048]{1,0:T(8,128)} copy-done((f32[512,2048]{1,0:T(8,128)}, f32[512,2048]{1,0:T(8,128)S(1)}, u32[]{:S(2)}) %copy-start.3) | copy-done | bytes 4194328
  65.8 0.0 all-to-all-done.2
  65.8 0.0 copy-done.6
  65.8 0.0 copy-start
  65.8 2.8 %copy-done = bf16[2048,1536]{1,0:T(8,128)(2,1)S(1)} copy-done((bf16[2048,1536]{1,0:T(8,128)(2,1)S(1)}, bf16[2048,1536]{1,0:T(8,128)(2,1)}, u32[]{:S(2)}) %copy-start) | copy-done | bytes 6291480
  68.6 0.0 copy-start.2
  68.6 2.2 %copy-done.2 = f32[512,2048]{1,0:T(8,128)S(1)} copy-done((f32[512,2048]{1,0:T(8,128)S(1)}, f32[512,2048]{1,0:T(8,128)}, u32[]{:S(2)}) %copy-start.2) | copy-done | bytes 4194328
  70.8 0.0 copy-start.4
  70.8 2.2 %copy-done.4 = f32[512,2048]{1,0:T(8,128)S(1)} copy-done((f32[512,2048]{1,0:T(8,128)S(1)}, f32[512,2048]{1,0:T(8,128)}, u32[]{:S(2)}) %copy-start.4) | copy-done | bytes 4194328
  73.0 7.5 %projected_tokens.1 = bf16[512,1536]{1,0:T(8,128)(2,1)S(1)} custom-call(bf16[2048,128]{1,0:T(8,128)(2,1)S(1)} %bitcast.13, bf16[512,128]{1,0:T(8,128)(2,1)S(1)} %bitcast.15, f32[512,2048]{1,0:T(8,128)S(1)} %copy-done.2, f32[512,2048]{1,0:T(8,128)S(1)} %copy-done.4, f32[1,2048]{1,0:T(1,128)S(1)} %bitcast.16, bf16[2048,1536]{1,0:T(8,128)(2,1)S(1)} %copy-done), custom_call_target="tpu_custom_call" | custom-call | flops 4000000000 | bytes 16777216 | tf_op jit(solution)/shard_map/projected_tokens/pallas_call | solution.py:311
  80.5 0.0 copy-start.7
  80.5 44.2 %all_to_all.22 = bf16[64,8,1536]{2,1,0:T(8,128)(2,1)S(1)} all-to-all(bf16[64,8,1536]{2,1,0:T(8,128)(2,1)S(1)} %bitcast.12), channel_id=1, replica_groups=mesh['z'=8,'y'=4,'core'=2,'view'=4] {'z','y','core'}, dimensions={0} | all-to-all | bytes 3145728 | tf_op jit(solution)/shard_map/all_to_all | solution.py:363
  124.8 0.0 copy-done.7
  124.8 1.7 %chosen_tiles.1 = bf16[512,1536]{1,0:T(8,128)(2,1)} custom-call(s32[1,4]{1,0:T(1,128)S(1)} %copy-done.7, bf16[512,1536]{1,0:T(8,128)(2,1)S(1)} %bitcast.11), custom_call_target="tpu_custom_call" | custom-call | bytes 3145728 | tf_op jit(solution)/shard_map/chosen_tiles/pallas_call | solution.py:350
Async XLA Ops:
  0.0 1.6 %copy-start.8 = (bf16[1,1,512,2048]{3,2,1,0:T(8,128)(2,1)S(1)}, bf16[1,1,512,2048]{3,2,1,0:T(8,128)(2,1)}, u32[]{:S(2)}) copy-start(bf16[1,1,512,2048]{3,2,1,0:T(8,128)(2,1)} %param.10) | copy-start | bytes 6291460
  1.6 0.9 copy-start.11
  2.5 0.8 copy-start.13
  3.3 0.7 copy-start.15
  28.4 24.1 %copy-start.5 = (bf16[1,1,512,128]{3,2,1,0:T(8,128)(2,1)S(1)}, bf16[1,1,512,128]{3,2,1,0:T(8,128)(2,1)}, u32[]{:S(2)}) copy-start(bf16[1,1,512,128]{3,2,1,0:T(8,128)(2,1)} %param.13) | copy-start | bytes 393220
  28.4 24.1 %copy-start.9 = (bf16[1,1,512,2048]{3,2,1,0:T(8,128)(2,1)S(1)}, bf16[1,1,512,2048]{3,2,1,0:T(8,128)(2,1)}, u32[]{:S(2)}) copy-start(bf16[1,1,512,2048]{3,2,1,0:T(8,128)(2,1)} %param.10) | copy-start | bytes 6291460
  28.4 24.1 %copy-start.12 = (bf16[1,1,512,128]{3,2,1,0:T(8,128)(2,1)S(1)}, bf16[1,1,512,128]{3,2,1,0:T(8,128)(2,1)}, u32[]{:S(2)}) copy-start(bf16[1,1,512,128]{3,2,1,0:T(8,128)(2,1)} %param.12) | copy-start | bytes 393220
  28.4 24.1 %copy-start.14 = (f32[1,1,32,512]{3,2,1,0:T(8,128)S(1)}, f32[1,1,32,512]{3,2,1,0:T(8,128)}, u32[]{:S(2)}) copy-start(f32[1,1,32,512]{3,2,1,0:T(8,128)} %param.14) | copy-start | bytes 196612
  28.4 24.1 %copy-start.16 = (f32[32]{0:T(128)S(1)}, f32[32]{0:T(128)}, u32[]{:S(2)}) copy-start(f32[32]{0:T(128)} %param.15) | copy-start | bytes 388
  46.3 19.6 %all-to-all-start.2 = ((bf16[32,64,128]{2,1,0:T(8,128)(2,1)}), bf16[32,64,128]{2,1,0:T(8,128)(2,1)S(1)}, u32[]{:S(2)}, u32[]{:S(2)}) async-start(bf16[32,64,128]{2,1,0:T(8,128)(2,1)} %entering_states.1), calls=%async_computation.2 | async-start | bytes 1048576 | tf_op jit(solution)/shard_map/all_to_all | solution.py:363
  52.5 1.6 %copy-start.10 = (bf16[1,1,512,2048]{3,2,1,0:T(8,128)(2,1)S(1)}, bf16[1,1,512,2048]{3,2,1,0:T(8,128)(2,1)}, u32[]{:S(2)}) copy-start(bf16[1,1,512,2048]{3,2,1,0:T(8,128)(2,1)} %param.11) | copy-start | bytes 6291460
  54.1 11.7 %copy-start.6 = (f32[2048]{0:T(1024)S(1)}, f32[2048]{0:T(1024)}, u32[]{:S(2)}) copy-start(f32[2048]{0:T(1024)} %param.16) | copy-start | bytes 24580
  61.9 2.0 %copy-start.1 = (f32[512,2048]{1,0:T(8,128)}, f32[512,2048]{1,0:T(8,128)S(1)}, u32[]{:S(2)}) copy-start(f32[512,2048]{1,0:T(8,128)S(1)} %get-tuple-element.7.local_ref) | copy-start | bytes 12582916
  63.8 2.0 %copy-start.3 = (f32[512,2048]{1,0:T(8,128)}, f32[512,2048]{1,0:T(8,128)S(1)}, u32[]{:S(2)}) copy-start(f32[512,2048]{1,0:T(8,128)S(1)} %get-tuple-element.8.factor_ref) | copy-start | bytes 12582916
  65.8 2.8 %copy-start = (bf16[2048,1536]{1,0:T(8,128)(2,1)S(1)}, bf16[2048,1536]{1,0:T(8,128)(2,1)}, u32[]{:S(2)}) copy-start(bf16[2048,1536]{1,0:T(8,128)(2,1)} %weight_ref.1) | copy-start | bytes 18874372
  68.6 2.2 %copy-start.2 = (f32[512,2048]{1,0:T(8,128)S(1)}, f32[512,2048]{1,0:T(8,128)}, u32[]{:S(2)}) copy-start(f32[512,2048]{1,0:T(8,128)} %copy-done.1) | copy-start | bytes 12582916
  70.8 2.2 %copy-start.4 = (f32[512,2048]{1,0:T(8,128)S(1)}, f32[512,2048]{1,0:T(8,128)}, u32[]{:S(2)}) copy-start(f32[512,2048]{1,0:T(8,128)} %copy-done.3) | copy-start | bytes 12582916
  80.5 44.3 %copy-start.7 = (s32[1,4]{1,0:T(1,128)S(1)}, s32[1,4]{1,0:T(1,128)}, u32[]{:S(2)}) copy-start(s32[1,4]{1,0:T(1,128)} %order_ref.3) | copy-start | bytes 52

commit v2 on v1

--- a/solution.py
+++ b/solution.py
@@ -21,6 +21,7 @@
 SEQ = ("z", "y", "core")
 PLANE = ("y", "core", "view")
 TAIL = 16
+PIECES = 4
 ROWS = HEAD + TAIL
 BF = jnp.bfloat16
 F32 = jnp.float32
@@ -40,14 +41,26 @@
     return hi, mid, rest - mid
 
 
-def sums_over(mask, logs):
-    return sum(dot(mask, part.astype(BF), (1, 1)) for part in three_terms(logs))
+def chunk_sums(logs):
+    shape = (CHUNK, CHUNK)
+    row = lax.broadcasted_iota(jnp.int32, shape, 0)
+    column = lax.broadcasted_iota(jnp.int32, shape, 1)
+    upto = jnp.where(column <= row, 1.0, 0.0).astype(BF)
+    parts = [part.astype(BF) for part in three_terms(logs)]
+    return [
+        sum(dot(upto, part[:, k * CHUNK : (k + 1) * CHUNK], (1, 1)) for part in parts)
+        for k in range(CHUNKS)
+    ]
 
 
 def halves(x):
     hi = x.astype(BF).astype(F32)
     lane = lax.broadcasted_iota(jnp.int32, x.shape, x.ndim - 1)
     return jnp.where(lane < H, hi, x - hi).astype(BF)
+
+
+def in_hbm(x):
+    return pltpu.with_memory_space_constraint(x, pltpu.HBM)
 
 
 def spread(first_head, heads_twice=True):
@@ -63,10 +76,12 @@
     @pl.when(step == 0)
     def _():
         logs = log_ref[...]
-        row = lax.broadcasted_iota(jnp.int32, (TOKENS_PER_BLOCK, TOKENS_PER_BLOCK), 0)
-        column = lax.broadcasted_iota(jnp.int32, (TOKENS_PER_BLOCK, TOKENS_PER_BLOCK), 1)
-        after = jnp.where(column > row, 1.0, 0.0).astype(BF)
-        w_scr[...] = halves(jnp.exp(sums_over(after, jnp.concatenate([logs, logs], axis=0))))
+        sums = chunk_sums(jnp.concatenate([logs, logs], axis=0))
+        later = jnp.zeros((1, 2 * H), F32)
+        for k in reversed(range(CHUNKS)):
+            end = sums[k][CHUNK - 1 : CHUNK]
+            w_scr[k * CHUNK : (k + 1) * CHUNK, :] = halves(jnp.exp(end - sums[k] + later))
+            later = later + end
         total = jnp.exp(jnp.sum(logs, axis=1, keepdims=True))
         decay_scr[...] = jnp.broadcast_to(total, (H, N))
         bt_scr[...] = b_ref[...].astype(F32).T.astype(BF)
@@ -110,7 +125,7 @@
         compiler_params=pltpu.CompilerParams(vmem_limit_bytes=16 * MIB),
         cost_estimate=pl.CostEstimate(flops=2 * 10**9, bytes_accessed=3 * MIB, transcendentals=0),
         name="block_states",
-    )(order, logs, b, x)
+    )(*(in_hbm(part) for part in (order, logs, b, x)))
 
 
 def read_tail(ref, at):
@@ -142,7 +157,7 @@
     return running, product
 
 
-def total_kernel(in_ref, out_ref):
+def total_kernel(in_ref, token_ref, out_ref):
     total, product = scan_plane(in_ref, jnp.zeros((HEAD, N), F32), None)
     hi, mid, lo = three_terms(product)
     place = lax.broadcasted_iota(jnp.int32, (TAIL, N), 0)
@@ -152,14 +167,15 @@
         out_ref[k, HEAD:ROWS, :] = tail.astype(BF)
 
 
-def plane_totals(states, planes):
+def plane_totals(states, token, planes):
     return pl.pallas_call(
         total_kernel,
+        in_specs=[pl.BlockSpec(memory_space=pltpu.VMEM), pl.BlockSpec(memory_space=pl.ANY)],
         out_shape=jax.ShapeDtypeStruct((planes, ROWS, N), BF),
         compiler_params=pltpu.CompilerParams(vmem_limit_bytes=8 * MIB),
         cost_estimate=pl.CostEstimate(flops=10**6, bytes_accessed=MIB, transcendentals=0),
         name="plane_totals",
-    )(states)
+    )(states, token)
 
 
 def entering_kernel(in_ref, totals_ref, out_ref):
@@ -187,27 +203,25 @@
 
 
 def local_kernel(
-    log_ref, skip_ref, b_ref, c_ref, x_ref, gate_ref, local_ref, factor_ref,
+    log_ref, skip_ref, b_ref, c_ref, x_ref, gate_ref, local_ref, factor_ref, token_ref,
     bt_scr, left_scr, in_scr, out_scr, enter_scr, row_scr,
 ):
     step = pl.program_id(0)
 
     @pl.when(step == 0)
     def _():
+        token_ref[...] = jnp.zeros_like(token_ref)
         logs = log_ref[...]
-        shape = (TOKENS_PER_BLOCK, TOKENS_PER_BLOCK)
-        row = lax.broadcasted_iota(jnp.int32, shape, 0)
-        column = lax.broadcasted_iota(jnp.int32, shape, 1)
-        upto = (column <= row) & (column // CHUNK == row // CHUNK)
-        sums = sums_over(
-            jnp.where(upto, 1.0, 0.0).astype(BF), jnp.concatenate([logs, logs], axis=0)
-        )
+        sums = chunk_sums(jnp.concatenate([logs, logs], axis=0))
         before = jnp.zeros((1, 2 * H), F32)
         row_scr[...] = jnp.zeros_like(row_scr)
-        causal = upto[0:CHUNK, 0:CHUNK]
+        shape = (CHUNK, CHUNK)
+        causal = lax.broadcasted_iota(jnp.int32, shape, 1) <= lax.broadcasted_iota(
+            jnp.int32, shape, 0
+        )
         for k in range(CHUNKS):
             rows = slice(k * CHUNK, (k + 1) * CHUNK)
-            part = sums[rows]
+            part = sums[k]
             middle = part[CHUNK // 2 - 1 : CHUNK // 2]
             end = part[CHUNK - 1 : CHUNK]
             in_scr[rows, :] = halves(jnp.exp(middle - part))
@@ -219,9 +233,12 @@
             before = before + end
             b_part, c_part = b_ref[rows, :], c_ref[rows, :]
             bt_scr[k] = b_part.astype(F32).T.astype(BF)
-            scores = dot(c_part, b_part, (1, 1))
-            left_scr[k, :, 0:CHUNK] = jnp.where(causal, scores, 0.0).astype(BF)
-            left_scr[k, :, CHUNK : CHUNK + N] = c_part
+            scores = jnp.where(causal, dot(c_part, b_part, (1, 1)), 0.0)
+            hi = scores.astype(BF)
+            left_scr[k, :, 0:CHUNK] = hi
+            left_scr[k, :, CHUNK : 2 * CHUNK] = hi
+            left_scr[k, :, 2 * CHUNK : 3 * CHUNK] = (scores - hi.astype(F32)).astype(BF)
+            left_scr[k, :, 3 * CHUNK : 3 * CHUNK + N] = c_part
 
     heads = COLS // HEAD
     twice = spread(step * heads)
@@ -233,26 +250,26 @@
     for k in range(CHUNKS):
         rows = slice(k * CHUNK, (k + 1) * CHUNK)
         x = x_ref[rows, :].astype(F32)
-        scaled = (x * dot(in_scr[rows, :], twice)).astype(BF)
-        if running is None:
-            inner = dot(left_scr[k, :, 0:CHUNK], scaled)
-        else:
-            carried = (running * ends[4 + k : 5 + k]).astype(BF)
-            inner = dot(left_scr[k], jnp.concatenate([scaled, carried], axis=0))
+        exact = x * dot(in_scr[rows, :], twice)
+        scaled = exact.astype(BF)
+        right = [scaled, (exact - scaled.astype(F32)).astype(BF), scaled]
+        if running is not None:
+            right.append((running * ends[4 + k : 5 + k]).astype(BF))
+        inner = dot(left_scr[k, :, 0 : CHUNK * len(right)], jnp.concatenate(right, axis=0))
         if k + 1 < CHUNKS:
             made = dot(bt_scr[k], scaled) * ends[k : k + 1]
             running = made if running is None else running * ends[8 + k : 9 + k] + made
         gate = gate_ref[rows, :].astype(F32)
         opened = gate / (1.0 + jnp.exp(-gate))
         mixed = inner * dot(out_scr[rows, :], twice) + skip * x
-        local_ref[rows, :] = mixed * opened
+        local_ref[rows, :] = (mixed * opened).astype(BF)
         factor_ref[rows, :] = dot(enter_scr[rows, :], twice) * opened
 
 
 def local_part(logs, skip, b, c, x, gate):
     whole = lambda i: (0, 0)
     columns = lambda i: (0, i)
-    shape = jax.ShapeDtypeStruct((TOKENS_PER_BLOCK, DI), F32)
+    wide = (TOKENS_PER_BLOCK, DI)
     return pl.pallas_call(
         local_kernel,
         grid=(DI // COLS,),
@@ -264,25 +281,36 @@
             pl.BlockSpec((TOKENS_PER_BLOCK, COLS), columns),
             pl.BlockSpec((TOKENS_PER_BLOCK, COLS), columns),
         ],
-        out_specs=[pl.BlockSpec((TOKENS_PER_BLOCK, COLS), columns)] * 2,
-        out_shape=[shape, shape],
+        out_specs=[
+            pl.BlockSpec((TOKENS_PER_BLOCK, COLS), columns),
+            pl.BlockSpec((TOKENS_PER_BLOCK, COLS), columns),
+            pl.BlockSpec((8, N), whole),
+        ],
+        out_shape=[
+            pltpu.HBM(wide, BF),
+            pltpu.HBM(wide, F32),
+            jax.ShapeDtypeStruct((8, N), F32),
+        ],
         scratch_shapes=[
             pltpu.VMEM((CHUNKS, N, CHUNK), BF),
-            pltpu.VMEM((CHUNKS, CHUNK, CHUNK + N), BF),
+            pltpu.VMEM((CHUNKS, CHUNK, 3 * CHUNK + N), BF),
             pltpu.VMEM((TOKENS_PER_BLOCK, 2 * H), BF),
             pltpu.VMEM((TOKENS_PER_BLOCK, 2 * H), BF),
             pltpu.VMEM((TOKENS_PER_BLOCK, 2 * H), BF),
             pltpu.VMEM((16, 2 * H), F32),
         ],
-        compiler_params=pltpu.CompilerParams(vmem_limit_bytes=24 * MIB),
+        compiler_params=pltpu.CompilerParams(vmem_limit_bytes=16 * MIB),
         cost_estimate=pl.CostEstimate(
             flops=8 * 10**9, bytes_accessed=12 * MIB, transcendentals=2 * 10**6
         ),
         name="local_part",
-    )(logs, skip, b, c, x, gate)
-
-
-def output_kernel(state_ref, c_ref, local_ref, factor_ref, gain_ref, weight_ref, out_ref, normed_scr):
+    )(*(in_hbm(part) for part in (logs, skip, b, c, x, gate)))
+
+
+def output_kernel(
+    state_ref, c_ref, gain_ref, local_hbm, factor_hbm, weight_hbm, out_ref,
+    local_ref, factor_ref, weight_ref, normed_scr, row_sems, weight_sems,
+):
     width = 256
     shape = (width, width)
     same = (
@@ -290,56 +318,85 @@
         == lax.broadcasted_iota(jnp.int32, shape, 1) // HEAD
     )
     mean_of = jnp.where(same, 1.0 / HEAD, 0.0).astype(BF)
-    c = c_ref[...]
-    for k in range(DI // width):
-        columns = slice(k * width, (k + 1) * width)
-        carried = dot(c, state_ref[columns, :], (1, 1))
-        gated = local_ref[:, columns] + factor_ref[:, columns] * carried
-        square = gated * gated
-        hi = square.astype(BF)
-        mean = dot(hi, mean_of) + dot((square - hi.astype(F32)).astype(BF), mean_of)
-        normed = gated * lax.rsqrt(mean + EPS) * gain_ref[:, columns]
-        normed_scr[:, columns] = normed.astype(BF)
-    out_ref[...] = dot(normed_scr[...], weight_ref[...]).astype(BF)
+
+    def row_copies(k):
+        rows = pl.ds(pl.multiple_of(k * CHUNK, CHUNK), CHUNK)
+        return (
+            pltpu.make_async_copy(local_hbm.at[rows, :], local_ref.at[rows, :], row_sems.at[0, k]),
+            pltpu.make_async_copy(factor_hbm.at[rows, :], factor_ref.at[rows, :], row_sems.at[1, k]),
+        )
+
+    def weight_copy(j):
+        columns = pl.ds(j * width, width)
+        return pltpu.make_async_copy(
+            weight_hbm.at[:, columns], weight_ref.at[:, columns], weight_sems.at[j]
+        )
+
+    pieces = out_ref.shape[1] // width
+    for k in range(CHUNKS):
+        for copy in row_copies(k):
+            copy.start()
+
+    def norm_rows(k, carry):
+        for copy in row_copies(k):
+            copy.wait()
+
+        @pl.when(k == 0)
+        def _():
+            for j in range(pieces):
+                weight_copy(j).start()
+
+        rows = pl.ds(pl.multiple_of(k * CHUNK, CHUNK), CHUNK)
+        c = c_ref[rows, :]
+        for j in range(DI // width):
+            columns = slice(j * width, (j + 1) * width)
+            carried = dot(c, state_ref[columns, :], (1, 1))
+            gated = local_ref[rows, columns].astype(F32) + factor_ref[rows, columns] * carried
+            mean = dot((gated * gated).astype(BF), mean_of)
+            normed = gated * (lax.rsqrt(mean + EPS) * gain_ref[:, columns])
+            normed_scr[rows, columns] = normed.astype(BF)
+        return carry
+
+    lax.fori_loop(0, CHUNKS, norm_rows, 0)
+    for j in range(pieces):
+        weight_copy(j).wait()
+        columns = slice(j * width, (j + 1) * width)
+        out_ref[:, columns] = dot(normed_scr[...], weight_ref[:, columns]).astype(BF)
 
 
 def projected_tokens(state, c, local, factor, gain, weight):
-    rows = 128
     width_out = weight.shape[1]
-    whole = lambda i: (0, 0)
-    block = lambda i: (i, 0)
+    vmem, anywhere = pl.BlockSpec(memory_space=pltpu.VMEM), pl.BlockSpec(memory_space=pl.ANY)
     return pl.pallas_call(
         output_kernel,
-        grid=(TOKENS_PER_BLOCK // rows,),
-        in_specs=[
-            pl.BlockSpec((DI, N), whole),
-            pl.BlockSpec((rows, N), block),
-            pl.BlockSpec((rows, DI), block),
-            pl.BlockSpec((rows, DI), block),
-            pl.BlockSpec((1, DI), whole),
-            pl.BlockSpec((DI, width_out), whole),
-        ],
-        out_specs=pl.BlockSpec((rows, width_out), block),
+        in_specs=[vmem, vmem, vmem, anywhere, anywhere, anywhere],
+        out_specs=vmem,
         out_shape=jax.ShapeDtypeStruct((TOKENS_PER_BLOCK, width_out), BF),
-        scratch_shapes=[pltpu.VMEM((rows, DI), BF)],
-        compiler_params=pltpu.CompilerParams(vmem_limit_bytes=32 * MIB),
+        scratch_shapes=[
+            pltpu.VMEM((TOKENS_PER_BLOCK, DI), BF),
+            pltpu.VMEM((TOKENS_PER_BLOCK, DI), F32),
+            pltpu.VMEM(weight.shape, BF),
+            pltpu.VMEM((TOKENS_PER_BLOCK, DI), BF),
+            pltpu.SemaphoreType.DMA((2, CHUNKS)),
+            pltpu.SemaphoreType.DMA((width_out // 256,)),
+        ],
+        compiler_params=pltpu.CompilerParams(vmem_limit_bytes=28 * MIB),
         cost_estimate=pl.CostEstimate(
             flops=4 * 10**9, bytes_accessed=16 * MIB, transcendentals=10**6
         ),
         name="projected_tokens",
-    )(state, c, local, factor, gain, weight)
+    )(state, c, gain, in_hbm(local), in_hbm(factor), in_hbm(weight))
 
 
 def tile_kernel(order_ref, in_ref, out_ref, sems):
-    tiles = TOKENS_PER_BLOCK // TILE
-    copies = [
-        pltpu.make_async_copy(
-            in_ref.at[pl.ds(pl.multiple_of(order_ref[0, k] * TILE, TILE), TILE), :],
-            out_ref.at[pl.ds(k * TILE, TILE), :],
-            sems.at[k],
-        )
-        for k in range(tiles)
-    ]
+    piece = TILE // PIECES
+    copies = []
+    for k in range(TOKENS_PER_BLOCK // TILE):
+        first = pl.multiple_of(order_ref[0, k] * TILE, TILE)
+        for i in range(PIECES):
+            source = in_ref.at[pl.ds(first + i * piece, piece), :]
+            target = out_ref.at[pl.ds(k * TILE + i * piece, piece), :]
+            copies.append(pltpu.make_async_copy(source, target, sems.at[k * PIECES + i]))
     for copy in copies:
         copy.start()
     for copy in copies:
@@ -352,7 +409,7 @@
         in_specs=[pl.BlockSpec(memory_space=pltpu.SMEM), pl.BlockSpec(memory_space=pl.ANY)],
         out_specs=pl.BlockSpec(memory_space=pl.ANY),
         out_shape=jax.ShapeDtypeStruct(arrived.shape, arrived.dtype),
-        scratch_shapes=[pltpu.SemaphoreType.DMA((TOKENS_PER_BLOCK // TILE,))],
+        scratch_shapes=[pltpu.SemaphoreType.DMA((PIECES * TOKENS_PER_BLOCK // TILE,))],
         compiler_params=pltpu.CompilerParams(vmem_limit_bytes=MIB),
         cost_estimate=pl.CostEstimate(flops=0, bytes_accessed=3 * MIB, transcendentals=0),
         name="chosen_tiles",
@@ -380,8 +437,8 @@
     x, gate, b, c = (part[0, 0] for part in (ssd_input, gate_input, b_matrix, c_matrix))
     logs = log_decay[0, 0]
     states = swapped(block_states(view_order, logs, b, x), PLANE)
-    local, factor = local_part(logs, d_skip.reshape(1, H), b, c, x, gate)
-    totals = swapped(plane_totals(states, lax.axis_size("z")), "z")
+    local, factor, token = local_part(logs, d_skip.reshape(1, H), b, c, x, gate)
+    totals = swapped(plane_totals(states, token, lax.axis_size("z")), "z")
     entering = swapped(entering_states(states, totals), PLANE).reshape(DI, N)
     projected = projected_tokens(
         entering, c, local, factor, norm_gain.reshape(1, DI), out_weight

time: 127 us -> 118 us (0.929)
  local copies, waits for them, and re-layouts: 16.7 us -> 0.02 us
  Pallas kernels: 22.1 us -> 29 us
  blocking collectives: 81.4 us -> 77.5 us
  starting transfers between devices: 6.21 us -> 8.59 us
  waiting for transfers between devices: 0.01 us -> 2.34 us
    unnamed x34 -> x6, local copies, waits for them, and re-layouts: 16.7 us -> 0.02 us
    all_to_all x3, blocking collectives: 81.4 us -> 77.5 us  [swapped(): return lax.all_to_all(x, axes, split_axis=0, concat_axis=0, tiled=True)]
    pallas_call x2, Pallas kernels: 7.88 us -> 11.6 us  [the longest x1 11.2 us: projected_tokens(): pl.pallas_call(output_kernel, in_specs=[vmem, vmem, vmem, anywhere, anywh...]
    pallas_call x1, Pallas kernels: 7.76 us -> 10.2 us  [local_part(): pl.pallas_call(local_kernel, grid=(DI // COLS,), in_specs=[pl.BlockSpec((...]
    all_to_all x1, starting transfers between devices: 6.21 us -> 8.59 us  [swapped(): return lax.all_to_all(x, axes, split_axis=0, concat_axis=0, tiled=True)]
    all_to_all x1, waiting for transfers between devices: 0.01 us -> 2.34 us  [swapped(): return lax.all_to_all(x, axes, split_axis=0, concat_axis=0, tiled=True)]
    pallas_call x1, Pallas kernels: 3.49 us -> 4.95 us  [block_states(): pl.pallas_call(state_kernel, grid=(steps,), in_specs=[pl.BlockSpec(memory...]
  transfers between devices with their start and end apart: 1 -> 1, of which waited for: 0 -> 1; matrix products, arithmetic and copies ran while one was open for 0% -> 0% of each run, Pallas kernels for 6% -> 9%
where the time goes in v2:
time: 118 us
  blocking collectives  77.5 us (66%)
  Pallas kernels  29 us (25%)
  starting transfers between devices  8.59 us (7%)
  waiting for transfers between devices  2.34 us (2%)
    all_to_all x3, blocking collectives, swapped(): return lax.all_to_all(x, axes, split_axis=0, concat_axis=0, tiled=True)  77.5 us
    pallas_call x1, Pallas kernels, projected_tokens(): pl.pallas_call(output_kernel, in_specs=[vmem, vmem, vmem, anywhere, anywh...  11.2 us
    pallas_call x1, Pallas kernels, local_part(): pl.pallas_call(local_kernel, grid=(DI // COLS,), in_specs=[pl.BlockSpec((...  10.2 us
    all_to_all x1, starting transfers between devices, swapped(): return lax.all_to_all(x, axes, split_axis=0, concat_axis=0, tiled=True)  8.59 us
    pallas_call x1, Pallas kernels, block_states(): pl.pallas_call(state_kernel, grid=(steps,), in_specs=[pl.BlockSpec(memory...  4.95 us
  transfers between devices with their start and end apart: 1, of which 1 were waited for; matrix products, arithmetic and copies ran while one was open for 0% of the time, Pallas kernels for 9%

profile of v2, /device:TPU:1, one launch (start us, length us, event | category | flops | bytes accessed | tf_op | source)
XLA Modules:
  0.0 117.5 jit_solution(12007918418233009394)
XLA Ops:
  0.0 4.9 %block_states.1 = bf16[32,80,128]{2,1,0:T(8,128)(2,1)} custom-call(s32[1,4]{1,0:T(1,128)} %order_ref.2, f32[32,512]{1,0:T(8,128)} %bitcast.22, bf16[512,128]{1,0:T(8,128)(2,1)} %bitcast.20, bf16[512,2048]{1,0:T(8,128)(2,1)} %bitcast.17), custom_call_target="tpu_custom_call" | custom-call | flops 2000000000 | bytes 3145728 | tf_op jit(solution)/shard_map/block_states/pallas_call | solution.py:109
  5.0 8.6 %all-to-all-start = ((bf16[32,80,128]{2,1,0:T(8,128)(2,1)}), bf16[32,80,128]{2,1,0:T(8,128)(2,1)S(1)}, u32[]{:S(2)}, u32[]{:S(2)}) async-start(bf16[32,80,128]{2,1,0:T(8,128)(2,1)} %block_states.1), calls=%async_computation | async-start | bytes 1310720 | tf_op jit(solution)/shard_map/all_to_all | solution.py:420
  13.5 10.2 %local_part.1 = (bf16[512,2048]{1,0:T(8,128)(2,1)}, f32[512,2048]{1,0:T(8,128)}, f32[8,128]{1,0:T(8,128)S(1)}) custom-call(f32[32,512]{1,0:T(8,128)} %bitcast.23, f32[1,32]{1,0:T(1,128)} %bitcast.24, bf16[512,128]{1,0:T(8,128)(2,1)} %bitcast.21, bf16[512,128]{1,0:T(8,128)(2,1)} %bitcast.14, bf16[512,2048]{1,0:T(8,128)(2,1)} %bitcast.18, ...), custom_call_target="tpu_custom_call" | custom-call | flops 8000000000 | bytes 12582912 | tf_op jit(solution)/shard_map/local_part/pallas_call | solution.py:273
  23.7 0.0 copy-start
  23.7 0.0 copy-start.1
  23.7 2.3 %all-to-all-done.in_ref = bf16[32,80,128]{2,1,0:T(8,128)(2,1)S(1)} async-done(((bf16[32,80,128]{2,1,0:T(8,128)(2,1)}), bf16[32,80,128]{2,1,0:T(8,128)(2,1)S(1)}, u32[]{:S(2)}, u32[]{:S(2)}) %all-to-all-start) | async-done | bytes 655392 | tf_op jit(solution)/shard_map/all_to_all | solution.py:420
  26.1 0.4 plane_totals.1
  26.5 16.1 %all_to_all.20.totals_ref = bf16[8,80,128]{2,1,0:T(8,128)(2,1)S(1)} all-to-all(bf16[8,80,128]{2,1,0:T(8,128)(2,1)S(1)} %plane_totals.1), channel_id=1, replica_groups=mesh['z'=8,'y'=4,'core'=2,'view'=4] {'z'}, dimensions={0} | all-to-all | bytes 327680 | tf_op jit(solution)/shard_map/all_to_all | solution.py:420
  42.5 0.5 entering_states.1
  43.0 18.5 %all_to_all.21 = bf16[32,64,128]{2,1,0:T(8,128)(2,1)S(1)} all-to-all(bf16[32,64,128]{2,1,0:T(8,128)(2,1)S(1)} %entering_states.1), channel_id=1, replica_groups=mesh['z'=8,'y'=4,'core'=2,'view'=4] {'y','core','view'}, dimensions={0} | all-to-all | bytes 1048576 | tf_op jit(solution)/shard_map/all_to_all | solution.py:420
  61.5 0.0 copy-done
  61.5 0.0 copy-done.1
  61.5 11.2 %projected_tokens.1 = bf16[512,1536]{1,0:T(8,128)(2,1)S(1)} custom-call(bf16[2048,128]{1,0:T(8,128)(2,1)S(1)} %bitcast.13, bf16[512,128]{1,0:T(8,128)(2,1)S(1)} %bitcast.15, f32[1,2048]{1,0:T(1,128)S(1)} %bitcast.16, bf16[512,2048]{1,0:T(8,128)(2,1)} %get-tuple-element.9.local_hbm, f32[512,2048]{1,0:T(8,128)} %get-tuple-element.10.factor_hbm, ...), custom_call_target="tpu_custom_call" | custom-call | flops 4000000000 | bytes 16777216 | tf_op jit(solution)/shard_map/projected_tokens/pallas_call | solution.py:370
  72.7 0.0 copy-start.2
  72.7 43.0 %all_to_all.22 = bf16[64,8,1536]{2,1,0:T(8,128)(2,1)S(1)} all-to-all(bf16[64,8,1536]{2,1,0:T(8,128)(2,1)S(1)} %bitcast.11), channel_id=1, replica_groups=mesh['z'=8,'y'=4,'core'=2,'view'=4] {'z','y','core'}, dimensions={0} | all-to-all | bytes 3145728 | tf_op jit(solution)/shard_map/all_to_all | solution.py:420
  115.7 0.0 copy-done.2
  115.7 1.8 %chosen_tiles.1 = bf16[512,1536]{1,0:T(8,128)(2,1)} custom-call(s32[1,4]{1,0:T(1,128)S(1)} %copy-done.2, bf16[512,1536]{1,0:T(8,128)(2,1)S(1)} %bitcast.12), custom_call_target="tpu_custom_call" | custom-call | bytes 3145728 | tf_op jit(solution)/shard_map/chosen_tiles/pallas_call | solution.py:407
Async XLA Ops:
  5.0 21.1 %all-to-all-start = ((bf16[32,80,128]{2,1,0:T(8,128)(2,1)}), bf16[32,80,128]{2,1,0:T(8,128)(2,1)S(1)}, u32[]{:S(2)}, u32[]{:S(2)}) async-start(bf16[32,80,128]{2,1,0:T(8,128)(2,1)} %block_states.1), calls=%async_computation | async-start | bytes 1310720 | tf_op jit(solution)/shard_map/all_to_all | solution.py:420
  23.7 37.8 %copy-start = (bf16[1,1,512,128]{3,2,1,0:T(8,128)(2,1)S(1)}, bf16[1,1,512,128]{3,2,1,0:T(8,128)(2,1)}, u32[]{:S(2)}) copy-start(bf16[1,1,512,128]{3,2,1,0:T(8,128)(2,1)} %param.13) | copy-start | bytes 393220
  23.7 37.8 %copy-start.1 = (f32[2048]{0:T(1024)S(1)}, f32[2048]{0:T(1024)}, u32[]{:S(2)}) copy-start(f32[2048]{0:T(1024)} %param.16) | copy-start | bytes 24580
  72.7 43.0 %copy-start.2 = (s32[1,4]{1,0:T(1,128)S(1)}, s32[1,4]{1,0:T(1,128)}, u32[]{:S(2)}) copy-start(s32[1,4]{1,0:T(1,128)} %order_ref.3) | copy-start | bytes 52

commit v3 on v2

--- a/solution.py
+++ b/solution.py
@@ -22,6 +22,8 @@
 PLANE = ("y", "core", "view")
 TAIL = 16
 PIECES = 4
+HELD = 512
+SHARES = 2
 ROWS = HEAD + TAIL
 BF = jnp.bfloat16
 F32 = jnp.float32
@@ -175,7 +177,7 @@
         compiler_params=pltpu.CompilerParams(vmem_limit_bytes=8 * MIB),
         cost_estimate=pl.CostEstimate(flops=10**6, bytes_accessed=MIB, transcendentals=0),
         name="plane_totals",
-    )(states, token)
+    )(states, in_hbm(token))
 
 
 def entering_kernel(in_ref, totals_ref, out_ref):
@@ -203,14 +205,17 @@
 
 
 def local_kernel(
-    log_ref, skip_ref, b_ref, c_ref, x_ref, gate_ref, local_ref, factor_ref, token_ref,
-    bt_scr, left_scr, in_scr, out_scr, enter_scr, row_scr,
+    first_head, after_ref, log_ref, skip_ref, b_ref, c_ref, x_ref, gate_ref, weight_ref,
+    local_ref, factor_ref, held_ref,
+    bt_scr, left_scr, in_scr, out_scr, enter_scr, row_scr, sem,
 ):
     step = pl.program_id(0)
+    columns = pl.ds(first_head * HEAD * HELD // DI, held_ref.shape[1])
+    held = pltpu.make_async_copy(weight_ref.at[:, columns], held_ref, sem)
 
     @pl.when(step == 0)
     def _():
-        token_ref[...] = jnp.zeros_like(token_ref)
+        held.start()
         logs = log_ref[...]
         sums = chunk_sums(jnp.concatenate([logs, logs], axis=0))
         before = jnp.zeros((1, 2 * H), F32)
@@ -240,9 +245,9 @@
             left_scr[k, :, 2 * CHUNK : 3 * CHUNK] = (scores - hi.astype(F32)).astype(BF)
             left_scr[k, :, 3 * CHUNK : 3 * CHUNK + N] = c_part
 
-    heads = COLS // HEAD
-    twice = spread(step * heads)
-    once = spread(step * heads, False)
+    head = first_head + step * (COLS // HEAD)
+    twice = spread(head)
+    once = spread(head, False)
     ends = dot(halves(row_scr[...]), twice)
     skip_parts = three_terms(jnp.broadcast_to(skip_ref[...], (16, H)))
     skip = sum(dot(part.astype(BF), once) for part in skip_parts)[0:1]
@@ -263,33 +268,42 @@
         opened = gate / (1.0 + jnp.exp(-gate))
         mixed = inner * dot(out_scr[rows, :], twice) + skip * x
         local_ref[rows, :] = (mixed * opened).astype(BF)
-        factor_ref[rows, :] = dot(enter_scr[rows, :], twice) * opened
-
-
-def local_part(logs, skip, b, c, x, gate):
+        factor_ref[rows, :] = (dot(enter_scr[rows, :], twice) * opened).astype(BF)
+
+    @pl.when(step == pl.num_programs(0) - 1)
+    def _():
+        held.wait()
+
+
+def local_part(after, share, logs, skip, b, c, x, gate, weight):
+    wide = (TOKENS_PER_BLOCK, DI // SHARES)
+    steps = wide[1] // COLS
     whole = lambda i: (0, 0)
-    columns = lambda i: (0, i)
-    wide = (TOKENS_PER_BLOCK, DI)
-    return pl.pallas_call(
-        local_kernel,
-        grid=(DI // COLS,),
+    mine = lambda i: (0, i)
+    taken = lambda i: (0, i + share * steps)
+    anywhere = pl.BlockSpec(memory_space=pl.ANY)
+    return pl.pallas_call(
+        functools.partial(local_kernel, share * (H // SHARES)),
+        grid=(steps,),
         in_specs=[
+            anywhere,
             pl.BlockSpec((H, TOKENS_PER_BLOCK), whole),
             pl.BlockSpec((1, H), whole),
             pl.BlockSpec((TOKENS_PER_BLOCK, N), whole),
             pl.BlockSpec((TOKENS_PER_BLOCK, N), whole),
-            pl.BlockSpec((TOKENS_PER_BLOCK, COLS), columns),
-            pl.BlockSpec((TOKENS_PER_BLOCK, COLS), columns),
+            pl.BlockSpec((TOKENS_PER_BLOCK, COLS), taken),
+            pl.BlockSpec((TOKENS_PER_BLOCK, COLS), taken),
+            anywhere,
         ],
         out_specs=[
-            pl.BlockSpec((TOKENS_PER_BLOCK, COLS), columns),
-            pl.BlockSpec((TOKENS_PER_BLOCK, COLS), columns),
-            pl.BlockSpec((8, N), whole),
+            pl.BlockSpec((TOKENS_PER_BLOCK, COLS), mine),
+            pl.BlockSpec((TOKENS_PER_BLOCK, COLS), mine),
+            pl.BlockSpec(memory_space=pltpu.VMEM),
         ],
         out_shape=[
             pltpu.HBM(wide, BF),
-            pltpu.HBM(wide, F32),
-            jax.ShapeDtypeStruct((8, N), F32),
+            pltpu.HBM(wide, BF),
+            pltpu.VMEM((DI, HELD // SHARES), BF),
         ],
         scratch_shapes=[
             pltpu.VMEM((CHUNKS, N, CHUNK), BF),
@@ -298,55 +312,56 @@
             pltpu.VMEM((TOKENS_PER_BLOCK, 2 * H), BF),
             pltpu.VMEM((TOKENS_PER_BLOCK, 2 * H), BF),
             pltpu.VMEM((16, 2 * H), F32),
+            pltpu.SemaphoreType.DMA,
         ],
         compiler_params=pltpu.CompilerParams(vmem_limit_bytes=16 * MIB),
         cost_estimate=pl.CostEstimate(
-            flops=8 * 10**9, bytes_accessed=12 * MIB, transcendentals=2 * 10**6
+            flops=4 * 10**9, bytes_accessed=6 * MIB, transcendentals=10**6
         ),
         name="local_part",
-    )(*(in_hbm(part) for part in (logs, skip, b, c, x, gate)))
+    )(after, *(in_hbm(part) for part in (logs, skip, b, c, x, gate, weight)))
 
 
 def output_kernel(
-    state_ref, c_ref, gain_ref, local_hbm, factor_hbm, weight_hbm, out_ref,
-    local_ref, factor_ref, weight_ref, normed_scr, row_sems, weight_sems,
+    state_ref, c_ref, gain_ref, held_refs, local_hbms, factor_hbms, weight_hbm, out_ref,
+    local_ref, factor_ref, weight_ref, normed_scr, row_sems, weight_sem,
 ):
     width = 256
+    half_rows = TOKENS_PER_BLOCK // 2
     shape = (width, width)
+    copies = []
+    for k in range(2):
+        rows = pl.ds(k * half_rows, half_rows)
+        group = []
+        for part in range(SHARES):
+            columns = pl.ds(part * (DI // SHARES), DI // SHARES)
+            for i, (source, target) in enumerate(
+                ((local_hbms[part], local_ref), (factor_hbms[part], factor_ref))
+            ):
+                group.append(
+                    pltpu.make_async_copy(
+                        source.at[rows, :],
+                        target.at[rows, columns],
+                        row_sems.at[k, part * 2 + i],
+                    )
+                )
+        for copy in group:
+            copy.start()
+        copies.append(group)
+    rest = out_ref.shape[1] - HELD
+    weight_copy = pltpu.make_async_copy(
+        weight_hbm.at[:, pl.ds(HELD, rest)], weight_ref, weight_sem
+    )
+    weight_copy.start()
     same = (
         lax.broadcasted_iota(jnp.int32, shape, 0) // HEAD
         == lax.broadcasted_iota(jnp.int32, shape, 1) // HEAD
     )
     mean_of = jnp.where(same, 1.0 / HEAD, 0.0).astype(BF)
-
-    def row_copies(k):
-        rows = pl.ds(pl.multiple_of(k * CHUNK, CHUNK), CHUNK)
-        return (
-            pltpu.make_async_copy(local_hbm.at[rows, :], local_ref.at[rows, :], row_sems.at[0, k]),
-            pltpu.make_async_copy(factor_hbm.at[rows, :], factor_ref.at[rows, :], row_sems.at[1, k]),
-        )
-
-    def weight_copy(j):
-        columns = pl.ds(j * width, width)
-        return pltpu.make_async_copy(
-            weight_hbm.at[:, columns], weight_ref.at[:, columns], weight_sems.at[j]
-        )
-
-    pieces = out_ref.shape[1] // width
-    for k in range(CHUNKS):
-        for copy in row_copies(k):
-            copy.start()
-
-    def norm_rows(k, carry):
-        for copy in row_copies(k):
+    for k in range(2):
+        for copy in copies[k]:
             copy.wait()
-
-        @pl.when(k == 0)
-        def _():
-            for j in range(pieces):
-                weight_copy(j).start()
-
-        rows = pl.ds(pl.multiple_of(k * CHUNK, CHUNK), CHUNK)
+        rows = slice(k * half_rows, (k + 1) * half_rows)
         c = c_ref[rows, :]
         for j in range(DI // width):
             columns = slice(j * width, (j + 1) * width)
@@ -355,37 +370,40 @@
             mean = dot((gated * gated).astype(BF), mean_of)
             normed = gated * (lax.rsqrt(mean + EPS) * gain_ref[:, columns])
             normed_scr[rows, columns] = normed.astype(BF)
-        return carry
-
-    lax.fori_loop(0, CHUNKS, norm_rows, 0)
-    for j in range(pieces):
-        weight_copy(j).wait()
+    each = HELD // SHARES
+    for part in range(SHARES):
+        columns = slice(part * each, (part + 1) * each)
+        out_ref[:, columns] = dot(normed_scr[...], held_refs[part][...]).astype(BF)
+    weight_copy.wait()
+    for j in range(rest // width):
         columns = slice(j * width, (j + 1) * width)
-        out_ref[:, columns] = dot(normed_scr[...], weight_ref[:, columns]).astype(BF)
-
-
-def projected_tokens(state, c, local, factor, gain, weight):
+        made = dot(normed_scr[...], weight_ref[:, columns])
+        out_ref[:, HELD + j * width : HELD + (j + 1) * width] = made.astype(BF)
+
+
+def projected_tokens(state, c, gain, weight, local, factor, held):
     width_out = weight.shape[1]
     vmem, anywhere = pl.BlockSpec(memory_space=pltpu.VMEM), pl.BlockSpec(memory_space=pl.ANY)
+    held_vmem = [pltpu.with_memory_space_constraint(part, pltpu.VMEM) for part in held]
     return pl.pallas_call(
         output_kernel,
-        in_specs=[vmem, vmem, vmem, anywhere, anywhere, anywhere],
+        in_specs=[vmem, vmem, vmem, [vmem] * SHARES, [anywhere] * SHARES, [anywhere] * SHARES, anywhere],
         out_specs=vmem,
         out_shape=jax.ShapeDtypeStruct((TOKENS_PER_BLOCK, width_out), BF),
         scratch_shapes=[
             pltpu.VMEM((TOKENS_PER_BLOCK, DI), BF),
-            pltpu.VMEM((TOKENS_PER_BLOCK, DI), F32),
-            pltpu.VMEM(weight.shape, BF),
             pltpu.VMEM((TOKENS_PER_BLOCK, DI), BF),
-            pltpu.SemaphoreType.DMA((2, CHUNKS)),
-            pltpu.SemaphoreType.DMA((width_out // 256,)),
+            pltpu.VMEM((DI, width_out - HELD), BF),
+            pltpu.VMEM((TOKENS_PER_BLOCK, DI), BF),
+            pltpu.SemaphoreType.DMA((2, 2 * SHARES)),
+            pltpu.SemaphoreType.DMA,
         ],
         compiler_params=pltpu.CompilerParams(vmem_limit_bytes=28 * MIB),
         cost_estimate=pl.CostEstimate(
-            flops=4 * 10**9, bytes_accessed=16 * MIB, transcendentals=10**6
+            flops=4 * 10**9, bytes_accessed=12 * MIB, transcendentals=10**6
         ),
         name="projected_tokens",
-    )(state, c, gain, in_hbm(local), in_hbm(factor), in_hbm(weight))
+    )(state, c, gain, held_vmem, [in_hbm(p) for p in local], [in_hbm(p) for p in factor], in_hbm(weight))
 
 
 def tile_kernel(order_ref, in_ref, out_ref, sems):
@@ -436,12 +454,14 @@
     width_out = out_weight.shape[1]
     x, gate, b, c = (part[0, 0] for part in (ssd_input, gate_input, b_matrix, c_matrix))
     logs = log_decay[0, 0]
+    own = (logs, d_skip.reshape(1, H), b, c, x, gate, out_weight)
     states = swapped(block_states(view_order, logs, b, x), PLANE)
-    local, factor, token = local_part(logs, d_skip.reshape(1, H), b, c, x, gate)
-    totals = swapped(plane_totals(states, token, lax.axis_size("z")), "z")
-    entering = swapped(entering_states(states, totals), PLANE).reshape(DI, N)
+    first = local_part(in_hbm(view_order), 0, *own)
+    totals = plane_totals(states, first[0], lax.axis_size("z"))
+    second = local_part(totals, 1, *own)
+    entering = swapped(entering_states(states, swapped(totals, "z")), PLANE).reshape(DI, N)
     projected = projected_tokens(
-        entering, c, local, factor, norm_gain.reshape(1, DI), out_weight
+        entering, c, norm_gain.reshape(1, DI), out_weight, *zip(first, second)
     )
     arrived = swapped(projected.reshape(bands, TOKENS_PER_BLOCK // bands, width_out), SEQ)
     chosen = chosen_tiles(tile_order, arrived.reshape(TOKENS_PER_BLOCK, width_out))

time: 118 us -> 114 us (0.966)
  blocking collectives: 77.5 us -> 59 us
  waiting for transfers between devices: 2.34 us -> 10.9 us
  starting transfers between devices: 8.59 us -> 14.8 us
    all_to_all x3 -> x2, blocking collectives: 77.5 us -> 59 us  [swapped(): return lax.all_to_all(x, axes, split_axis=0, concat_axis=0, tiled=True)]
    all_to_all x1 -> x2, waiting for transfers between devices: 2.34 us -> 10.9 us  [swapped(): return lax.all_to_all(x, axes, split_axis=0, concat_axis=0, tiled=True)]
    all_to_all x1 -> x2, starting transfers between devices: 8.59 us -> 14.8 us  [swapped(): return lax.all_to_all(x, axes, split_axis=0, concat_axis=0, tiled=True)]
    pallas_call x2 -> x3, Pallas kernels: 21.4 us -> 19.9 us  [the longest x2 13.1 us: local_part(): pl.pallas_call(functools.partial(local_kernel, share * (H // SHARES)), gr...]
  transfers between devices with their start and end apart: 1 -> 2, of which waited for: 1 -> 2; matrix products, arithmetic and copies ran while one was open for 0% -> 0% of each run, Pallas kernels for 9% -> 12%
where the time goes in v3:
time: 114 us; the launch traced here: 113 us
  blocking collectives  59 us (52%)
  Pallas kernels  28.3 us (25%)
  starting transfers between devices  14.8 us (13%)
  waiting for transfers between devices  10.9 us (10%)
    all_to_all x2, blocking collectives, swapped(): return lax.all_to_all(x, axes, split_axis=0, concat_axis=0, tiled=True)  59 us
    all_to_all x2, starting transfers between devices, swapped(): return lax.all_to_all(x, axes, split_axis=0, concat_axis=0, tiled=True)  14.8 us
    pallas_call x2, Pallas kernels, local_part(): pl.pallas_call(functools.partial(local_kernel, share * (H // SHARES)), gr...  13.1 us
    all_to_all x2, waiting for transfers between devices, swapped(): return lax.all_to_all(x, axes, split_axis=0, concat_axis=0, tiled=True)  10.9 us
    pallas_call x1, Pallas kernels, projected_tokens(): pl.pallas_call(output_kernel, in_specs=[vmem, vmem, vmem, [vmem] * SHARES...  6.78 us
    pallas_call x1, Pallas kernels, block_states(): pl.pallas_call(state_kernel, grid=(steps,), in_specs=[pl.BlockSpec(memory...  4.95 us
  transfers between devices with their start and end apart: 2, of which 2 were waited for; matrix products, arithmetic and copies ran while one was open for 0% of the time, Pallas kernels for 12%

profile of v3, /device:TPU:1, one launch (start us, length us, event | category | flops | bytes accessed | tf_op | source)
XLA Modules:
  0.0 113.1 jit_solution(5237332373877660283)
XLA Ops:
  0.0 5.0 %block_states.1 = bf16[32,80,128]{2,1,0:T(8,128)(2,1)} custom-call(s32[1,4]{1,0:T(1,128)} %after_ref.1, f32[32,512]{1,0:T(8,128)} %bitcast.26, bf16[512,128]{1,0:T(8,128)(2,1)} %bitcast.23, bf16[512,2048]{1,0:T(8,128)(2,1)} %bitcast.18), custom_call_target="tpu_custom_call" | custom-call | flops 2000000000 | bytes 3145728 | tf_op jit(solution)/shard_map/block_states/pallas_call | solution.py:111
  5.0 8.6 %all-to-all-start = ((bf16[32,80,128]{2,1,0:T(8,128)(2,1)}), bf16[32,80,128]{2,1,0:T(8,128)(2,1)S(1)}, u32[]{:S(2)}, u32[]{:S(2)}) async-start(bf16[32,80,128]{2,1,0:T(8,128)(2,1)} %block_states.1), calls=%async_computation | async-start | bytes 1310720 | tf_op jit(solution)/shard_map/all_to_all | solution.py:438
  13.5 6.5 %local_part.2 = (bf16[512,1024]{1,0:T(8,128)(2,1)}, bf16[512,1024]{1,0:T(8,128)(2,1)}, bf16[2048,256]{1,0:T(8,128)(2,1)S(1)}) custom-call(s32[1,4]{1,0:T(1,128)} %after_ref.1, f32[32,512]{1,0:T(8,128)} %bitcast.27, f32[1,32]{1,0:T(1,128)} %bitcast.29, bf16[512,128]{1,0:T(8,128)(2,1)} %bitcast.24, bf16[512,128]{1,0:T(8,128)(2,1)} %bitcast.14, ...), custom_call_target="tpu_custom_call" | custom-call | flops 4000000000 | bytes 6291456 | tf_op jit(solution)/shard_map/local_part/pallas_call | solution.py:285
  20.0 6.1 %all-to-all-done.in_ref = bf16[32,80,128]{2,1,0:T(8,128)(2,1)S(1)} async-done(((bf16[32,80,128]{2,1,0:T(8,128)(2,1)}), bf16[32,80,128]{2,1,0:T(8,128)(2,1)S(1)}, u32[]{:S(2)}, u32[]{:S(2)}) %all-to-all-start) | async-done | bytes 655392 | tf_op jit(solution)/shard_map/all_to_all | solution.py:438
  26.1 0.4 plane_totals.1.after_ref
  26.5 16.1 %all_to_all.20.totals_ref = bf16[8,80,128]{2,1,0:T(8,128)(2,1)S(1)} all-to-all(bf16[8,80,128]{2,1,0:T(8,128)(2,1)S(1)} %plane_totals.1.after_ref), channel_id=1, replica_groups=mesh['z'=8,'y'=4,'core'=2,'view'=4] {'z'}, dimensions={0} | all-to-all | bytes 327680 | tf_op jit(solution)/shard_map/all_to_all | solution.py:438
  42.5 1.3 %entering_states.1 = bf16[32,64,128]{2,1,0:T(8,128)(2,1)} custom-call(bf16[32,80,128]{2,1,0:T(8,128)(2,1)S(1)} %all-to-all-done.in_ref, bf16[8,80,128]{2,1,0:T(8,128)(2,1)S(1)} %all_to_all.20.totals_ref), custom_call_target="tpu_custom_call" | custom-call | flops 1000000 | bytes 2097152 | tf_op jit(solution)/shard_map/entering_states/pallas_call | solution.py:198
  43.8 6.2 %all-to-all-start.2 = ((bf16[32,64,128]{2,1,0:T(8,128)(2,1)}), bf16[32,64,128]{2,1,0:T(8,128)(2,1)S(1)}, u32[]{:S(2)}, u32[]{:S(2)}) async-start(bf16[32,64,128]{2,1,0:T(8,128)(2,1)} %entering_states.1), calls=%async_computation.2 | async-start | bytes 1048576 | tf_op jit(solution)/shard_map/all_to_all | solution.py:438
  50.0 0.0 copy-start
  50.0 0.0 copy-start.1
  50.0 6.6 %local_part.3 = (bf16[512,1024]{1,0:T(8,128)(2,1)}, bf16[512,1024]{1,0:T(8,128)(2,1)}, bf16[2048,256]{1,0:T(8,128)(2,1)S(1)}) custom-call(bf16[8,80,128]{2,1,0:T(8,128)(2,1)S(1)} %plane_totals.1.after_ref, f32[32,512]{1,0:T(8,128)} %bitcast.28, f32[1,32]{1,0:T(1,128)} %bitcast.30, bf16[512,128]{1,0:T(8,128)(2,1)} %bitcast.25, bf16[512,128]{1,0:T(8,128)(2,1)} %bitcast.15, ...), custom_call_target="tpu_custom_call" | custom-call | flops 4000000000 | bytes 6291456 | tf_op jit(solution)/shard_map/local_part/pallas_call | solution.py:285
  56.7 4.8 %all-to-all-done.2 = bf16[32,64,128]{2,1,0:T(8,128)(2,1)S(1)} async-done(((bf16[32,64,128]{2,1,0:T(8,128)(2,1)}), bf16[32,64,128]{2,1,0:T(8,128)(2,1)S(1)}, u32[]{:S(2)}, u32[]{:S(2)}) %all-to-all-start.2) | async-done | bytes 524320 | tf_op jit(solution)/shard_map/all_to_all | solution.py:438
  61.5 0.0 copy-done
  61.5 0.0 copy-done.1
  61.5 6.8 %projected_tokens.1 = bf16[512,1536]{1,0:T(8,128)(2,1)S(1)} custom-call(bf16[2048,128]{1,0:T(8,128)(2,1)S(1)} %bitcast.13, bf16[512,128]{1,0:T(8,128)(2,1)S(1)} %bitcast.16, f32[1,2048]{1,0:T(1,128)S(1)} %bitcast.17, bf16[2048,256]{1,0:T(8,128)(2,1)S(1)} %get-tuple-element.12.held_refs_0_, bf16[2048,256]{1,0:T(8,128)(2,1)S(1)} %get-tuple-element.13.held_refs_1_, ...), custom_call_target="tpu_custom_call" | custom-call | flops 4000000000 | bytes 12582912 | tf_op jit(solution)/shard_map/projected_tokens/pallas_call | solution.py:388
  68.3 0.0 copy-start.2
  68.3 43.0 %all_to_all.21 = bf16[64,8,1536]{2,1,0:T(8,128)(2,1)S(1)} all-to-all(bf16[64,8,1536]{2,1,0:T(8,128)(2,1)S(1)} %bitcast.11), channel_id=1, replica_groups=mesh['z'=8,'y'=4,'core'=2,'view'=4] {'z','y','core'}, dimensions={0} | all-to-all | bytes 3145728 | tf_op jit(solution)/shard_map/all_to_all | solution.py:438
  111.2 0.0 copy-done.2
  111.2 1.8 %chosen_tiles.1 = bf16[512,1536]{1,0:T(8,128)(2,1)} custom-call(s32[1,4]{1,0:T(1,128)S(1)} %copy-done.2, bf16[512,1536]{1,0:T(8,128)(2,1)S(1)} %bitcast.12), custom_call_target="tpu_custom_call" | custom-call | bytes 3145728 | tf_op jit(solution)/shard_map/chosen_tiles/pallas_call | solution.py:425
Async XLA Ops:
  5.0 21.1 %all-to-all-start = ((bf16[32,80,128]{2,1,0:T(8,128)(2,1)}), bf16[32,80,128]{2,1,0:T(8,128)(2,1)S(1)}, u32[]{:S(2)}, u32[]{:S(2)}) async-start(bf16[32,80,128]{2,1,0:T(8,128)(2,1)} %block_states.1), calls=%async_computation | async-start | bytes 1310720 | tf_op jit(solution)/shard_map/all_to_all | solution.py:438
  43.8 17.7 %all-to-all-start.2 = ((bf16[32,64,128]{2,1,0:T(8,128)(2,1)}), bf16[32,64,128]{2,1,0:T(8,128)(2,1)S(1)}, u32[]{:S(2)}, u32[]{:S(2)}) async-start(bf16[32,64,128]{2,1,0:T(8,128)(2,1)} %entering_states.1), calls=%async_computation.2 | async-start | bytes 1048576 | tf_op jit(solution)/shard_map/all_to_all | solution.py:438
  50.0 11.5 %copy-start = (bf16[1,1,512,128]{3,2,1,0:T(8,128)(2,1)S(1)}, bf16[1,1,512,128]{3,2,1,0:T(8,128)(2,1)}, u32[]{:S(2)}) copy-start(bf16[1,1,512,128]{3,2,1,0:T(8,128)(2,1)} %param.13) | copy-start | bytes 393220
  50.0 11.5 %copy-start.1 = (f32[2048]{0:T(1024)S(1)}, f32[2048]{0:T(1024)}, u32[]{:S(2)}) copy-start(f32[2048]{0:T(1024)} %param.16) | copy-start | bytes 24580
  68.3 43.0 %copy-start.2 = (s32[1,4]{1,0:T(1,128)S(1)}, s32[1,4]{1,0:T(1,128)}, u32[]{:S(2)}) copy-start(s32[1,4]{1,0:T(1,128)} %order_ref.3) | copy-start | bytes 52

commit v4 on v3

v4 whole, which is shorter than its diff:
```python
import functools

import jax
import jax.numpy as jnp
from jax import lax
from jax.experimental import pallas as pl
from jax.experimental.pallas import tpu as pltpu
from jax.sharding import Mesh
from jax.sharding import PartitionSpec as P

H = 32
HEAD = 64
N = 128
TILE = 128
TOKENS_PER_BLOCK = 512
DI = H * HEAD
CHUNK = 128
CHUNKS = TOKENS_PER_BLOCK // CHUNK
COLS = 1024
EPS = 1e-05
SEQ = ("z", "y", "core")
PLANE = ("y", "core", "view")
TAIL = 16
PIECES = 4
HELD = 512
ROWS = HEAD + TAIL
BF = jnp.bfloat16
F32 = jnp.float32
MIB = 2**20


def dot(a, b, contract=(1, 0)):
    return lax.dot_general(
        a, b, (((contract[0],), (contract[1],)), ((), ())), preferred_element_type=F32
    )


def three_terms(x):
    hi = x.astype(BF).astype(F32)
    rest = x - hi
    mid = rest.astype(BF).astype(F32)
    return hi, mid, rest - mid


def chunk_sums(logs):
    shape = (CHUNK, CHUNK)
    row = lax.broadcasted_iota(jnp.int32, shape, 0)
    column = lax.broadcasted_iota(jnp.int32, shape, 1)
    upto = jnp.where(column <= row, 1.0, 0.0).astype(BF)
    parts = [part.astype(BF) for part in three_terms(logs)]
    return [
        sum(dot(upto, part[:, k * CHUNK : (k + 1) * CHUNK], (1, 1)) for part in parts)
        for k in range(CHUNKS)
    ]


def halves(x):
    hi = x.astype(BF).astype(F32)
    lane = lax.broadcasted_iota(jnp.int32, x.shape, x.ndim - 1)
    return jnp.where(lane < H, hi, x - hi).astype(BF)


def in_hbm(x):
    return pltpu.with_memory_space_constraint(x, pltpu.HBM)


def spread(first_head, columns, copies=2):
    shape = (copies * H, columns)
    head = lax.broadcasted_iota(jnp.int32, shape, 0) % H
    column = lax.broadcasted_iota(jnp.int32, shape, 1) // HEAD + first_head
    return jnp.where(head == column, 1.0, 0.0).astype(BF)


def column_copies(source, target, sems):
    return [
        pltpu.make_async_copy(
            source.at[:, pl.ds(k * COLS, COLS)], target.at[:, pl.ds(k * COLS, COLS)], sems.at[k]
        )
        for k in range(DI // COLS)
    ]


def state_kernel(order_ref, log_hbm, b_hbm, x_hbm, out_ref, logs_scr, b_scr, x_scr, sems, x_sems):
    log_copy = pltpu.make_async_copy(log_hbm, logs_scr, sems.at[0])
    b_copy = pltpu.make_async_copy(b_hbm, b_scr, sems.at[1])
    x_copies = column_copies(x_hbm, x_scr, x_sems)
    for copy in (log_copy, b_copy, *x_copies):
        copy.start()
    log_copy.wait()
    logs = logs_scr[...]
    sums = chunk_sums(jnp.concatenate([logs, logs], axis=0))
    later = jnp.zeros((1, 2 * H), F32)
    weights = []
    for k in reversed(range(CHUNKS)):
        end = sums[k][CHUNK - 1 : CHUNK]
        weights.insert(0, halves(jnp.exp(end - sums[k] + later)))
        later = later + end
    weights = jnp.concatenate(weights, axis=0)

    view = lax.axis_index("view")
    rank = jnp.int32(0)
    for k in range(1, 4):
        rank = rank + jnp.where(order_ref[0, k] == view, k, 0)
    decay = jnp.broadcast_to(jnp.exp(jnp.sum(logs, axis=1, keepdims=True)), (H, N))
    hi, mid, lo = (part[:, None, :] for part in three_terms(decay))
    place = lax.broadcasted_iota(jnp.int32, (H, TAIL, N), 1)
    tail = jnp.where(place == 0, hi, jnp.where(place == 1, mid, jnp.where(place == 2, lo, 0.0)))
    tail = jnp.where(place == 3, rank.astype(F32), tail)
    out_ref[:, HEAD:ROWS, :] = tail.astype(BF)

    b_copy.wait()
    b_rows = b_scr[...].astype(F32).T.astype(BF)
    heads = COLS // HEAD
    for k, copy in enumerate(x_copies):
        copy.wait()
        x = x_scr[:, k * COLS : (k + 1) * COLS].astype(F32)
        scaled = (x * dot(weights, spread(k * heads, COLS))).astype(BF)
        state = dot(b_rows, scaled).T.astype(BF)
        out_ref[k * heads : (k + 1) * heads, 0:HEAD, :] = state.reshape(heads, HEAD, N)


def block_states(order, logs, b, x):
    anywhere = pl.BlockSpec(memory_space=pl.ANY)
    return pl.pallas_call(
        state_kernel,
        in_specs=[pl.BlockSpec(memory_space=pltpu.SMEM), anywhere, anywhere, anywhere],
        out_shape=jax.ShapeDtypeStruct((H, ROWS, N), BF),
        scratch_shapes=[
            pltpu.VMEM(logs.shape, F32),
            pltpu.VMEM(b.shape, BF),
            pltpu.VMEM(x.shape, BF),
            pltpu.SemaphoreType.DMA((2,)),
            pltpu.SemaphoreType.DMA((DI // COLS,)),
        ],
        compiler_params=pltpu.CompilerParams(vmem_limit_bytes=16 * MIB),
        cost_estimate=pl.CostEstimate(flops=2 * 10**9, bytes_accessed=3 * MIB, transcendentals=0),
        name="block_states",
    )(*(in_hbm(part) for part in (order, logs, b, x)))


def read_tail(ref, at):
    tail = ref[at, HEAD:ROWS, :].astype(F32)
    return tail[0:1] + tail[1:2] + tail[2:3], tail[3:4]


def scan_plane(ref, running, emit):
    views = 4
    product = jnp.ones((1, N), F32)
    for band in range(ref.shape[0] // views):
        blocks = [band * views + v for v in range(views)]
        states = [ref[k, 0:HEAD, :].astype(F32) for k in blocks]
        decays, ranks = zip(*(read_tail(ref, k) for k in blocks))
        entering = [None] * views
        for place in range(views):
            chosen, decay = states[0], decays[0]
            for v in range(views):
                here = ranks[v] == float(place)
                entering[v] = running if place == 0 else jnp.where(here, running, entering[v])
                if v:
                    chosen = jnp.where(here, states[v], chosen)
                    decay = jnp.where(here, decays[v], decay)
            running = decay * running + chosen
            product = product * decay
        if emit is not None:
            for v in range(views):
                emit(blocks[v], entering[v])
    return running, product


def total_kernel(in_ref, token_ref, out_ref):
    total, product = scan_plane(in_ref, jnp.zeros((HEAD, N), F32), None)
    hi, mid, lo = three_terms(product)
    place = lax.broadcasted_iota(jnp.int32, (TAIL, N), 0)
    tail = jnp.where(place == 0, hi, jnp.where(place == 1, mid, jnp.where(place == 2, lo, 0.0)))
    for k in range(out_ref.shape[0]):
        out_ref[k, 0:HEAD, :] = total.astype(BF)
        out_ref[k, HEAD:ROWS, :] = tail.astype(BF)


def plane_totals(states, token, planes):
    return pl.pallas_call(
        total_kernel,
        in_specs=[pl.BlockSpec(memory_space=pltpu.VMEM), pl.BlockSpec(memory_space=pl.ANY)],
        out_shape=jax.ShapeDtypeStruct((planes, ROWS, N), BF),
        compiler_params=pltpu.CompilerParams(vmem_limit_bytes=8 * MIB),
        cost_estimate=pl.CostEstimate(flops=10**6, bytes_accessed=MIB, transcendentals=0),
        name="plane_totals",
    )(states, in_hbm(token))


def entering_kernel(in_ref, totals_ref, out_ref):
    mine = lax.axis_index("z")
    carry = jnp.zeros((HEAD, N), F32)
    for k in range(totals_ref.shape[0] - 1):
        decay, _ = read_tail(totals_ref, k)
        later = decay * carry + totals_ref[k, 0:HEAD, :].astype(F32)
        carry = jnp.where(k < mine, later, carry)

    def emit(block, value):
        out_ref[block, :, :] = value.astype(BF)

    scan_plane(in_ref, carry, emit)


def entering_states(states, totals):
    return pl.pallas_call(
        entering_kernel,
        out_shape=jax.ShapeDtypeStruct((states.shape[0], HEAD, N), BF),
        compiler_params=pltpu.CompilerParams(vmem_limit_bytes=8 * MIB),
        cost_estimate=pl.CostEstimate(flops=10**6, bytes_accessed=2 * MIB, transcendentals=0),
        name="entering_states",
    )(states, totals)


def local_kernel(
    skip_ref, log_hbm, b_hbm, c_hbm, x_hbm, gate_hbm, weight_hbm,
    local_hbm, factor_hbm, held_ref,
    log_scr, b_scr, c_scr, x_scr, gate_scr, local_scr, factor_scr, row_scr,
    sems, x_sems, gate_sems, local_sems, factor_sems,
):
    log_copy = pltpu.make_async_copy(log_hbm, log_scr, sems.at[0])
    b_copy = pltpu.make_async_copy(b_hbm, b_scr, sems.at[1])
    c_copy = pltpu.make_async_copy(c_hbm, c_scr, sems.at[2])
    held_copy = pltpu.make_async_copy(weight_hbm.at[:, pl.ds(0, HELD)], held_ref, sems.at[3])
    x_copies = column_copies(x_hbm, x_scr, x_sems)
    gate_copies = column_copies(gate_hbm, gate_scr, gate_sems)
    local_copies = column_copies(local_scr, local_hbm, local_sems)
    factor_copies = column_copies(factor_scr, factor_hbm, factor_sems)
    for copy in (log_copy, b_copy, c_copy):
        copy.start()
    for pair in zip(x_copies, gate_copies):
        for copy in pair:
            copy.start()
    held_copy.start()

    log_copy.wait()
    logs = log_scr[...]
    sums = chunk_sums(jnp.concatenate([logs, logs], axis=0))
    before = jnp.zeros((1, 2 * H), F32)
    row_scr[...] = jnp.zeros_like(row_scr)
    inward, outward, entered = [], [], []
    for k in range(CHUNKS):
        part = sums[k]
        middle = part[CHUNK // 2 - 1 : CHUNK // 2]
        end = part[CHUNK - 1 : CHUNK]
        inward.append(halves(jnp.exp(middle - part)))
        outward.append(halves(jnp.exp(part - middle)))
        entered.append(halves(jnp.exp(before + part)))
        row_scr[k : k + 1, :] = jnp.exp(end - middle)
        row_scr[4 + k : 5 + k, :] = jnp.exp(middle)
        row_scr[8 + k : 9 + k, :] = jnp.exp(end)
        before = before + end
    ends_once = halves(row_scr[...])
    skips = [part.astype(BF) for part in three_terms(jnp.broadcast_to(skip_ref[...], (16, H)))]

    b_copy.wait()
    c_copy.wait()
    shape = (CHUNK, CHUNK)
    causal = lax.broadcasted_iota(jnp.int32, shape, 1) <= lax.broadcasted_iota(
        jnp.int32, shape, 0
    )
    b_rows, left = [], []
    for k in range(CHUNKS):
        rows = slice(k * CHUNK, (k + 1) * CHUNK)
        b_part, c_part = b_scr[rows, :], c_scr[rows, :]
        b_rows.append(b_part.astype(F32).T.astype(BF))
        scores = jnp.where(causal, dot(c_part, b_part, (1, 1)), 0.0)
        hi = scores.astype(BF)
        lo = (scores - hi.astype(F32)).astype(BF)
        left.append(jnp.concatenate([hi, hi, lo, c_part], axis=1))

    for block in range(DI // COLS):
        columns = slice(block * COLS, (block + 1) * COLS)
        head = block * (COLS // HEAD)
        twice = spread(head, COLS)
        once = spread(head, COLS, 1)
        ends = dot(ends_once, twice)
        skip = sum(dot(part, once) for part in skips)[0:1]
        running = None
        x_copies[block].wait()
        gate_copies[block].wait()
        for k in range(CHUNKS):
            rows = slice(k * CHUNK, (k + 1) * CHUNK)
            x = x_scr[rows, columns].astype(F32)
            exact = x * dot(inward[k], twice)
            scaled = exact.astype(BF)
            right = [scaled, (exact - scaled.astype(F32)).astype(BF), scaled]
            if running is not None:
                right.append((running * ends[4 + k : 5 + k]).astype(BF))
            inner = dot(left[k][:, 0 : CHUNK * len(right)], jnp.concatenate(right, axis=0))
            if k + 1 < CHUNKS:
                made = dot(b_rows[k], scaled) * ends[k : k + 1]
                running = made if running is None else running * ends[8 + k : 9 + k] + made
            half = 0.5 * gate_scr[rows, columns].astype(F32)
            opened = half + half * jnp.tanh(half)
            mixed = inner * dot(outward[k], twice) + skip * x
            local_scr[rows, columns] = (mixed * opened).astype(BF)
            factor_scr[rows, columns] = (dot(entered[k], twice) * opened).astype(BF)
        local_copies[block].start()
        factor_copies[block].start()
    for copy in (held_copy, *local_copies, *factor_copies):
        copy.wait()


def local_part(logs, skip, b, c, x, gate, weight):
    blocks = DI // COLS
    anywhere = pl.BlockSpec(memory_space=pl.ANY)
    return pl.pallas_call(
        local_kernel,
        in_specs=[pl.BlockSpec(memory_space=pltpu.VMEM)] + [anywhere] * 6,
        out_specs=[anywhere, anywhere, pl.BlockSpec(memory_space=pltpu.VMEM)],
        out_shape=[pltpu.HBM(x.shape, BF), pltpu.HBM(x.shape, BF), pltpu.VMEM((DI, HELD), BF)],
        scratch_shapes=[
            pltpu.VMEM(logs.shape, F32),
            pltpu.VMEM(b.shape, BF),
            pltpu.VMEM(c.shape, BF),
            pltpu.VMEM(x.shape, BF),
            pltpu.VMEM(x.shape, BF),
            pltpu.VMEM(x.shape, BF),
            pltpu.VMEM(x.shape, BF),
            pltpu.VMEM((16, 2 * H), F32),
            pltpu.SemaphoreType.DMA((4,)),
            *[pltpu.SemaphoreType.DMA((blocks,))] * 4,
        ],
        compiler_params=pltpu.CompilerParams(vmem_limit_bytes=32 * MIB),
        cost_estimate=pl.CostEstimate(
            flops=8 * 10**9, bytes_accessed=12 * MIB, transcendentals=10**6
        ),
        name="local_part",
    )(skip, *(in_hbm(part) for part in (logs, b, c, x, gate, weight)))


def output_kernel(
    state_ref, c_ref, gain_ref, held_ref, local_hbm, factor_hbm, weight_hbm, out_ref,
    local_ref, factor_ref, weight_ref, normed_scr, row_sems, weight_sem,
):
    width = 256
    half_rows = TOKENS_PER_BLOCK // 2
    shape = (width, width)
    copies = []
    for k in range(2):
        rows = pl.ds(k * half_rows, half_rows)
        group = [
            pltpu.make_async_copy(source.at[rows, :], target.at[rows, :], row_sems.at[k, i])
            for i, (source, target) in enumerate(
                ((local_hbm, local_ref), (factor_hbm, factor_ref))
            )
        ]
        for copy in group:
            copy.start()
        copies.append(group)
    rest = out_ref.shape[1] - HELD
    weight_copy = pltpu.make_async_copy(
        weight_hbm.at[:, pl.ds(HELD, rest)], weight_ref, weight_sem
    )
    weight_copy.start()
    same = (
        lax.broadcasted_iota(jnp.int32, shape, 0) // HEAD
        == lax.broadcasted_iota(jnp.int32, shape, 1) // HEAD
    )
    mean_of = jnp.where(same, 1.0 / HEAD, 0.0).astype(BF)
    for k in range(2):
        for copy in copies[k]:
            copy.wait()
        rows = slice(k * half_rows, (k + 1) * half_rows)
        c = c_ref[rows, :]
        for j in range(DI // width):
            columns = slice(j * width, (j + 1) * width)
            carried = dot(c, state_ref[columns, :], (1, 1))
            gated = local_ref[rows, columns].astype(F32) + factor_ref[rows, columns] * carried
            mean = dot((gated * gated).astype(BF), mean_of)
            normed = gated * (lax.rsqrt(mean + EPS) * gain_ref[:, columns])
            normed_scr[rows, columns] = normed.astype(BF)
    for j in range(HELD // width):
        columns = slice(j * width, (j + 1) * width)
        out_ref[:, columns] = dot(normed_scr[...], held_ref[:, columns]).astype(BF)
    weight_copy.wait()
    for j in range(rest // width):
        columns = slice(j * width, (j + 1) * width)
        made = dot(normed_scr[...], weight_ref[:, columns])
        out_ref[:, HELD + j * width : HELD + (j + 1) * width] = made.astype(BF)


def projected_tokens(state, c, gain, weight, local, factor, held):
    width_out = weight.shape[1]
    vmem, anywhere = pl.BlockSpec(memory_space=pltpu.VMEM), pl.BlockSpec(memory_space=pl.ANY)
    held = pltpu.with_memory_space_constraint(held, pltpu.VMEM)
    return pl.pallas_call(
        output_kernel,
        in_specs=[vmem] * 4 + [anywhere] * 3,
        out_specs=vmem,
        out_shape=jax.ShapeDtypeStruct((TOKENS_PER_BLOCK, width_out), BF),
        scratch_shapes=[
            pltpu.VMEM((TOKENS_PER_BLOCK, DI), BF),
            pltpu.VMEM((TOKENS_PER_BLOCK, DI), BF),
            pltpu.VMEM((DI, width_out - HELD), BF),
            pltpu.VMEM((TOKENS_PER_BLOCK, DI), BF),
            pltpu.SemaphoreType.DMA((2, 2)),
            pltpu.SemaphoreType.DMA,
        ],
        compiler_params=pltpu.CompilerParams(vmem_limit_bytes=28 * MIB),
        cost_estimate=pl.CostEstimate(
            flops=4 * 10**9, bytes_accessed=12 * MIB, transcendentals=10**6
        ),
        name="projected_tokens",
    )(state, c, gain, held, in_hbm(local), in_hbm(factor), in_hbm(weight))


def tile_kernel(order_ref, in_ref, out_ref, sems):
    piece = TILE // PIECES
    copies = []
    for k in range(TOKENS_PER_BLOCK // TILE):
        first = pl.multiple_of(order_ref[0, k] * TILE, TILE)
        for i in range(PIECES):
            source = in_ref.at[pl.ds(first + i * piece, piece), :]
            target = out_ref.at[pl.ds(k * TILE + i * piece, piece), :]
            copies.append(pltpu.make_async_copy(source, target, sems.at[k * PIECES + i]))
    for copy in copies:
        copy.start()
    for copy in copies:
        copy.wait()


def chosen_tiles(order, arrived):
    return pl.pallas_call(
        tile_kernel,
        in_specs=[pl.BlockSpec(memory_space=pltpu.SMEM), pl.BlockSpec(memory_space=pl.ANY)],
        out_specs=pl.BlockSpec(memory_space=pl.ANY),
        out_shape=jax.ShapeDtypeStruct(arrived.shape, arrived.dtype),
        scratch_shapes=[pltpu.SemaphoreType.DMA((PIECES * TOKENS_PER_BLOCK // TILE,))],
        compiler_params=pltpu.CompilerParams(vmem_limit_bytes=MIB),
        cost_estimate=pl.CostEstimate(flops=0, bytes_accessed=3 * MIB, transcendentals=0),
        name="chosen_tiles",
    )(order, arrived)


def swapped(x, axes):
    return lax.all_to_all(x, axes, split_axis=0, concat_axis=0, tiled=True)


def shards(
    ssd_input,
    gate_input,
    b_matrix,
    c_matrix,
    log_decay,
    d_skip,
    norm_gain,
    out_weight,
    view_order,
    tile_order,
):
    bands = lax.axis_size(SEQ)
    width_out = out_weight.shape[1]
    x, gate, b, c = (part[0, 0] for part in (ssd_input, gate_input, b_matrix, c_matrix))
    logs = log_decay[0, 0]
    states = swapped(block_states(view_order, logs, b, x), PLANE)
    local, factor, held = local_part(logs, d_skip.reshape(1, H), b, c, x, gate, out_weight)
    totals = swapped(plane_totals(states, local, lax.axis_size("z")), "z")
    entering = swapped(entering_states(states, totals), PLANE).reshape(DI, N)
    projected = projected_tokens(
        entering, c, norm_gain.reshape(1, DI), out_weight, local, factor, held
    )
    arrived = swapped(projected.reshape(bands, TOKENS_PER_BLOCK // bands, width_out), SEQ)
    chosen = chosen_tiles(tile_order, arrived.reshape(TOKENS_PER_BLOCK, width_out))
    return chosen.reshape(1, 1, TOKENS_PER_BLOCK, width_out)


def solution(mesh):
    split = Mesh(mesh.devices.reshape(8, 4, 2, mesh.shape["view"]), (*SEQ, "view"))
    whole = P(SEQ, "view", None, None)
    in_specs = (whole,) * 5 + (P(),) * 3 + (P(SEQ, None),) * 2
    return jax.shard_map(shards, mesh=split, in_specs=in_specs, out_specs=whole, check_vma=False)
```

time: 114 us -> 112 us (0.982)
  blocking collectives: 59 us -> 76.4 us
  waiting for transfers between devices: 10.9 us -> 3.96 us
  starting transfers between devices: 14.8 us -> 8.6 us
  Pallas kernels: 28.3 us -> 22.3 us
    all_to_all x2 -> x3, blocking collectives: 59 us -> 76.4 us  [swapped(): return lax.all_to_all(x, axes, split_axis=0, concat_axis=0, tiled=True)]
    all_to_all x2 -> x1, waiting for transfers between devices: 10.9 us -> 3.96 us  [swapped(): return lax.all_to_all(x, axes, split_axis=0, concat_axis=0, tiled=True)]
    all_to_all x2 -> x1, starting transfers between devices: 14.8 us -> 8.6 us  [swapped(): return lax.all_to_all(x, axes, split_axis=0, concat_axis=0, tiled=True)]
    pallas_call x4 -> x3, Pallas kernels: 24.8 us -> 19.6 us  [the longest x1 8.55 us: local_part(): pl.pallas_call(local_kernel, in_specs=[pl.BlockSpec(memory_space=pltpu.VM...]
  transfers between devices with their start and end apart: 2 -> 1, of which waited for: 2 -> 1; matrix products, arithmetic and copies ran while one was open for 0% -> 0% of each run, Pallas kernels for 12% -> 8%
where the time goes in v4:
time: 112 us; the launch traced here: 111 us
  blocking collectives  76.4 us (68%)
  Pallas kernels  22.3 us (20%)
  starting transfers between devices  8.6 us (8%)
  waiting for transfers between devices  3.96 us (4%)
    all_to_all x3, blocking collectives, swapped(): return lax.all_to_all(x, axes, split_axis=0, concat_axis=0, tiled=True)  76.4 us
    all_to_all x1, starting transfers between devices, swapped(): return lax.all_to_all(x, axes, split_axis=0, concat_axis=0, tiled=True)  8.6 us
    pallas_call x1, Pallas kernels, local_part(): pl.pallas_call(local_kernel, in_specs=[pl.BlockSpec(memory_space=pltpu.VM...  8.55 us
    pallas_call x1, Pallas kernels, projected_tokens(): pl.pallas_call(output_kernel, in_specs=[vmem] * 4 + [anywhere] * 3, out_s...  6.76 us
    pallas_call x1, Pallas kernels, block_states(): pl.pallas_call(state_kernel, in_specs=[pl.BlockSpec(memory_space=pltpu.SM...  4.31 us
    all_to_all x1, waiting for transfers between devices, swapped(): return lax.all_to_all(x, axes, split_axis=0, concat_axis=0, tiled=True)  3.96 us
  transfers between devices with their start and end apart: 1, of which 1 were waited for; matrix products, arithmetic and copies ran while one was open for 0% of the time, Pallas kernels for 8%

profile of v4, /device:TPU:1, one launch (start us, length us, event | category | flops | bytes accessed | tf_op | source)
XLA Modules:
  0.0 111.5 jit_solution(9617785443306121326)
XLA Ops:
  0.0 0.0 copy-start.3
  0.0 4.3 %block_states.1 = bf16[32,80,128]{2,1,0:T(8,128)(2,1)} custom-call(s32[1,4]{1,0:T(1,128)} %order_ref.2, f32[32,512]{1,0:T(8,128)} %bitcast.23, bf16[512,128]{1,0:T(8,128)(2,1)} %bitcast.21, bf16[512,2048]{1,0:T(8,128)(2,1)} %bitcast.18), custom_call_target="tpu_custom_call" | custom-call | flops 2000000000 | bytes 3145728 | tf_op jit(solution)/shard_map/block_states/pallas_call | solution.py:124
  4.3 8.6 %all-to-all-start = ((bf16[32,80,128]{2,1,0:T(8,128)(2,1)}), bf16[32,80,128]{2,1,0:T(8,128)(2,1)S(1)}, u32[]{:S(2)}, u32[]{:S(2)}) async-start(bf16[32,80,128]{2,1,0:T(8,128)(2,1)} %block_states.1), calls=%async_computation | async-start | bytes 1310720 | tf_op jit(solution)/shard_map/all_to_all | solution.py:438
  12.9 0.0 copy-done.3
  12.9 8.5 %local_part.1 = (bf16[512,2048]{1,0:T(8,128)(2,1)}, bf16[512,2048]{1,0:T(8,128)(2,1)}, bf16[2048,512]{1,0:T(8,128)(2,1)S(1)}) custom-call(f32[1,32]{1,0:T(1,128)S(1)} %bitcast.17, f32[32,512]{1,0:T(8,128)} %bitcast.24, bf16[512,128]{1,0:T(8,128)(2,1)} %bitcast.22, bf16[512,128]{1,0:T(8,128)(2,1)} %bitcast.14, bf16[512,2048]{1,0:T(8,128)(2,1)} %bitcast.19, ...), custom_call_target="tpu_custom_call" | custom-call | flops 8000000000 | bytes 12582912 | tf_op jit(solution)/shard_map/local_part/pallas_call | solution.py:308
  21.5 4.0 %all-to-all-done.in_ref = bf16[32,80,128]{2,1,0:T(8,128)(2,1)S(1)} async-done(((bf16[32,80,128]{2,1,0:T(8,128)(2,1)}), bf16[32,80,128]{2,1,0:T(8,128)(2,1)S(1)}, u32[]{:S(2)}, u32[]{:S(2)}) %all-to-all-start) | async-done | bytes 655392 | tf_op jit(solution)/shard_map/all_to_all | solution.py:438
  25.5 0.0 copy-start
  25.5 0.0 copy-start.1
  25.5 0.4 plane_totals.1
  25.8 16.1 %all_to_all.20.totals_ref = bf16[8,80,128]{2,1,0:T(8,128)(2,1)S(1)} all-to-all(bf16[8,80,128]{2,1,0:T(8,128)(2,1)S(1)} %plane_totals.1), channel_id=1, replica_groups=mesh['z'=8,'y'=4,'core'=2,'view'=4] {'z'}, dimensions={0} | all-to-all | bytes 327680 | tf_op jit(solution)/shard_map/all_to_all | solution.py:438
  41.9 0.5 entering_states.1
  42.4 17.4 %all_to_all.21 = bf16[32,64,128]{2,1,0:T(8,128)(2,1)S(1)} all-to-all(bf16[32,64,128]{2,1,0:T(8,128)(2,1)S(1)} %entering_states.1), channel_id=1, replica_groups=mesh['z'=8,'y'=4,'core'=2,'view'=4] {'y','core','view'}, dimensions={0} | all-to-all | bytes 1048576 | tf_op jit(solution)/shard_map/all_to_all | solution.py:438
  59.8 0.0 copy-done
  59.8 0.0 copy-done.1
  59.8 6.8 %projected_tokens.1 = bf16[512,1536]{1,0:T(8,128)(2,1)S(1)} custom-call(bf16[2048,128]{1,0:T(8,128)(2,1)S(1)} %bitcast.13, bf16[512,128]{1,0:T(8,128)(2,1)S(1)} %bitcast.15, f32[1,2048]{1,0:T(1,128)S(1)} %bitcast.16, bf16[2048,512]{1,0:T(8,128)(2,1)S(1)} %get-tuple-element.9.held_ref, bf16[512,2048]{1,0:T(8,128)(2,1)} %get-tuple-element.8.token_ref.local_hbm, ...), custom_call_target="tpu_custom_call" | custom-call | flops 4000000000 | bytes 12582912 | tf_op jit(solution)/shard_map/projected_tokens/pallas_call | solution.py:388
  66.5 0.0 copy-start.2
  66.5 43.0 %all_to_all.22 = bf16[64,8,1536]{2,1,0:T(8,128)(2,1)S(1)} all-to-all(bf16[64,8,1536]{2,1,0:T(8,128)(2,1)S(1)} %bitcast.11), channel_id=1, replica_groups=mesh['z'=8,'y'=4,'core'=2,'view'=4] {'z','y','core'}, dimensions={0} | all-to-all | bytes 3145728 | tf_op jit(solution)/shard_map/all_to_all | solution.py:438
  109.5 0.0 copy-done.2
  109.5 1.8 %chosen_tiles.1 = bf16[512,1536]{1,0:T(8,128)(2,1)} custom-call(s32[1,4]{1,0:T(1,128)S(1)} %copy-done.2, bf16[512,1536]{1,0:T(8,128)(2,1)S(1)} %bitcast.12), custom_call_target="tpu_custom_call" | custom-call | bytes 3145728 | tf_op jit(solution)/shard_map/chosen_tiles/pallas_call | solution.py:425
Async XLA Ops:
  0.0 12.9 %copy-start.3 = (f32[32]{0:T(128)S(1)}, f32[32]{0:T(128)}, u32[]{:S(2)}) copy-start(f32[32]{0:T(128)} %param.15) | copy-start | bytes 388
  4.3 21.1 %all-to-all-start = ((bf16[32,80,128]{2,1,0:T(8,128)(2,1)}), bf16[32,80,128]{2,1,0:T(8,128)(2,1)S(1)}, u32[]{:S(2)}, u32[]{:S(2)}) async-start(bf16[32,80,128]{2,1,0:T(8,128)(2,1)} %block_states.1), calls=%async_computation | async-start | bytes 1310720 | tf_op jit(solution)/shard_map/all_to_all | solution.py:438
  25.5 34.3 %copy-start = (bf16[1,1,512,128]{3,2,1,0:T(8,128)(2,1)S(1)}, bf16[1,1,512,128]{3,2,1,0:T(8,128)(2,1)}, u32[]{:S(2)}) copy-start(bf16[1,1,512,128]{3,2,1,0:T(8,128)(2,1)} %param.13) | copy-start | bytes 393220
  25.5 34.3 %copy-start.1 = (f32[2048]{0:T(1024)S(1)}, f32[2048]{0:T(1024)}, u32[]{:S(2)}) copy-start(f32[2048]{0:T(1024)} %param.16) | copy-start | bytes 24580
  66.5 43.0 %copy-start.2 = (s32[1,4]{1,0:T(1,128)S(1)}, s32[1,4]{1,0:T(1,128)}, u32[]{:S(2)}) copy-start(s32[1,4]{1,0:T(1,128)} %order_ref.3) | copy-start | bytes 52

commit v5 on v4

--- a/solution.py
+++ b/solution.py
@@ -20,10 +20,10 @@
 EPS = 1e-05
 SEQ = ("z", "y", "core")
 PLANE = ("y", "core", "view")
-TAIL = 16
-PIECES = 4
+SUB = 8
+PARTS = HEAD // SUB
+MESSAGE = (PARTS + 1, SUB, N)
 HELD = 512
-ROWS = HEAD + TAIL
 BF = jnp.bfloat16
 F32 = jnp.float32
 MIB = 2**20
@@ -103,10 +103,10 @@
         rank = rank + jnp.where(order_ref[0, k] == view, k, 0)
     decay = jnp.broadcast_to(jnp.exp(jnp.sum(logs, axis=1, keepdims=True)), (H, N))
     hi, mid, lo = (part[:, None, :] for part in three_terms(decay))
-    place = lax.broadcasted_iota(jnp.int32, (H, TAIL, N), 1)
+    place = lax.broadcasted_iota(jnp.int32, (H, SUB, N), 1)
     tail = jnp.where(place == 0, hi, jnp.where(place == 1, mid, jnp.where(place == 2, lo, 0.0)))
     tail = jnp.where(place == 3, rank.astype(F32), tail)
-    out_ref[:, HEAD:ROWS, :] = tail.astype(BF)
+    out_ref[:, PARTS] = tail.astype(BF)
 
     b_copy.wait()
     b_rows = b_scr[...].astype(F32).T.astype(BF)
@@ -115,8 +115,8 @@
         copy.wait()
         x = x_scr[:, k * COLS : (k + 1) * COLS].astype(F32)
         scaled = (x * dot(weights, spread(k * heads, COLS))).astype(BF)
-        state = dot(b_rows, scaled).T.astype(BF)
-        out_ref[k * heads : (k + 1) * heads, 0:HEAD, :] = state.reshape(heads, HEAD, N)
+        state = dot(b_rows, scaled).T.reshape(heads, PARTS, SUB, N)
+        out_ref[k * heads : (k + 1) * heads, 0:PARTS] = state.astype(BF)
 
 
 def block_states(order, logs, b, x):
@@ -124,7 +124,7 @@
     return pl.pallas_call(
         state_kernel,
         in_specs=[pl.BlockSpec(memory_space=pltpu.SMEM), anywhere, anywhere, anywhere],
-        out_shape=jax.ShapeDtypeStruct((H, ROWS, N), BF),
+        out_shape=jax.ShapeDtypeStruct((H, *MESSAGE), BF),
         scratch_shapes=[
             pltpu.VMEM(logs.shape, F32),
             pltpu.VMEM(b.shape, BF),
@@ -139,8 +139,12 @@
 
 
 def read_tail(ref, at):
-    tail = ref[at, HEAD:ROWS, :].astype(F32)
+    tail = ref[at, PARTS].astype(F32)
     return tail[0:1] + tail[1:2] + tail[2:3], tail[3:4]
+
+
+def read_state(ref, at):
+    return ref[at, 0:PARTS].astype(F32).reshape(HEAD, N)
 
 
 def scan_plane(ref, running, emit):
@@ -148,7 +152,7 @@
     product = jnp.ones((1, N), F32)
     for band in range(ref.shape[0] // views):
         blocks = [band * views + v for v in range(views)]
-        states = [ref[k, 0:HEAD, :].astype(F32) for k in blocks]
+        states = [read_state(ref, k) for k in blocks]
         decays, ranks = zip(*(read_tail(ref, k) for k in blocks))
         entering = [None] * views
         for place in range(views):
@@ -170,18 +174,18 @@
 def total_kernel(in_ref, token_ref, out_ref):
     total, product = scan_plane(in_ref, jnp.zeros((HEAD, N), F32), None)
     hi, mid, lo = three_terms(product)
-    place = lax.broadcasted_iota(jnp.int32, (TAIL, N), 0)
+    place = lax.broadcasted_iota(jnp.int32, (SUB, N), 0)
     tail = jnp.where(place == 0, hi, jnp.where(place == 1, mid, jnp.where(place == 2, lo, 0.0)))
     for k in range(out_ref.shape[0]):
-        out_ref[k, 0:HEAD, :] = total.astype(BF)
-        out_ref[k, HEAD:ROWS, :] = tail.astype(BF)
+        out_ref[k, 0:PARTS] = total.reshape(PARTS, SUB, N).astype(BF)
+        out_ref[k, PARTS] = tail.astype(BF)
 
 
 def plane_totals(states, token, planes):
     return pl.pallas_call(
         total_kernel,
         in_specs=[pl.BlockSpec(memory_space=pltpu.VMEM), pl.BlockSpec(memory_space=pl.ANY)],
-        out_shape=jax.ShapeDtypeStruct((planes, ROWS, N), BF),
+        out_shape=jax.ShapeDtypeStruct((planes, *MESSAGE), BF),
         compiler_params=pltpu.CompilerParams(vmem_limit_bytes=8 * MIB),
         cost_estimate=pl.CostEstimate(flops=10**6, bytes_accessed=MIB, transcendentals=0),
         name="plane_totals",
@@ -193,7 +197,7 @@
     carry = jnp.zeros((HEAD, N), F32)
     for k in range(totals_ref.shape[0] - 1):
         decay, _ = read_tail(totals_ref, k)
-        later = decay * carry + totals_ref[k, 0:HEAD, :].astype(F32)
+        later = decay * carry + read_state(totals_ref, k)
         carry = jnp.where(k < mine, later, carry)
 
     def emit(block, value):
@@ -407,14 +411,11 @@
 
 
 def tile_kernel(order_ref, in_ref, out_ref, sems):
-    piece = TILE // PIECES
     copies = []
     for k in range(TOKENS_PER_BLOCK // TILE):
-        first = pl.multiple_of(order_ref[0, k] * TILE, TILE)
-        for i in range(PIECES):
-            source = in_ref.at[pl.ds(first + i * piece, piece), :]
-            target = out_ref.at[pl.ds(k * TILE + i * piece, piece), :]
-            copies.append(pltpu.make_async_copy(source, target, sems.at[k * PIECES + i]))
+        source = in_ref.at[pl.ds(pl.multiple_of(order_ref[0, k] * TILE, TILE), TILE), :]
+        target = out_ref.at[pl.ds(k * TILE, TILE), :]
+        copies.append(pltpu.make_async_copy(source, target, sems.at[k]))
     for copy in copies:
         copy.start()
     for copy in copies:
@@ -427,7 +428,7 @@
         in_specs=[pl.BlockSpec(memory_space=pltpu.SMEM), pl.BlockSpec(memory_space=pl.ANY)],
         out_specs=pl.BlockSpec(memory_space=pl.ANY),
         out_shape=jax.ShapeDtypeStruct(arrived.shape, arrived.dtype),
-        scratch_shapes=[pltpu.SemaphoreType.DMA((PIECES * TOKENS_PER_BLOCK // TILE,))],
+        scratch_shapes=[pltpu.SemaphoreType.DMA((TOKENS_PER_BLOCK // TILE,))],
         compiler_params=pltpu.CompilerParams(vmem_limit_bytes=MIB),
         cost_estimate=pl.CostEstimate(flops=0, bytes_accessed=3 * MIB, transcendentals=0),
         name="chosen_tiles",

time: 112 us -> 111 us (level)
  no operation moved by 1% of the time
where the time goes in v5:
time: 111 us
  blocking collectives  76.1 us (69%)
  Pallas kernels  22.1 us (20%)
  starting transfers between devices  8.6 us (8%)
  waiting for transfers between devices  3.4 us (3%)
    all_to_all x3, blocking collectives, swapped(): return lax.all_to_all(x, axes, split_axis=0, concat_axis=0, tiled=True)  76.1 us
    all_to_all x1, starting transfers between devices, swapped(): return lax.all_to_all(x, axes, split_axis=0, concat_axis=0, tiled=True)  8.6 us
    pallas_call x1, Pallas kernels, local_part(): pl.pallas_call(local_kernel, in_specs=[pl.BlockSpec(memory_space=pltpu.VM...  8.54 us
    pallas_call x1, Pallas kernels, projected_tokens(): pl.pallas_call(output_kernel, in_specs=[vmem] * 4 + [anywhere] * 3, out_s...  6.76 us
    pallas_call x1, Pallas kernels, block_states(): pl.pallas_call(state_kernel, in_specs=[pl.BlockSpec(memory_space=pltpu.SM...  4.28 us
    all_to_all x1, waiting for transfers between devices, swapped(): return lax.all_to_all(x, axes, split_axis=0, concat_axis=0, tiled=True)  3.4 us
  transfers between devices with their start and end apart: 1, of which 1 were waited for; matrix products, arithmetic and copies ran while one was open for 0% of the time, Pallas kernels for 8%

profile of v5, /device:TPU:1, one launch (start us, length us, event | category | flops | bytes accessed | tf_op | source)
XLA Modules:
  0.0 110.5 jit_solution(14129551607520785450)
XLA Ops:
  0.0 0.0 copy-start.3
  0.0 4.3 %block_states.1 = bf16[32,9,8,128]{3,2,1,0:T(8,128)(2,1)} custom-call(s32[1,4]{1,0:T(1,128)} %order_ref.2, f32[32,512]{1,0:T(8,128)} %bitcast.23, bf16[512,128]{1,0:T(8,128)(2,1)} %bitcast.21, bf16[512,2048]{1,0:T(8,128)(2,1)} %bitcast.18), custom_call_target="tpu_custom_call" | custom-call | flops 2000000000 | bytes 3145728 | tf_op jit(solution)/shard_map/block_states/pallas_call | solution.py:124
  4.3 8.6 %all-to-all-start = ((bf16[32,9,8,128]{3,2,1,0:T(8,128)(2,1)}), bf16[32,9,8,128]{3,2,1,0:T(8,128)(2,1)S(1)}, u32[]{:S(2)}, u32[]{:S(2)}) async-start(bf16[32,9,8,128]{3,2,1,0:T(8,128)(2,1)} %block_states.1), calls=%async_computation | async-start | bytes 1179648 | tf_op jit(solution)/shard_map/all_to_all | solution.py:439
  12.9 0.0 copy-done.3
  12.9 8.5 %local_part.1 = (bf16[512,2048]{1,0:T(8,128)(2,1)}, bf16[512,2048]{1,0:T(8,128)(2,1)}, bf16[2048,512]{1,0:T(8,128)(2,1)S(1)}) custom-call(f32[1,32]{1,0:T(1,128)S(1)} %bitcast.17, f32[32,512]{1,0:T(8,128)} %bitcast.24, bf16[512,128]{1,0:T(8,128)(2,1)} %bitcast.22, bf16[512,128]{1,0:T(8,128)(2,1)} %bitcast.14, bf16[512,2048]{1,0:T(8,128)(2,1)} %bitcast.19, ...), custom_call_target="tpu_custom_call" | custom-call | flops 8000000000 | bytes 12582912 | tf_op jit(solution)/shard_map/local_part/pallas_call | solution.py:312
  21.5 3.4 %all-to-all-done.in_ref = bf16[32,9,8,128]{3,2,1,0:T(8,128)(2,1)S(1)} async-done(((bf16[32,9,8,128]{3,2,1,0:T(8,128)(2,1)}), bf16[32,9,8,128]{3,2,1,0:T(8,128)(2,1)S(1)}, u32[]{:S(2)}, u32[]{:S(2)}) %all-to-all-start) | async-done | bytes 589856 | tf_op jit(solution)/shard_map/all_to_all | solution.py:439
  24.9 0.0 copy-start
  24.9 0.0 copy-start.1
  24.9 0.4 plane_totals.1
  25.2 15.9 %all_to_all.20.totals_ref = bf16[8,9,8,128]{3,2,1,0:T(8,128)(2,1)S(1)} all-to-all(bf16[8,9,8,128]{3,2,1,0:T(8,128)(2,1)S(1)} %plane_totals.1), channel_id=1, replica_groups=mesh['z'=8,'y'=4,'core'=2,'view'=4] {'z'}, dimensions={0} | all-to-all | bytes 294912 | tf_op jit(solution)/shard_map/all_to_all | solution.py:439
  41.1 0.5 entering_states.1
  41.6 17.3 %all_to_all.21 = bf16[32,64,128]{2,1,0:T(8,128)(2,1)S(1)} all-to-all(bf16[32,64,128]{2,1,0:T(8,128)(2,1)S(1)} %entering_states.1), channel_id=1, replica_groups=mesh['z'=8,'y'=4,'core'=2,'view'=4] {'y','core','view'}, dimensions={0} | all-to-all | bytes 1048576 | tf_op jit(solution)/shard_map/all_to_all | solution.py:439
  58.9 0.0 copy-done
  58.9 0.0 copy-done.1
  58.9 6.8 %projected_tokens.1 = bf16[512,1536]{1,0:T(8,128)(2,1)S(1)} custom-call(bf16[2048,128]{1,0:T(8,128)(2,1)S(1)} %bitcast.13, bf16[512,128]{1,0:T(8,128)(2,1)S(1)} %bitcast.15, f32[1,2048]{1,0:T(1,128)S(1)} %bitcast.16, bf16[2048,512]{1,0:T(8,128)(2,1)S(1)} %get-tuple-element.9.held_ref, bf16[512,2048]{1,0:T(8,128)(2,1)} %get-tuple-element.8.token_ref.local_hbm, ...), custom_call_target="tpu_custom_call" | custom-call | flops 4000000000 | bytes 12582912 | tf_op jit(solution)/shard_map/projected_tokens/pallas_call | solution.py:392
  65.7 0.0 copy-start.2
  65.7 43.0 %all_to_all.22 = bf16[64,8,1536]{2,1,0:T(8,128)(2,1)S(1)} all-to-all(bf16[64,8,1536]{2,1,0:T(8,128)(2,1)S(1)} %bitcast.11), channel_id=1, replica_groups=mesh['z'=8,'y'=4,'core'=2,'view'=4] {'z','y','core'}, dimensions={0} | all-to-all | bytes 3145728 | tf_op jit(solution)/shard_map/all_to_all | solution.py:439
  108.7 0.0 copy-done.2
  108.7 1.7 %chosen_tiles.1 = bf16[512,1536]{1,0:T(8,128)(2,1)} custom-call(s32[1,4]{1,0:T(1,128)S(1)} %copy-done.2, bf16[512,1536]{1,0:T(8,128)(2,1)S(1)} %bitcast.12), custom_call_target="tpu_custom_call" | custom-call | bytes 3145728 | tf_op jit(solution)/shard_map/chosen_tiles/pallas_call | solution.py:426
Async XLA Ops:
  0.0 12.9 %copy-start.3 = (f32[32]{0:T(128)S(1)}, f32[32]{0:T(128)}, u32[]{:S(2)}) copy-start(f32[32]{0:T(128)} %param.15) | copy-start | bytes 388
  4.3 20.6 %all-to-all-start = ((bf16[32,9,8,128]{3,2,1,0:T(8,128)(2,1)}), bf16[32,9,8,128]{3,2,1,0:T(8,128)(2,1)S(1)}, u32[]{:S(2)}, u32[]{:S(2)}) async-start(bf16[32,9,8,128]{3,2,1,0:T(8,128)(2,1)} %block_states.1), calls=%async_computation | async-start | bytes 1179648 | tf_op jit(solution)/shard_map/all_to_all | solution.py:439
  24.9 34.0 %copy-start = (bf16[1,1,512,128]{3,2,1,0:T(8,128)(2,1)S(1)}, bf16[1,1,512,128]{3,2,1,0:T(8,128)(2,1)}, u32[]{:S(2)}) copy-start(bf16[1,1,512,128]{3,2,1,0:T(8,128)(2,1)} %param.13) | copy-start | bytes 393220
  24.9 34.0 %copy-start.1 = (f32[2048]{0:T(1024)S(1)}, f32[2048]{0:T(1024)}, u32[]{:S(2)}) copy-start(f32[2048]{0:T(1024)} %param.16) | copy-start | bytes 24580
  65.7 43.0 %copy-start.2 = (s32[1,4]{1,0:T(1,128)S(1)}, s32[1,4]{1,0:T(1,128)}, u32[]{:S(2)}) copy-start(s32[1,4]{1,0:T(1,128)} %order_ref.3) | copy-start | bytes 52

commit v6 on v5

--- a/solution.py
+++ b/solution.py
@@ -80,11 +80,14 @@
     ]
 
 
-def state_kernel(order_ref, log_hbm, b_hbm, x_hbm, out_ref, logs_scr, b_scr, x_scr, sems, x_sems):
+def state_kernel(
+    order_hbm, log_hbm, b_hbm, x_hbm, out_ref, order_scr, logs_scr, b_scr, x_scr, sems, x_sems
+):
+    order_copy = pltpu.make_async_copy(order_hbm, order_scr, sems.at[2])
     log_copy = pltpu.make_async_copy(log_hbm, logs_scr, sems.at[0])
     b_copy = pltpu.make_async_copy(b_hbm, b_scr, sems.at[1])
     x_copies = column_copies(x_hbm, x_scr, x_sems)
-    for copy in (log_copy, b_copy, *x_copies):
+    for copy in (log_copy, order_copy, b_copy, *x_copies):
         copy.start()
     log_copy.wait()
     logs = logs_scr[...]
@@ -97,15 +100,16 @@
         later = later + end
     weights = jnp.concatenate(weights, axis=0)
 
-    view = lax.axis_index("view")
-    rank = jnp.int32(0)
-    for k in range(1, 4):
-        rank = rank + jnp.where(order_ref[0, k] == view, k, 0)
+    order_copy.wait()
+    order = order_scr[...]
+    turn = lax.broadcasted_iota(jnp.int32, order.shape, 1)
+    found = jnp.where(order == lax.axis_index("view"), turn, 0)
+    rank = jnp.sum(found.astype(F32), axis=1, keepdims=True)[None]
     decay = jnp.broadcast_to(jnp.exp(jnp.sum(logs, axis=1, keepdims=True)), (H, N))
     hi, mid, lo = (part[:, None, :] for part in three_terms(decay))
     place = lax.broadcasted_iota(jnp.int32, (H, SUB, N), 1)
     tail = jnp.where(place == 0, hi, jnp.where(place == 1, mid, jnp.where(place == 2, lo, 0.0)))
-    tail = jnp.where(place == 3, rank.astype(F32), tail)
+    tail = jnp.where(place == 3, rank, tail)
     out_ref[:, PARTS] = tail.astype(BF)
 
     b_copy.wait()
@@ -123,13 +127,14 @@
     anywhere = pl.BlockSpec(memory_space=pl.ANY)
     return pl.pallas_call(
         state_kernel,
-        in_specs=[pl.BlockSpec(memory_space=pltpu.SMEM), anywhere, anywhere, anywhere],
+        in_specs=[anywhere] * 4,
         out_shape=jax.ShapeDtypeStruct((H, *MESSAGE), BF),
         scratch_shapes=[
+            pltpu.VMEM(order.shape, order.dtype),
             pltpu.VMEM(logs.shape, F32),
             pltpu.VMEM(b.shape, BF),
             pltpu.VMEM(x.shape, BF),
-            pltpu.SemaphoreType.DMA((2,)),
+            pltpu.SemaphoreType.DMA((3,)),
             pltpu.SemaphoreType.DMA((DI // COLS,)),
         ],
         compiler_params=pltpu.CompilerParams(vmem_limit_bytes=16 * MIB),
@@ -411,9 +416,10 @@
 
 
 def tile_kernel(order_ref, in_ref, out_ref, sems):
+    order = order_ref[...]
     copies = []
     for k in range(TOKENS_PER_BLOCK // TILE):
-        source = in_ref.at[pl.ds(pl.multiple_of(order_ref[0, k] * TILE, TILE), TILE), :]
+        source = in_ref.at[pl.ds(pl.multiple_of(order[0, k] * TILE, TILE), TILE), :]
         target = out_ref.at[pl.ds(k * TILE, TILE), :]
         copies.append(pltpu.make_async_copy(source, target, sems.at[k]))
     for copy in copies:
@@ -425,7 +431,7 @@
 def chosen_tiles(order, arrived):
     return pl.pallas_call(
         tile_kernel,
-        in_specs=[pl.BlockSpec(memory_space=pltpu.SMEM), pl.BlockSpec(memory_space=pl.ANY)],
+        in_specs=[pl.BlockSpec(memory_space=pltpu.VMEM), pl.BlockSpec(memory_space=pl.ANY)],
         out_specs=pl.BlockSpec(memory_space=pl.ANY),
         out_shape=jax.ShapeDtypeStruct(arrived.shape, arrived.dtype),
         scratch_shapes=[pltpu.SemaphoreType.DMA((TOKENS_PER_BLOCK // TILE,))],

time: 111 us -> 110 us (level)
  Pallas kernels: 22.1 us -> 20.9 us
    pallas_call x2, Pallas kernels: 6 us -> 4.77 us  [the longest x1 3.56 us: block_states(): pl.pallas_call(state_kernel, in_specs=[anywhere] * 4, out_shape=jax.Shape...]
where the time goes in v6:
time: 110 us; the launch traced here: 109 us
  blocking collectives  76.2 us (69%)
  Pallas kernels  20.9 us (19%)
  starting transfers between devices  8.6 us (8%)
  waiting for transfers between devices  3.4 us (3%)
    all_to_all x3, blocking collectives, swapped(): return lax.all_to_all(x, axes, split_axis=0, concat_axis=0, tiled=True)  76.2 us
    all_to_all x1, starting transfers between devices, swapped(): return lax.all_to_all(x, axes, split_axis=0, concat_axis=0, tiled=True)  8.6 us
    pallas_call x1, Pallas kernels, local_part(): pl.pallas_call(local_kernel, in_specs=[pl.BlockSpec(memory_space=pltpu.VM...  8.54 us
    pallas_call x1, Pallas kernels, projected_tokens(): pl.pallas_call(output_kernel, in_specs=[vmem] * 4 + [anywhere] * 3, out_s...  6.76 us
    pallas_call x1, Pallas kernels, block_states(): pl.pallas_call(state_kernel, in_specs=[anywhere] * 4, out_shape=jax.Shape...  3.56 us
    all_to_all x1, waiting for transfers between devices, swapped(): return lax.all_to_all(x, axes, split_axis=0, concat_axis=0, tiled=True)  3.4 us
  transfers between devices with their start and end apart: 1, of which 1 were waited for; matrix products, arithmetic and copies ran while one was open for 0% of the time, Pallas kernels for 8%

profile of v6, /device:TPU:1, one launch (start us, length us, event | category | flops | bytes accessed | tf_op | source)
XLA Modules:
  0.0 109.3 jit_solution(8030190240083172046)
XLA Ops:
  0.0 0.0 copy-start.3
  0.0 3.6 %block_states.1 = bf16[32,9,8,128]{3,2,1,0:T(8,128)(2,1)} custom-call(s32[1,4]{1,0:T(1,128)} %order_hbm.1, f32[32,512]{1,0:T(8,128)} %bitcast.23, bf16[512,128]{1,0:T(8,128)(2,1)} %bitcast.21, bf16[512,2048]{1,0:T(8,128)(2,1)} %bitcast.18), custom_call_target="tpu_custom_call" | custom-call | flops 2000000000 | bytes 3145728 | tf_op jit(solution)/shard_map/block_states/pallas_call | solution.py:128
  3.6 8.6 %all-to-all-start = ((bf16[32,9,8,128]{3,2,1,0:T(8,128)(2,1)}), bf16[32,9,8,128]{3,2,1,0:T(8,128)(2,1)S(1)}, u32[]{:S(2)}, u32[]{:S(2)}) async-start(bf16[32,9,8,128]{3,2,1,0:T(8,128)(2,1)} %block_states.1), calls=%async_computation | async-start | bytes 1179648 | tf_op jit(solution)/shard_map/all_to_all | solution.py:445
  12.2 0.0 copy-done.3
  12.2 8.5 %local_part.1 = (bf16[512,2048]{1,0:T(8,128)(2,1)}, bf16[512,2048]{1,0:T(8,128)(2,1)}, bf16[2048,512]{1,0:T(8,128)(2,1)S(1)}) custom-call(f32[1,32]{1,0:T(1,128)S(1)} %bitcast.17, f32[32,512]{1,0:T(8,128)} %bitcast.24, bf16[512,128]{1,0:T(8,128)(2,1)} %bitcast.22, bf16[512,128]{1,0:T(8,128)(2,1)} %bitcast.14, bf16[512,2048]{1,0:T(8,128)(2,1)} %bitcast.19, ...), custom_call_target="tpu_custom_call" | custom-call | flops 8000000000 | bytes 12582912 | tf_op jit(solution)/shard_map/local_part/pallas_call | solution.py:317
  20.7 3.4 %all-to-all-done.in_ref = bf16[32,9,8,128]{3,2,1,0:T(8,128)(2,1)S(1)} async-done(((bf16[32,9,8,128]{3,2,1,0:T(8,128)(2,1)}), bf16[32,9,8,128]{3,2,1,0:T(8,128)(2,1)S(1)}, u32[]{:S(2)}, u32[]{:S(2)}) %all-to-all-start) | async-done | bytes 589856 | tf_op jit(solution)/shard_map/all_to_all | solution.py:445
  24.1 0.0 copy-start
  24.1 0.0 copy-start.1
  24.1 0.4 plane_totals.1
  24.5 15.9 %all_to_all.20.totals_ref = bf16[8,9,8,128]{3,2,1,0:T(8,128)(2,1)S(1)} all-to-all(bf16[8,9,8,128]{3,2,1,0:T(8,128)(2,1)S(1)} %plane_totals.1), channel_id=1, replica_groups=mesh['z'=8,'y'=4,'core'=2,'view'=4] {'z'}, dimensions={0} | all-to-all | bytes 294912 | tf_op jit(solution)/shard_map/all_to_all | solution.py:445
  40.4 0.5 entering_states.1
  40.9 17.3 %all_to_all.21 = bf16[32,64,128]{2,1,0:T(8,128)(2,1)S(1)} all-to-all(bf16[32,64,128]{2,1,0:T(8,128)(2,1)S(1)} %entering_states.1), channel_id=1, replica_groups=mesh['z'=8,'y'=4,'core'=2,'view'=4] {'y','core','view'}, dimensions={0} | all-to-all | bytes 1048576 | tf_op jit(solution)/shard_map/all_to_all | solution.py:445
  58.2 0.0 copy-done
  58.2 0.0 copy-done.1
  58.2 6.8 %projected_tokens.1 = bf16[512,1536]{1,0:T(8,128)(2,1)S(1)} custom-call(bf16[2048,128]{1,0:T(8,128)(2,1)S(1)} %bitcast.13, bf16[512,128]{1,0:T(8,128)(2,1)S(1)} %bitcast.15, f32[1,2048]{1,0:T(1,128)S(1)} %bitcast.16, bf16[2048,512]{1,0:T(8,128)(2,1)S(1)} %get-tuple-element.9.held_ref, bf16[512,2048]{1,0:T(8,128)(2,1)} %get-tuple-element.8.token_ref.local_hbm, ...), custom_call_target="tpu_custom_call" | custom-call | flops 4000000000 | bytes 12582912 | tf_op jit(solution)/shard_map/projected_tokens/pallas_call | solution.py:397
  65.0 0.0 copy-start.2
  65.0 43.0 %all_to_all.22 = bf16[64,8,1536]{2,1,0:T(8,128)(2,1)S(1)} all-to-all(bf16[64,8,1536]{2,1,0:T(8,128)(2,1)S(1)} %bitcast.11), channel_id=1, replica_groups=mesh['z'=8,'y'=4,'core'=2,'view'=4] {'z','y','core'}, dimensions={0} | all-to-all | bytes 3145728 | tf_op jit(solution)/shard_map/all_to_all | solution.py:445
  107.9 0.0 copy-done.2
  107.9 1.2 %chosen_tiles.1 = bf16[512,1536]{1,0:T(8,128)(2,1)} custom-call(s32[1,4]{1,0:T(1,128)S(1)} %copy-done.2, bf16[512,1536]{1,0:T(8,128)(2,1)S(1)} %bitcast.12), custom_call_target="tpu_custom_call" | custom-call | bytes 3145728 | tf_op jit(solution)/shard_map/chosen_tiles/pallas_call | solution.py:432
Async XLA Ops:
  0.0 12.2 %copy-start.3 = (f32[32]{0:T(128)S(1)}, f32[32]{0:T(128)}, u32[]{:S(2)}) copy-start(f32[32]{0:T(128)} %param.15) | copy-start | bytes 388
  3.6 20.6 %all-to-all-start = ((bf16[32,9,8,128]{3,2,1,0:T(8,128)(2,1)}), bf16[32,9,8,128]{3,2,1,0:T(8,128)(2,1)S(1)}, u32[]{:S(2)}, u32[]{:S(2)}) async-start(bf16[32,9,8,128]{3,2,1,0:T(8,128)(2,1)} %block_states.1), calls=%async_computation | async-start | bytes 1179648 | tf_op jit(solution)/shard_map/all_to_all | solution.py:445
  24.1 34.1 %copy-start = (bf16[1,1,512,128]{3,2,1,0:T(8,128)(2,1)S(1)}, bf16[1,1,512,128]{3,2,1,0:T(8,128)(2,1)}, u32[]{:S(2)}) copy-start(bf16[1,1,512,128]{3,2,1,0:T(8,128)(2,1)} %param.13) | copy-start | bytes 393220
  24.1 34.1 %copy-start.1 = (f32[2048]{0:T(1024)S(1)}, f32[2048]{0:T(1024)}, u32[]{:S(2)}) copy-start(f32[2048]{0:T(1024)} %param.16) | copy-start | bytes 24580
  65.0 43.0 %copy-start.2 = (s32[1,4]{1,0:T(1,128)S(1)}, s32[1,4]{1,0:T(1,128)}, u32[]{:S(2)}) copy-start(s32[1,4]{1,0:T(1,128)} %order_ref.1) | copy-start | bytes 52

commit v7 on v6

--- a/solution.py
+++ b/solution.py
@@ -81,7 +81,8 @@
 
 
 def state_kernel(
-    order_hbm, log_hbm, b_hbm, x_hbm, out_ref, order_scr, logs_scr, b_scr, x_scr, sems, x_sems
+    order_hbm, log_hbm, b_hbm, x_hbm, out_ref, sums_ref,
+    order_scr, logs_scr, b_scr, x_scr, sems, x_sems,
 ):
     order_copy = pltpu.make_async_copy(order_hbm, order_scr, sems.at[2])
     log_copy = pltpu.make_async_copy(log_hbm, logs_scr, sems.at[0])
@@ -95,6 +96,7 @@
     later = jnp.zeros((1, 2 * H), F32)
     weights = []
     for k in reversed(range(CHUNKS)):
+        sums_ref[k * CHUNK : (k + 1) * CHUNK, :] = sums[k]
         end = sums[k][CHUNK - 1 : CHUNK]
         weights.insert(0, halves(jnp.exp(end - sums[k] + later)))
         later = later + end
@@ -128,7 +130,11 @@
     return pl.pallas_call(
         state_kernel,
         in_specs=[anywhere] * 4,
-        out_shape=jax.ShapeDtypeStruct((H, *MESSAGE), BF),
+        out_specs=[pl.BlockSpec(), pl.BlockSpec(memory_space=pltpu.VMEM)],
+        out_shape=[
+            jax.ShapeDtypeStruct((H, *MESSAGE), BF),
+            pltpu.VMEM((TOKENS_PER_BLOCK, 2 * H), F32),
+        ],
         scratch_shapes=[
             pltpu.VMEM(order.shape, order.dtype),
             pltpu.VMEM(logs.shape, F32),
@@ -222,12 +228,11 @@
 
 
 def local_kernel(
-    skip_ref, log_hbm, b_hbm, c_hbm, x_hbm, gate_hbm, weight_hbm,
+    skip_ref, sums_ref, b_hbm, c_hbm, x_hbm, gate_hbm, weight_hbm,
     local_hbm, factor_hbm, held_ref,
-    log_scr, b_scr, c_scr, x_scr, gate_scr, local_scr, factor_scr, row_scr,
+    b_scr, c_scr, x_scr, gate_scr, local_scr, factor_scr, row_scr,
     sems, x_sems, gate_sems, local_sems, factor_sems,
 ):
-    log_copy = pltpu.make_async_copy(log_hbm, log_scr, sems.at[0])
     b_copy = pltpu.make_async_copy(b_hbm, b_scr, sems.at[1])
     c_copy = pltpu.make_async_copy(c_hbm, c_scr, sems.at[2])
     held_copy = pltpu.make_async_copy(weight_hbm.at[:, pl.ds(0, HELD)], held_ref, sems.at[3])
@@ -235,21 +240,18 @@
     gate_copies = column_copies(gate_hbm, gate_scr, gate_sems)
     local_copies = column_copies(local_scr, local_hbm, local_sems)
     factor_copies = column_copies(factor_scr, factor_hbm, factor_sems)
-    for copy in (log_copy, b_copy, c_copy):
+    for copy in (b_copy, c_copy):
         copy.start()
     for pair in zip(x_copies, gate_copies):
         for copy in pair:
             copy.start()
     held_copy.start()
 
-    log_copy.wait()
-    logs = log_scr[...]
-    sums = chunk_sums(jnp.concatenate([logs, logs], axis=0))
     before = jnp.zeros((1, 2 * H), F32)
     row_scr[...] = jnp.zeros_like(row_scr)
     inward, outward, entered = [], [], []
     for k in range(CHUNKS):
-        part = sums[k]
+        part = sums_ref[k * CHUNK : (k + 1) * CHUNK, :]
         middle = part[CHUNK // 2 - 1 : CHUNK // 2]
         end = part[CHUNK - 1 : CHUNK]
         inward.append(halves(jnp.exp(middle - part)))
@@ -274,9 +276,7 @@
         b_part, c_part = b_scr[rows, :], c_scr[rows, :]
         b_rows.append(b_part.astype(F32).T.astype(BF))
         scores = jnp.where(causal, dot(c_part, b_part, (1, 1)), 0.0)
-        hi = scores.astype(BF)
-        lo = (scores - hi.astype(F32)).astype(BF)
-        left.append(jnp.concatenate([hi, hi, lo, c_part], axis=1))
+        left.append(jnp.concatenate([scores.astype(BF), c_part], axis=1))
 
     for block in range(DI // COLS):
         columns = slice(block * COLS, (block + 1) * COLS)
@@ -291,9 +291,8 @@
         for k in range(CHUNKS):
             rows = slice(k * CHUNK, (k + 1) * CHUNK)
             x = x_scr[rows, columns].astype(F32)
-            exact = x * dot(inward[k], twice)
-            scaled = exact.astype(BF)
-            right = [scaled, (exact - scaled.astype(F32)).astype(BF), scaled]
+            scaled = (x * dot(inward[k], twice)).astype(BF)
+            right = [scaled]
             if running is not None:
                 right.append((running * ends[4 + k : 5 + k]).astype(BF))
             inner = dot(left[k][:, 0 : CHUNK * len(right)], jnp.concatenate(right, axis=0))
@@ -311,16 +310,15 @@
         copy.wait()
 
 
-def local_part(logs, skip, b, c, x, gate, weight):
+def local_part(skip, sums, b, c, x, gate, weight):
     blocks = DI // COLS
     anywhere = pl.BlockSpec(memory_space=pl.ANY)
     return pl.pallas_call(
         local_kernel,
-        in_specs=[pl.BlockSpec(memory_space=pltpu.VMEM)] + [anywhere] * 6,
+        in_specs=[pl.BlockSpec(memory_space=pltpu.VMEM)] * 2 + [anywhere] * 5,
         out_specs=[anywhere, anywhere, pl.BlockSpec(memory_space=pltpu.VMEM)],
         out_shape=[pltpu.HBM(x.shape, BF), pltpu.HBM(x.shape, BF), pltpu.VMEM((DI, HELD), BF)],
         scratch_shapes=[
-            pltpu.VMEM(logs.shape, F32),
             pltpu.VMEM(b.shape, BF),
             pltpu.VMEM(c.shape, BF),
             pltpu.VMEM(x.shape, BF),
@@ -336,7 +334,11 @@
             flops=8 * 10**9, bytes_accessed=12 * MIB, transcendentals=10**6
         ),
         name="local_part",
-    )(skip, *(in_hbm(part) for part in (logs, b, c, x, gate, weight)))
+    )(
+        skip,
+        pltpu.with_memory_space_constraint(sums, pltpu.VMEM),
+        *(in_hbm(part) for part in (b, c, x, gate, weight)),
+    )
 
 
 def output_kernel(
@@ -461,8 +463,9 @@
     width_out = out_weight.shape[1]
     x, gate, b, c = (part[0, 0] for part in (ssd_input, gate_input, b_matrix, c_matrix))
     logs = log_decay[0, 0]
-    states = swapped(block_states(view_order, logs, b, x), PLANE)
-    local, factor, held = local_part(logs, d_skip.reshape(1, H), b, c, x, gate, out_weight)
+    states, sums = block_states(view_order, logs, b, x)
+    states = swapped(states, PLANE)
+    local, factor, held = local_part(d_skip.reshape(1, H), sums, b, c, x, gate, out_weight)
     totals = swapped(plane_totals(states, local, lax.axis_size("z")), "z")
     entering = swapped(entering_states(states, totals), PLANE).reshape(DI, N)
     projected = projected_tokens(

time: 110 us -> 109 us (level)
  transfers between devices with their start and end apart: 1 -> 1, of which waited for: 1 -> 1; matrix products, arithmetic and copies ran while one was open for 0% -> 0% of each run, Pallas kernels for 8% -> 7%
where the time goes in v7:
time: 109 us
  blocking collectives  76.1 us (70%)
  Pallas kernels  20.1 us (18%)
  starting transfers between devices  8.6 us (8%)
  waiting for transfers between devices  4.22 us (4%)
    all_to_all x3, blocking collectives, swapped(): return lax.all_to_all(x, axes, split_axis=0, concat_axis=0, tiled=True)  76.1 us
    all_to_all x1, starting transfers between devices, swapped(): return lax.all_to_all(x, axes, split_axis=0, concat_axis=0, tiled=True)  8.6 us
    pallas_call x1, Pallas kernels, local_part(): pl.pallas_call(local_kernel, in_specs=[pl.BlockSpec(memory_space=pltpu.VM...  7.72 us
    pallas_call x1, Pallas kernels, projected_tokens(): pl.pallas_call(output_kernel, in_specs=[vmem] * 4 + [anywhere] * 3, out_s...  6.76 us
    all_to_all x1, waiting for transfers between devices, swapped(): return lax.all_to_all(x, axes, split_axis=0, concat_axis=0, tiled=True)  4.22 us
    pallas_call x1, Pallas kernels, block_states(): pl.pallas_call(state_kernel, in_specs=[anywhere] * 4, out_specs=[pl.Block...  3.56 us
  transfers between devices with their start and end apart: 1, of which 1 were waited for; matrix products, arithmetic and copies ran while one was open for 0% of the time, Pallas kernels for 7%

profile of v7, /device:TPU:1, one launch (start us, length us, event | category | flops | bytes accessed | tf_op | source)
XLA Modules:
  0.0 109.1 jit_solution(16723992023822785823)
XLA Ops:
  0.0 0.0 copy-start.3
  0.0 3.6 %block_states.1 = (bf16[32,9,8,128]{3,2,1,0:T(8,128)(2,1)}, f32[512,64]{1,0:T(8,128)S(1)}) custom-call(s32[1,4]{1,0:T(1,128)} %order_hbm.1, f32[32,512]{1,0:T(8,128)} %bitcast.23, bf16[512,128]{1,0:T(8,128)(2,1)} %bitcast.21, bf16[512,2048]{1,0:T(8,128)(2,1)} %bitcast.18), custom_call_target="tpu_custom_call" | custom-call | flops 2000000000 | bytes 3145728 | tf_op jit(solution)/shard_map/block_states/pallas_call | solution.py:130
  3.6 8.6 %all-to-all-start = ((bf16[32,9,8,128]{3,2,1,0:T(8,128)(2,1)}), bf16[32,9,8,128]{3,2,1,0:T(8,128)(2,1)S(1)}, u32[]{:S(2)}, u32[]{:S(2)}) async-start(bf16[32,9,8,128]{3,2,1,0:T(8,128)(2,1)} %get-tuple-element.10), calls=%async_computation | async-start | bytes 1179648 | tf_op jit(solution)/shard_map/all_to_all | solution.py:447
  12.2 0.0 copy-done.3
  12.2 7.7 %local_part.1 = (bf16[512,2048]{1,0:T(8,128)(2,1)}, bf16[512,2048]{1,0:T(8,128)(2,1)}, bf16[2048,512]{1,0:T(8,128)(2,1)S(1)}) custom-call(f32[1,32]{1,0:T(1,128)S(1)} %bitcast.17, f32[512,64]{1,0:T(8,128)S(1)} %get-tuple-element.11.sums_ref, bf16[512,128]{1,0:T(8,128)(2,1)} %bitcast.22, bf16[512,128]{1,0:T(8,128)(2,1)} %bitcast.14, ...), custom_call_target="tpu_custom_call" | custom-call | flops 8000000000 | bytes 12582912 | tf_op jit(solution)/shard_map/local_part/pallas_call | solution.py:316
  19.9 4.2 %all-to-all-done.in_ref = bf16[32,9,8,128]{3,2,1,0:T(8,128)(2,1)S(1)} async-done(((bf16[32,9,8,128]{3,2,1,0:T(8,128)(2,1)}), bf16[32,9,8,128]{3,2,1,0:T(8,128)(2,1)S(1)}, u32[]{:S(2)}, u32[]{:S(2)}) %all-to-all-start) | async-done | bytes 589856 | tf_op jit(solution)/shard_map/all_to_all | solution.py:447
  24.1 0.0 copy-start
  24.1 0.0 copy-start.1
  24.1 0.4 plane_totals.1
  24.5 15.9 %all_to_all.20.totals_ref = bf16[8,9,8,128]{3,2,1,0:T(8,128)(2,1)S(1)} all-to-all(bf16[8,9,8,128]{3,2,1,0:T(8,128)(2,1)S(1)} %plane_totals.1), channel_id=1, replica_groups=mesh['z'=8,'y'=4,'core'=2,'view'=4] {'z'}, dimensions={0} | all-to-all | bytes 294912 | tf_op jit(solution)/shard_map/all_to_all | solution.py:447
  40.4 0.5 entering_states.1
  40.9 17.3 %all_to_all.21 = bf16[32,64,128]{2,1,0:T(8,128)(2,1)S(1)} all-to-all(bf16[32,64,128]{2,1,0:T(8,128)(2,1)S(1)} %entering_states.1), channel_id=1, replica_groups=mesh['z'=8,'y'=4,'core'=2,'view'=4] {'y','core','view'}, dimensions={0} | all-to-all | bytes 1048576 | tf_op jit(solution)/shard_map/all_to_all | solution.py:447
  58.2 0.0 copy-done
  58.2 0.0 copy-done.1
  58.2 6.8 %projected_tokens.1 = bf16[512,1536]{1,0:T(8,128)(2,1)S(1)} custom-call(bf16[2048,128]{1,0:T(8,128)(2,1)S(1)} %bitcast.13, bf16[512,128]{1,0:T(8,128)(2,1)S(1)} %bitcast.15, f32[1,2048]{1,0:T(1,128)S(1)} %bitcast.16, bf16[2048,512]{1,0:T(8,128)(2,1)S(1)} %get-tuple-element.13.held_ref, bf16[512,2048]{1,0:T(8,128)(2,1)} %get-tuple-element.12.token_ref.local_hbm, ...), custom_call_target="tpu_custom_call" | custom-call | flops 4000000000 | bytes 12582912 | tf_op jit(solution)/shard_map/projected_tokens/pallas_call | solution.py:399
  64.9 0.0 copy-start.2
  64.9 43.0 %all_to_all.22 = bf16[64,8,1536]{2,1,0:T(8,128)(2,1)S(1)} all-to-all(bf16[64,8,1536]{2,1,0:T(8,128)(2,1)S(1)} %bitcast.11), channel_id=1, replica_groups=mesh['z'=8,'y'=4,'core'=2,'view'=4] {'z','y','core'}, dimensions={0} | all-to-all | bytes 3145728 | tf_op jit(solution)/shard_map/all_to_all | solution.py:447
  107.9 0.0 copy-done.2
  107.9 1.2 %chosen_tiles.1 = bf16[512,1536]{1,0:T(8,128)(2,1)} custom-call(s32[1,4]{1,0:T(1,128)S(1)} %copy-done.2, bf16[512,1536]{1,0:T(8,128)(2,1)S(1)} %bitcast.12), custom_call_target="tpu_custom_call" | custom-call | bytes 3145728 | tf_op jit(solution)/shard_map/chosen_tiles/pallas_call | solution.py:434
Async XLA Ops:
  0.0 12.2 %copy-start.3 = (f32[32]{0:T(128)S(1)}, f32[32]{0:T(128)}, u32[]{:S(2)}) copy-start(f32[32]{0:T(128)} %param.15) | copy-start | bytes 388
  3.6 20.6 %all-to-all-start = ((bf16[32,9,8,128]{3,2,1,0:T(8,128)(2,1)}), bf16[32,9,8,128]{3,2,1,0:T(8,128)(2,1)S(1)}, u32[]{:S(2)}, u32[]{:S(2)}) async-start(bf16[32,9,8,128]{3,2,1,0:T(8,128)(2,1)} %get-tuple-element.10), calls=%async_computation | async-start | bytes 1179648 | tf_op jit(solution)/shard_map/all_to_all | solution.py:447
  24.1 34.0 %copy-start = (bf16[1,1,512,128]{3,2,1,0:T(8,128)(2,1)S(1)}, bf16[1,1,512,128]{3,2,1,0:T(8,128)(2,1)}, u32[]{:S(2)}) copy-start(bf16[1,1,512,128]{3,2,1,0:T(8,128)(2,1)} %param.13) | copy-start | bytes 393220
  24.1 34.0 %copy-start.1 = (f32[2048]{0:T(1024)S(1)}, f32[2048]{0:T(1024)}, u32[]{:S(2)}) copy-start(f32[2048]{0:T(1024)} %param.16) | copy-start | bytes 24580
  64.9 43.0 %copy-start.2 = (s32[1,4]{1,0:T(1,128)S(1)}, s32[1,4]{1,0:T(1,128)}, u32[]{:S(2)}) copy-start(s32[1,4]{1,0:T(1,128)} %order_ref.1) | copy-start | bytes 52

commit v8 on v7

--- a/solution.py
+++ b/solution.py
@@ -13,6 +13,7 @@
 N = 128
 TILE = 128
 TOKENS_PER_BLOCK = 512
+RETURN_PARTS = 4
 DI = H * HEAD
 CHUNK = 128
 CHUNKS = TOKENS_PER_BLOCK // CHUNK
@@ -182,7 +183,7 @@
     return running, product
 
 
-def total_kernel(in_ref, token_ref, out_ref):
+def total_kernel(in_ref, out_ref):
     total, product = scan_plane(in_ref, jnp.zeros((HEAD, N), F32), None)
     hi, mid, lo = three_terms(product)
     place = lax.broadcasted_iota(jnp.int32, (SUB, N), 0)
@@ -192,18 +193,17 @@
         out_ref[k, PARTS] = tail.astype(BF)
 
 
-def plane_totals(states, token, planes):
+def plane_totals(states, planes):
     return pl.pallas_call(
         total_kernel,
-        in_specs=[pl.BlockSpec(memory_space=pltpu.VMEM), pl.BlockSpec(memory_space=pl.ANY)],
         out_shape=jax.ShapeDtypeStruct((planes, *MESSAGE), BF),
         compiler_params=pltpu.CompilerParams(vmem_limit_bytes=8 * MIB),
         cost_estimate=pl.CostEstimate(flops=10**6, bytes_accessed=MIB, transcendentals=0),
         name="plane_totals",
-    )(states, in_hbm(token))
-
-
-def entering_kernel(in_ref, totals_ref, out_ref):
+    )(states)
+
+
+def entering_kernel(in_ref, totals_ref, out_hbm, out_ref, sems):
     mine = lax.axis_index("z")
     carry = jnp.zeros((HEAD, N), F32)
     for k in range(totals_ref.shape[0] - 1):
@@ -211,16 +211,31 @@
         later = decay * carry + read_state(totals_ref, k)
         carry = jnp.where(k < mine, later, carry)
 
+    group = in_ref.shape[0] // RETURN_PARTS
+    copies = []
+    for k in range(RETURN_PARTS):
+        blocks = pl.ds(k * group, group)
+        copies.append(pltpu.make_async_copy(out_ref.at[blocks], out_hbm.at[blocks], sems.at[k]))
+
     def emit(block, value):
         out_ref[block, :, :] = value.astype(BF)
+        if block % group == group - 1:
+            copies[block // group].start()
 
     scan_plane(in_ref, carry, emit)
+    for copy in copies:
+        copy.wait()
 
 
 def entering_states(states, totals):
     return pl.pallas_call(
         entering_kernel,
-        out_shape=jax.ShapeDtypeStruct((states.shape[0], HEAD, N), BF),
+        out_specs=pl.BlockSpec(memory_space=pl.ANY),
+        out_shape=pltpu.HBM((states.shape[0], HEAD, N), BF),
+        scratch_shapes=[
+            pltpu.VMEM((states.shape[0], HEAD, N), BF),
+            pltpu.SemaphoreType.DMA((RETURN_PARTS,)),
+        ],
         compiler_params=pltpu.CompilerParams(vmem_limit_bytes=8 * MIB),
         cost_estimate=pl.CostEstimate(flops=10**6, bytes_accessed=2 * MIB, transcendentals=0),
         name="entering_states",
@@ -228,7 +243,7 @@
 
 
 def local_kernel(
-    skip_ref, sums_ref, b_hbm, c_hbm, x_hbm, gate_hbm, weight_hbm,
+    after_ref, skip_ref, sums_ref, b_hbm, c_hbm, x_hbm, gate_hbm, weight_hbm,
     local_hbm, factor_hbm, held_ref,
     b_scr, c_scr, x_scr, gate_scr, local_scr, factor_scr, row_scr,
     sems, x_sems, gate_sems, local_sems, factor_sems,
@@ -310,12 +325,12 @@
         copy.wait()
 
 
-def local_part(skip, sums, b, c, x, gate, weight):
+def local_part(after, skip, sums, b, c, x, gate, weight):
     blocks = DI // COLS
     anywhere = pl.BlockSpec(memory_space=pl.ANY)
     return pl.pallas_call(
         local_kernel,
-        in_specs=[pl.BlockSpec(memory_space=pltpu.VMEM)] * 2 + [anywhere] * 5,
+        in_specs=[anywhere] + [pl.BlockSpec(memory_space=pltpu.VMEM)] * 2 + [anywhere] * 5,
         out_specs=[anywhere, anywhere, pl.BlockSpec(memory_space=pltpu.VMEM)],
         out_shape=[pltpu.HBM(x.shape, BF), pltpu.HBM(x.shape, BF), pltpu.VMEM((DI, HELD), BF)],
         scratch_shapes=[
@@ -335,6 +350,7 @@
         ),
         name="local_part",
     )(
+        after,
         skip,
         pltpu.with_memory_space_constraint(sums, pltpu.VMEM),
         *(in_hbm(part) for part in (b, c, x, gate, weight)),
@@ -465,9 +481,11 @@
     logs = log_decay[0, 0]
     states, sums = block_states(view_order, logs, b, x)
     states = swapped(states, PLANE)
-    local, factor, held = local_part(d_skip.reshape(1, H), sums, b, c, x, gate, out_weight)
-    totals = swapped(plane_totals(states, local, lax.axis_size("z")), "z")
+    totals = swapped(plane_totals(states, lax.axis_size("z")), "z")
     entering = swapped(entering_states(states, totals), PLANE).reshape(DI, N)
+    local, factor, held = local_part(
+        totals, d_skip.reshape(1, H), sums, b, c, x, gate, out_weight
+    )
     projected = projected_tokens(
         entering, c, norm_gain.reshape(1, DI), out_weight, local, factor, held
     )

time: 109 us -> 109 us (level)
  blocking collectives: 76.1 us -> 79.2 us
  starting transfers between devices: 8.6 us -> 6.08 us
    all_to_all x3, blocking collectives: 76.1 us -> 79.2 us  [swapped(): return lax.all_to_all(x, axes, split_axis=0, concat_axis=0, tiled=True)]
    all_to_all x1, starting transfers between devices: 8.6 us -> 6.08 us  [swapped(): return lax.all_to_all(x, axes, split_axis=0, concat_axis=0, tiled=True)]
where the time goes in v8:
time: 109 us
  blocking collectives  79.2 us (73%)
  Pallas kernels  20.1 us (18%)
  starting transfers between devices  6.08 us (6%)
  waiting for transfers between devices  3.62 us (3%)
    all_to_all x3, blocking collectives, swapped(): return lax.all_to_all(x, axes, split_axis=0, concat_axis=0, tiled=True)  79.2 us
    pallas_call x1, Pallas kernels, local_part(): pl.pallas_call(local_kernel, in_specs=[anywhere] + [pl.BlockSpec(memory_s...  7.76 us
    pallas_call x1, Pallas kernels, projected_tokens(): pl.pallas_call(output_kernel, in_specs=[vmem] * 4 + [anywhere] * 3, out_s...  6.88 us
    all_to_all x1, starting transfers between devices, swapped(): return lax.all_to_all(x, axes, split_axis=0, concat_axis=0, tiled=True)  6.08 us
    all_to_all x1, waiting for transfers between devices, swapped(): return lax.all_to_all(x, axes, split_axis=0, concat_axis=0, tiled=True)  3.62 us
    pallas_call x1, Pallas kernels, block_states(): pl.pallas_call(state_kernel, in_specs=[anywhere] * 4, out_specs=[pl.Block...  2.74 us
  transfers between devices with their start and end apart: 1, of which 1 were waited for; matrix products, arithmetic and copies ran while one was open for 0% of the time, Pallas kernels for 7%

profile of v8, /device:TPU:1, one launch (start us, length us, event | category | flops | bytes accessed | tf_op | source)
XLA Modules:
  0.0 109.1 jit_solution(6814211266186287800)
XLA Ops:
  0.0 2.7 %block_states.1 = (bf16[32,9,8,128]{3,2,1,0:T(8,128)(2,1)S(1)}, f32[512,64]{1,0:T(8,128)S(1)}) custom-call(s32[1,4]{1,0:T(1,128)} %order_hbm.1, f32[32,512]{1,0:T(8,128)} %bitcast.23, bf16[512,128]{1,0:T(8,128)(2,1)} %bitcast.21, bf16[512,2048]{1,0:T(8,128)(2,1)} %bitcast.18), custom_call_target="tpu_custom_call" | custom-call | flops 2000000000 | bytes 3145728 | tf_op jit(solution)/shard_map/block_states/pallas_call | solution.py:131
  2.7 0.0 copy-start.3
  2.8 20.3 %all_to_all.20.in_ref = bf16[32,9,8,128]{3,2,1,0:T(8,128)(2,1)S(1)} all-to-all(bf16[32,9,8,128]{3,2,1,0:T(8,128)(2,1)S(1)} %get-tuple-element.10), channel_id=1, replica_groups=mesh['z'=8,'y'=4,'core'=2,'view'=4] {'y','core','view'}, dimensions={0} | all-to-all | bytes 1179648 | tf_op jit(solution)/shard_map/all_to_all | solution.py:463
  23.1 0.4 plane_totals.1
  23.5 15.9 %all_to_all.21.totals_ref.after_ref = bf16[8,9,8,128]{3,2,1,0:T(8,128)(2,1)S(1)} all-to-all(bf16[8,9,8,128]{3,2,1,0:T(8,128)(2,1)S(1)} %plane_totals.1), channel_id=1, replica_groups=mesh['z'=8,'y'=4,'core'=2,'view'=4] {'z'}, dimensions={0} | all-to-all | bytes 294912 | tf_op jit(solution)/shard_map/all_to_all | solution.py:463
  39.4 1.2 %entering_states.1 = bf16[32,64,128]{2,1,0:T(8,128)(2,1)} custom-call(bf16[32,9,8,128]{3,2,1,0:T(8,128)(2,1)S(1)} %all_to_all.20.in_ref, bf16[8,9,8,128]{3,2,1,0:T(8,128)(2,1)S(1)} %all_to_all.21.totals_ref.after_ref), custom_call_target="tpu_custom_call" | custom-call | flops 1000000 | bytes 2097152 | tf_op jit(solution)/shard_map/entering_states/pallas_call | solution.py:231
  40.6 6.1 %all-to-all-start.2 = ((bf16[32,64,128]{2,1,0:T(8,128)(2,1)}), bf16[32,64,128]{2,1,0:T(8,128)(2,1)S(1)}, u32[]{:S(2)}, u32[]{:S(2)}) async-start(bf16[32,64,128]{2,1,0:T(8,128)(2,1)} %entering_states.1), calls=%async_computation.2 | async-start | bytes 1048576 | tf_op jit(solution)/shard_map/all_to_all | solution.py:463
  46.6 0.0 copy-done.3
  46.7 0.0 copy-start
  46.7 0.0 copy-start.1
  46.7 7.8 %local_part.1 = (bf16[512,2048]{1,0:T(8,128)(2,1)}, bf16[512,2048]{1,0:T(8,128)(2,1)}, bf16[2048,512]{1,0:T(8,128)(2,1)S(1)}) custom-call(bf16[8,9,8,128]{3,2,1,0:T(8,128)(2,1)S(1)} %all_to_all.21.totals_ref.after_ref, f32[1,32]{1,0:T(1,128)S(1)} %bitcast.17, f32[512,64]{1,0:T(8,128)S(1)} %get-tuple-element.11.sums_ref, bf16[512,128]{1,0:T(8,128)(2,1)} %bitcast.22, ...), custom_call_target="tpu_custom_call" | custom-call | flops 8000000000 | bytes 12582912 | tf_op jit(solution)/shard_map/local_part/pallas_call | solution.py:331
  54.4 3.6 %all-to-all-done.2 = bf16[32,64,128]{2,1,0:T(8,128)(2,1)S(1)} async-done(((bf16[32,64,128]{2,1,0:T(8,128)(2,1)}), bf16[32,64,128]{2,1,0:T(8,128)(2,1)S(1)}, u32[]{:S(2)}, u32[]{:S(2)}) %all-to-all-start.2) | async-done | bytes 524320 | tf_op jit(solution)/shard_map/all_to_all | solution.py:463
  58.1 0.0 copy-done
  58.1 0.0 copy-done.1
  58.1 6.9 %projected_tokens.1 = bf16[512,1536]{1,0:T(8,128)(2,1)S(1)} custom-call(bf16[2048,128]{1,0:T(8,128)(2,1)S(1)} %bitcast.13, bf16[512,128]{1,0:T(8,128)(2,1)S(1)} %bitcast.15, f32[1,2048]{1,0:T(1,128)S(1)} %bitcast.16, bf16[2048,512]{1,0:T(8,128)(2,1)S(1)} %get-tuple-element.12.held_ref, bf16[512,2048]{1,0:T(8,128)(2,1)} %get-tuple-element.13.local_hbm, ...), custom_call_target="tpu_custom_call" | custom-call | flops 4000000000 | bytes 12582912 | tf_op jit(solution)/shard_map/projected_tokens/pallas_call | solution.py:415
  65.0 0.0 copy-start.2
  65.0 43.0 %all_to_all.22 = bf16[64,8,1536]{2,1,0:T(8,128)(2,1)S(1)} all-to-all(bf16[64,8,1536]{2,1,0:T(8,128)(2,1)S(1)} %bitcast.11), channel_id=1, replica_groups=mesh['z'=8,'y'=4,'core'=2,'view'=4] {'z','y','core'}, dimensions={0} | all-to-all | bytes 3145728 | tf_op jit(solution)/shard_map/all_to_all | solution.py:463
  107.9 0.0 copy-done.2
  107.9 1.2 %chosen_tiles.1 = bf16[512,1536]{1,0:T(8,128)(2,1)} custom-call(s32[1,4]{1,0:T(1,128)S(1)} %copy-done.2, bf16[512,1536]{1,0:T(8,128)(2,1)S(1)} %bitcast.12), custom_call_target="tpu_custom_call" | custom-call | bytes 3145728 | tf_op jit(solution)/shard_map/chosen_tiles/pallas_call | solution.py:450
Async XLA Ops:
  2.7 43.9 %copy-start.3 = (f32[32]{0:T(128)S(1)}, f32[32]{0:T(128)}, u32[]{:S(2)}) copy-start(f32[32]{0:T(128)} %param.15) | copy-start | bytes 388
  40.6 17.5 %all-to-all-start.2 = ((bf16[32,64,128]{2,1,0:T(8,128)(2,1)}), bf16[32,64,128]{2,1,0:T(8,128)(2,1)S(1)}, u32[]{:S(2)}, u32[]{:S(2)}) async-start(bf16[32,64,128]{2,1,0:T(8,128)(2,1)} %entering_states.1), calls=%async_computation.2 | async-start | bytes 1048576 | tf_op jit(solution)/shard_map/all_to_all | solution.py:463
  46.7 11.4 %copy-start = (bf16[1,1,512,128]{3,2,1,0:T(8,128)(2,1)S(1)}, bf16[1,1,512,128]{3,2,1,0:T(8,128)(2,1)}, u32[]{:S(2)}) copy-start(bf16[1,1,512,128]{3,2,1,0:T(8,128)(2,1)} %param.13) | copy-start | bytes 393220
  46.7 11.4 %copy-start.1 = (f32[2048]{0:T(1024)S(1)}, f32[2048]{0:T(1024)}, u32[]{:S(2)}) copy-start(f32[2048]{0:T(1024)} %param.16) | copy-start | bytes 24580
  65.0 43.0 %copy-start.2 = (s32[1,4]{1,0:T(1,128)S(1)}, s32[1,4]{1,0:T(1,128)}, u32[]{:S(2)}) copy-start(s32[1,4]{1,0:T(1,128)} %order_ref.1) | copy-start | bytes 52

commit v9 on v7

--- a/solution.py
+++ b/solution.py
@@ -276,7 +276,9 @@
         b_part, c_part = b_scr[rows, :], c_scr[rows, :]
         b_rows.append(b_part.astype(F32).T.astype(BF))
         scores = jnp.where(causal, dot(c_part, b_part, (1, 1)), 0.0)
-        left.append(jnp.concatenate([scores.astype(BF), c_part], axis=1))
+        hi = scores.astype(BF)
+        lo = (scores - hi.astype(F32)).astype(BF)
+        left.append(jnp.concatenate([hi, hi, lo, c_part], axis=1))
 
     for block in range(DI // COLS):
         columns = slice(block * COLS, (block + 1) * COLS)
@@ -291,8 +293,9 @@
         for k in range(CHUNKS):
             rows = slice(k * CHUNK, (k + 1) * CHUNK)
             x = x_scr[rows, columns].astype(F32)
-            scaled = (x * dot(inward[k], twice)).astype(BF)
-            right = [scaled]
+            exact = x * dot(inward[k], twice)
+            scaled = exact.astype(BF)
+            right = [scaled, (exact - scaled.astype(F32)).astype(BF), scaled]
             if running is not None:
                 right.append((running * ends[4 + k : 5 + k]).astype(BF))
             inner = dot(left[k][:, 0 : CHUNK * len(right)], jnp.concatenate(right, axis=0))

time: 109 us -> 110 us (level)
  transfers between devices with their start and end apart: 1 -> 1, of which waited for: 1 -> 1; matrix products, arithmetic and copies ran while one was open for 0% -> 0% of each run, Pallas kernels for 7% -> 8%
where the time goes in v9:
time: 110 us; the launch traced here: 109 us
  blocking collectives  76.1 us (69%)
  Pallas kernels  20.9 us (19%)
  starting transfers between devices  8.59 us (8%)
  waiting for transfers between devices  3.41 us (3%)
    all_to_all x3, blocking collectives, swapped(): return lax.all_to_all(x, axes, split_axis=0, concat_axis=0, tiled=True)  76.1 us
    all_to_all x1, starting transfers between devices, swapped(): return lax.all_to_all(x, axes, split_axis=0, concat_axis=0, tiled=True)  8.59 us
    pallas_call x1, Pallas kernels, local_part(): pl.pallas_call(local_kernel, in_specs=[pl.BlockSpec(memory_space=pltpu.VM...  8.53 us
    pallas_call x1, Pallas kernels, projected_tokens(): pl.pallas_call(output_kernel, in_specs=[vmem] * 4 + [anywhere] * 3, out_s...  6.77 us
    pallas_call x1, Pallas kernels, block_states(): pl.pallas_call(state_kernel, in_specs=[anywhere] * 4, out_specs=[pl.Block...  3.57 us
    all_to_all x1, waiting for transfers between devices, swapped(): return lax.all_to_all(x, axes, split_axis=0, concat_axis=0, tiled=True)  3.41 us
  transfers between devices with their start and end apart: 1, of which 1 were waited for; matrix products, arithmetic and copies ran while one was open for 0% of the time, Pallas kernels for 8%

profile of v9, /device:TPU:1, one launch (start us, length us, event | category | flops | bytes accessed | tf_op | source)
XLA Modules:
  0.0 109.3 jit_solution(1992153990638716962)
XLA Ops:
  0.0 0.0 copy-start.3
  0.0 3.6 %block_states.1 = (bf16[32,9,8,128]{3,2,1,0:T(8,128)(2,1)}, f32[512,64]{1,0:T(8,128)S(1)}) custom-call(s32[1,4]{1,0:T(1,128)} %order_hbm.1, f32[32,512]{1,0:T(8,128)} %bitcast.23, bf16[512,128]{1,0:T(8,128)(2,1)} %bitcast.21, bf16[512,2048]{1,0:T(8,128)(2,1)} %bitcast.18), custom_call_target="tpu_custom_call" | custom-call | flops 2000000000 | bytes 3145728 | tf_op jit(solution)/shard_map/block_states/pallas_call | solution.py:130
  3.6 8.6 %all-to-all-start = ((bf16[32,9,8,128]{3,2,1,0:T(8,128)(2,1)}), bf16[32,9,8,128]{3,2,1,0:T(8,128)(2,1)S(1)}, u32[]{:S(2)}, u32[]{:S(2)}) async-start(bf16[32,9,8,128]{3,2,1,0:T(8,128)(2,1)} %get-tuple-element.10), calls=%async_computation | async-start | bytes 1179648 | tf_op jit(solution)/shard_map/all_to_all | solution.py:450
  12.2 0.0 copy-done.3
  12.2 8.5 %local_part.1 = (bf16[512,2048]{1,0:T(8,128)(2,1)}, bf16[512,2048]{1,0:T(8,128)(2,1)}, bf16[2048,512]{1,0:T(8,128)(2,1)S(1)}) custom-call(f32[1,32]{1,0:T(1,128)S(1)} %bitcast.17, f32[512,64]{1,0:T(8,128)S(1)} %get-tuple-element.11.sums_ref, bf16[512,128]{1,0:T(8,128)(2,1)} %bitcast.22, bf16[512,128]{1,0:T(8,128)(2,1)} %bitcast.14, ...), custom_call_target="tpu_custom_call" | custom-call | flops 8000000000 | bytes 12582912 | tf_op jit(solution)/shard_map/local_part/pallas_call | solution.py:319
  20.7 3.4 %all-to-all-done.in_ref = bf16[32,9,8,128]{3,2,1,0:T(8,128)(2,1)S(1)} async-done(((bf16[32,9,8,128]{3,2,1,0:T(8,128)(2,1)}), bf16[32,9,8,128]{3,2,1,0:T(8,128)(2,1)S(1)}, u32[]{:S(2)}, u32[]{:S(2)}) %all-to-all-start) | async-done | bytes 589856 | tf_op jit(solution)/shard_map/all_to_all | solution.py:450
  24.1 0.0 copy-start
  24.1 0.0 copy-start.1
  24.1 0.4 plane_totals.1
  24.5 15.9 %all_to_all.20.totals_ref = bf16[8,9,8,128]{3,2,1,0:T(8,128)(2,1)S(1)} all-to-all(bf16[8,9,8,128]{3,2,1,0:T(8,128)(2,1)S(1)} %plane_totals.1), channel_id=1, replica_groups=mesh['z'=8,'y'=4,'core'=2,'view'=4] {'z'}, dimensions={0} | all-to-all | bytes 294912 | tf_op jit(solution)/shard_map/all_to_all | solution.py:450
  40.4 0.5 entering_states.1
  40.9 17.3 %all_to_all.21 = bf16[32,64,128]{2,1,0:T(8,128)(2,1)S(1)} all-to-all(bf16[32,64,128]{2,1,0:T(8,128)(2,1)S(1)} %entering_states.1), channel_id=1, replica_groups=mesh['z'=8,'y'=4,'core'=2,'view'=4] {'y','core','view'}, dimensions={0} | all-to-all | bytes 1048576 | tf_op jit(solution)/shard_map/all_to_all | solution.py:450
  58.2 0.0 copy-done
  58.2 0.0 copy-done.1
  58.2 6.8 %projected_tokens.1 = bf16[512,1536]{1,0:T(8,128)(2,1)S(1)} custom-call(bf16[2048,128]{1,0:T(8,128)(2,1)S(1)} %bitcast.13, bf16[512,128]{1,0:T(8,128)(2,1)S(1)} %bitcast.15, f32[1,2048]{1,0:T(1,128)S(1)} %bitcast.16, bf16[2048,512]{1,0:T(8,128)(2,1)S(1)} %get-tuple-element.13.held_ref, bf16[512,2048]{1,0:T(8,128)(2,1)} %get-tuple-element.12.token_ref.local_hbm, ...), custom_call_target="tpu_custom_call" | custom-call | flops 4000000000 | bytes 12582912 | tf_op jit(solution)/shard_map/projected_tokens/pallas_call | solution.py:402
  65.0 0.0 copy-start.2
  65.0 42.9 %all_to_all.22 = bf16[64,8,1536]{2,1,0:T(8,128)(2,1)S(1)} all-to-all(bf16[64,8,1536]{2,1,0:T(8,128)(2,1)S(1)} %bitcast.11), channel_id=1, replica_groups=mesh['z'=8,'y'=4,'core'=2,'view'=4] {'z','y','core'}, dimensions={0} | all-to-all | bytes 3145728 | tf_op jit(solution)/shard_map/all_to_all | solution.py:450
  107.9 0.0 copy-done.2
  107.9 1.2 %chosen_tiles.1 = bf16[512,1536]{1,0:T(8,128)(2,1)} custom-call(s32[1,4]{1,0:T(1,128)S(1)} %copy-done.2, bf16[512,1536]{1,0:T(8,128)(2,1)S(1)} %bitcast.12), custom_call_target="tpu_custom_call" | custom-call | bytes 3145728 | tf_op jit(solution)/shard_map/chosen_tiles/pallas_call | solution.py:437
Async XLA Ops:
  0.0 12.2 %copy-start.3 = (f32[32]{0:T(128)S(1)}, f32[32]{0:T(128)}, u32[]{:S(2)}) copy-start(f32[32]{0:T(128)} %param.15) | copy-start | bytes 388
  3.6 20.6 %all-to-all-start = ((bf16[32,9,8,128]{3,2,1,0:T(8,128)(2,1)}), bf16[32,9,8,128]{3,2,1,0:T(8,128)(2,1)S(1)}, u32[]{:S(2)}, u32[]{:S(2)}) async-start(bf16[32,9,8,128]{3,2,1,0:T(8,128)(2,1)} %get-tuple-element.10), calls=%async_computation | async-start | bytes 1179648 | tf_op jit(solution)/shard_map/all_to_all | solution.py:450
  24.1 34.0 %copy-start = (bf16[1,1,512,128]{3,2,1,0:T(8,128)(2,1)S(1)}, bf16[1,1,512,128]{3,2,1,0:T(8,128)(2,1)}, u32[]{:S(2)}) copy-start(bf16[1,1,512,128]{3,2,1,0:T(8,128)(2,1)} %param.13) | copy-start | bytes 393220
  24.1 34.0 %copy-start.1 = (f32[2048]{0:T(1024)S(1)}, f32[2048]{0:T(1024)}, u32[]{:S(2)}) copy-start(f32[2048]{0:T(1024)} %param.16) | copy-start | bytes 24580
  65.0 43.0 %copy-start.2 = (s32[1,4]{1,0:T(1,128)S(1)}, s32[1,4]{1,0:T(1,128)}, u32[]{:S(2)}) copy-start(s32[1,4]{1,0:T(1,128)} %order_ref.1) | copy-start | bytes 52
